TPU v7x, 512 devices: a whole 4x4x16 slice. The times are simulated.
512 devices in a mesh: dp: 16 (over z), label: 32 (over y, x, core).
Axes of the slice: x: 4, y: 4, z: 16, core: 2. Of those that a mesh axis runs over, the one named last changes fastest.
Arguments:
- queries: bfloat16 [8192, 768], P('dp')
- embeddings: bfloat16 [16384, 768], P('label')
- shortlist: int32 [64, 48], P('dp'), may hold values from 0 to 127, as said below
- positive: int32 [8192], P('dp'), may hold values from 0 to 16383, as said below
Outputs:
- losses: float32 [8192], P('dp')
- query_grad: bfloat16 [8192, 768], P('dp')
- label_grad: float32 [128, 128, 768], P('dp', 'label')
Inputs may be any that keep to these rules, and one draw needn't show every extreme that they name: `shortlist`: each row lists 48 different label blocks. `shortlist`: of the blocks listed for one query block, at most 3 lie among the 4 blocks b with the same b // 4, and every row reaches 3 for some such group; for every even query block that group is b // 4 == 16. Each query's positive label lies in one of the blocks listed for its query block.
All inputs are finite; a program needn't handle non-finite values.
Results may differ from a plain program's by a relative error of at most 0.0037.
Values may be sent and summed in bfloat16 or wider, within the bound.
No kernel may reach another device: no remote copies, remote signals or barrier semaphores. Data moves between devices by JAX's collectives and lax.ppermute only.
A program may use at most 64 MiB of HBM per device.

v0:
```python
import jax
import jax.numpy as jnp
from jax import lax
from jax.sharding import PartitionSpec as P

BLOCK = 128


def body(queries, embeddings, shortlist, positive):
    rows_dev = queries.shape[0]
    labels_dev = embeddings.shape[0]
    width = queries.shape[1]
    query_blocks = rows_dev // BLOCK
    label_blocks = labels_dev // BLOCK
    listed_count = shortlist.shape[1]
    hits_most = min(label_blocks, max(1, 2 * listed_count // lax.axis_size("label")))
    first_block = lax.axis_index("label") * label_blocks
    is_local = shortlist // label_blocks == lax.axis_index("label")
    position = jnp.cumsum(is_local.astype(jnp.int32), axis=1) - 1
    matches = is_local[:, :, None] & (
        position[:, :, None] == jnp.arange(hits_most, dtype=jnp.int32)[None, None, :]
    )
    slot_ids = jnp.sum(jnp.where(matches, (shortlist - first_block)[:, :, None], 0), axis=1)
    valid = jnp.any(matches, axis=1)
    block_table = embeddings.reshape(label_blocks, BLOCK, width)
    picked = block_table[slot_ids]
    query_table = queries.reshape(query_blocks, BLOCK, width)
    scores = jnp.einsum("qid,qhjd->qihj", query_table, picked, preferred_element_type=jnp.float32)
    selected = jnp.broadcast_to(valid[:, None, :, None], scores.shape)
    local_positive = (positive - first_block * BLOCK).reshape(query_blocks, BLOCK)
    positive_block = local_positive // BLOCK
    positive_col = local_positive % BLOCK
    inside = (local_positive >= 0) & (local_positive < labels_dev)
    block_hit = (
        valid[:, None, :]
        & (slot_ids[:, None, :] == positive_block[:, :, None])
        & inside[:, :, None]
    )
    col_hit = positive_col[:, :, None] == jnp.arange(BLOCK, dtype=jnp.int32)[None, None, :]
    is_positive = block_hit[:, :, :, None] & col_hit[:, :, None, :]
    positive_part = jnp.sum(jnp.where(is_positive, scores, 0.0), axis=(2, 3)).reshape(rows_dev)
    local_top = jnp.max(jnp.where(selected, scores, -1e30), axis=(2, 3)).reshape(rows_dev)
    row_top = lax.pmax(local_top, "label")
    weights = jnp.exp(
        jnp.where(
            selected, scores - row_top.reshape(query_blocks, BLOCK)[:, :, None, None], -jnp.inf
        )
    )
    local_sum = jnp.sum(weights, axis=(2, 3)).reshape(rows_dev)
    row_total, positive_score = lax.psum((local_sum, positive_part), "label")
    losses = row_top + jnp.log(row_total) - positive_score
    gradient = (
        weights / row_total.reshape(query_blocks, BLOCK)[:, :, None, None]
        - is_positive.astype(jnp.float32)
    ).astype(jnp.bfloat16)
    partial_grad = jnp.einsum(
        "qihj,qhjd->qid", gradient, picked, preferred_element_type=jnp.float32
    ).reshape(rows_dev, width)
    query_grad = lax.psum(partial_grad, "label").astype(jnp.bfloat16)
    owner_table = (
        valid[:, :, None]
        & (slot_ids[:, :, None] == jnp.arange(label_blocks, dtype=jnp.int32)[None, None, :])
    ).astype(jnp.float32)
    owner_table = owner_table.reshape(query_blocks * hits_most, label_blocks)
    slot_terms = jnp.einsum(
        "qihj,qid->qhjd", gradient, query_table, preferred_element_type=jnp.float32
    )
    slot_terms = slot_terms.reshape(
        query_blocks * hits_most, lax.axis_size("dp") * (BLOCK // lax.axis_size("dp")), width
    )
    label_grad = lax.psum_scatter(
        jnp.einsum("sb,sjd->jbd", owner_table, slot_terms, precision=lax.Precision.HIGHEST),
        "dp",
        scatter_dimension=0,
        tiled=True,
    )
    return (losses, query_grad, label_grad)


def solution(mesh):
    in_specs = (P("dp", None), P("label", None), P("dp", None), P("dp"))
    out_specs = (P("dp"), P("dp", None), P("dp", "label", None))
    return jax.shard_map(body, mesh=mesh, in_specs=in_specs, out_specs=out_specs, check_vma=False)
```

profile of v0, /device:TPU:1, one launch (start us, length us, event | category | flops | bytes accessed | tf_op | source)
XLA Modules:
  0.0 305.9 jit_solution(18125803259026648651)
XLA Ops:
  7.2 0.0 copy-start
  7.2 0.0 all-reduce.5.cloned.1.call-start
  7.2 0.8 add_select_fusion.1
  8.0 0.7 fusion.21
  8.7 0.7 fusion.26
  9.4 0.2 reduce_window_sum.11
  9.6 0.7 broadcast_subtract_fusion
  10.3 0.1 fusion.13
  10.4 0.1 copy.17
  10.5 0.2 select_reduce_fusion.1
  10.7 0.1 copy.18
  10.8 0.1 reshape.132
  10.9 3.3 %gather_fusion = bf16[12,128,768]{2,1,0:T(8,128)(2,1)} fusion(bf16[4,128,768]{2,1,0:T(8,128)(2,1)} %bitcast.65, s32[1024]{0:T(1024)S(1)} %pad_clamp_fusion), kind=kCustom, calls=%fused_computation | custom fusion | bytes 4718640 | tf_op jit(solution)/shard_map/gather | solution.py:26
  14.2 0.0 copy-done
  14.2 2.4 select_reduce_fusion
  16.7 68.9 %pmax.7 = f32[512]{0:T(512)S(1)} all-reduce(f32[512]{0:T(512)S(1)} %bitcast.76), channel_id=1, replica_groups=mesh['dp'=16,'label'=32] {'label'}, use_global_device_ids=true, to_apply=%region_4.5 | all-reduce | flops 512 | bytes 4096 | tf_op jit(solution)/shard_map/pmax | solution.py:43
  85.6 0.1 and_and_fusion
  85.7 0.3 fusion.8
  86.0 62.7 %psum.21 = f32[512]{0:T(512)S(1)} all-reduce(f32[512]{0:T(512)S(1)} %bitcast.75), channel_id=1, replica_groups=mesh['dp'=16,'label'=32] {'label'}, use_global_device_ids=true, to_apply=%region_6.7 | all-reduce | flops 512 | bytes 4096 | tf_op jit(solution)/shard_map/psum | solution.py:50
  148.7 0.8 fusion.22
  149.5 6.4 %fusion.2 = f32[128,4,768]{2,1,0:T(4,128)} fusion(f32[4,3,128,768]{3,2,1,0:T(8,128)S(1)} %fusion.22, s32[4,3]{0,1:T(4,128)S(1)} %select_reduce_fusion.1, pred[4,3]{0,1:T(4,128)(4,1)S(1)} %fusion.13), kind=kOutput, calls=%fused_computation.3 | convolution fusion | flops 56623200 | bytes 6291516 | tf_op jit(solution)/shard_map/sb,sjd->jbd/dot_general | solution.py:72
  155.9 0.0 all-reduce.5.cloned.1.call-update
  155.9 2.5 fusion.24
  158.4 1.3 dynamic-slice
  160.3 136.7 %all-reduce.6 = (f32[512]{0:T(512)S(1)}, bf16[512,768]{1,0:T(8,128)(2,1)}) all-reduce(f32[512]{0:T(512)S(1)} %bitcast.74, f32[512,768]{1,0:T(8,128)S(1)} %bitcast.68), channel_id=1, replica_groups=mesh['dp'=16,'label'=32] {'label'}, use_global_device_ids=true, to_apply=%region_8.9 | all-reduce | flops 393728 | bytes 2363392 | tf_op jit(solution)/shard_map/psum | solution.py:50
  297.0 0.6 add_subtract_fusion
  297.6 0.0 all-reduce.5.cloned.1.call-done
  297.6 1.5 constant_dynamic-slice_fusion
  (3 shorter events, 0.1 us)
Async XLA Ops:
  7.2 7.1 %copy-start = (bf16[512,768]{1,0:T(8,128)(2,1)S(1)}, bf16[512,768]{1,0:T(8,128)(2,1)}, u32[]{:S(2)}) copy-start(bf16[512,768]{1,0:T(8,128)(2,1)} %param.4) | copy-start | bytes 2359300
  7.2 290.4 %all-reduce.5.cloned.1.call-start = ((), (), s32[]{:S(2)}) async-start(), calls=%async_computation | async-start | bytes 3145728
Sparse Core Ops, SparseCore 0:
  156.0 131.1 all-reduce.4
where the time goes:
time: 310 us; the launch traced here: 306 us
  blocking collectives  268 us (86%)
  between operations  14.7 us (5%)
  matrix products  12.1 us (4%)
  local copies, waits for them, and re-layouts  6.44 us (2%)
  other arithmetic  4.35 us (1%)
    psum x2, blocking collectives, body(): row_total, positive_score = lax.psum((local_sum, positive_part), 'label')  199 us
    pmax x1, blocking collectives, body(): row_top = lax.pmax(local_top, 'label')  68.9 us
    dot_general x1, matrix products, body(): jnp.einsum('sb,sjd->jbd', owner_table, slot_terms, precision=lax.Precisio...  6.37 us
  transfers between devices with their start and end apart: 1, of which 0 were waited for; matrix products, arithmetic and copies ran while one was open for 1% of the time, Pallas kernels for 0%

commit v1 on v0

v1 whole, which is shorter than its diff:
```python
import functools

import jax
import jax.numpy as jnp
from jax import lax
from jax.experimental import pallas as pl
from jax.experimental.pallas import tpu as pltpu
from jax.sharding import PartitionSpec as P

BLOCK = 128
LOWEST = -3.4028234e38
VMEM_LIMIT = 32 * 1024 * 1024
F32 = jnp.float32
BF16 = jnp.bfloat16


def call(kernel, out_shape, args, flops=0, smem=0, scratch=(), moved=2_000_000):
    specs = [pl.BlockSpec(memory_space=pltpu.SMEM)] * smem
    specs += [pl.BlockSpec(memory_space=pltpu.VMEM)] * (len(args) - smem)
    return pl.pallas_call(
        kernel,
        out_shape=out_shape,
        in_specs=specs,
        out_specs=jax.tree.map(lambda _: pl.BlockSpec(memory_space=pltpu.VMEM), out_shape),
        scratch_shapes=list(scratch),
        compiler_params=pltpu.CompilerParams(vmem_limit_bytes=VMEM_LIMIT),
        cost_estimate=pl.CostEstimate(flops=flops, bytes_accessed=moved, transcendentals=0),
    )(*args)


def local_scores(me, short_ref, positive_ref, queries_ref, embeddings_ref):
    labels, rows = embeddings_ref.shape[0], queries_ref.shape[0]
    label_blocks, query_blocks = labels // BLOCK, rows // BLOCK
    scores = lax.dot_general(
        embeddings_ref[...], queries_ref[...], (((1,), (1,)), ((), ())), preferred_element_type=F32
    )
    listed = short_ref[...]
    masked = []
    for b in range(label_blocks):
        hit = jnp.max(
            jnp.where(listed == me * label_blocks + b, 1.0, 0.0).astype(F32), axis=1, keepdims=True
        )
        row = jnp.concatenate(
            [jnp.broadcast_to(hit[q : q + 1], (1, BLOCK)) for q in range(query_blocks)], axis=1
        )
        masked.append(jnp.where(row > 0.5, scores[b * BLOCK : (b + 1) * BLOCK], -jnp.inf))
    masked = jnp.concatenate(masked, axis=0)
    place = positive_ref[...] - me * labels
    is_positive = lax.broadcasted_iota(jnp.int32, (labels, rows), 0) == place
    return scores, masked, is_positive


def stats_kernel(short_ref, positive_ref, queries_ref, embeddings_ref, out_ref):
    me = lax.axis_index("label")
    scores, masked, is_positive = local_scores(
        me, short_ref, positive_ref, queries_ref, embeddings_ref
    )
    top = jnp.maximum(jnp.max(masked, axis=0, keepdims=True), LOWEST)
    total = jnp.sum(jnp.exp(masked - top), axis=0, keepdims=True)
    positive = jnp.sum(jnp.where(is_positive, scores, 0.0), axis=0, keepdims=True)
    rows = jnp.concatenate([top, total, positive, jnp.zeros_like(top)], axis=0)
    out_ref[...] = jnp.broadcast_to(rows[None], out_ref.shape)


def gradient_kernel(
    short_ref, positive_ref, stats_ref, queries_ref, embeddings_ref, loss_ref, grad_ref, label_ref
):
    me = lax.axis_index("label")
    tops, totals = stats_ref[:, 0, :], stats_ref[:, 1, :]
    top = jnp.max(tops, axis=0, keepdims=True)
    total = jnp.sum(totals * jnp.exp(tops - top), axis=0, keepdims=True)
    positive = jnp.sum(stats_ref[:, 2, :], axis=0, keepdims=True)
    loss_ref[...] = top + jnp.log(total) - positive
    _, masked, is_positive = local_scores(me, short_ref, positive_ref, queries_ref, embeddings_ref)
    weights = jnp.exp(masked - top) * (1.0 / total)
    gradient = jnp.where(is_positive, weights - 1.0, weights).astype(BF16)
    grad_ref[...] = gradient
    part = jnp.dot(gradient, queries_ref[...], preferred_element_type=F32)
    parts = label_ref.shape[0]
    blocks = part.shape[0] // BLOCK
    deep = BLOCK // parts
    width = part.shape[1]
    part = part.reshape(blocks, parts, deep, width)
    for p in range(parts):
        label_ref[p] = part[:, p].reshape(blocks * deep, width).astype(BF16)


def query_kernel(grad_ref, embeddings_ref, out_ref):
    out_ref[...] = lax.dot_general(
        grad_ref[...], embeddings_ref[...], (((0,), (0,)), ((), ())), preferred_element_type=F32
    ).astype(BF16)


def spread_kernel(parts_ref, out_ref):
    total = parts_ref[0].astype(F32)
    for i in range(1, parts_ref.shape[0]):
        total = total + parts_ref[i].astype(F32)
    out_ref[...] = jnp.broadcast_to(total.astype(BF16)[None], out_ref.shape)


def body(queries, embeddings, shortlist, positive):
    rows, width = queries.shape
    labels = embeddings.shape[0]
    groups, planes = lax.axis_size("label"), lax.axis_size("dp")
    shape = jax.ShapeDtypeStruct
    positive = positive.reshape(1, rows)
    madds = rows * labels * width

    stats = call(
        stats_kernel,
        shape((groups, 4, rows), F32),
        (shortlist, positive, queries, embeddings),
        flops=2 * madds,
    )
    stats = lax.all_to_all(stats, "label", 0, 0)
    losses, gradient, label_part = call(
        gradient_kernel,
        (
            shape((1, rows), F32),
            shape((labels, rows), BF16),
            shape((planes, labels // planes, width), BF16),
        ),
        (shortlist, positive, stats, queries, embeddings),
        flops=4 * madds,
    )
    label_parts = lax.all_to_all(label_part, "dp", 0, 0)
    query_part = call(query_kernel, shape((rows, width), BF16), (gradient, embeddings), flops=2 * madds)
    query_parts = lax.all_to_all(
        query_part.reshape(groups, rows // groups, width), "label", 0, 0
    )
    chunk = call(spread_kernel, shape(query_parts.shape, BF16), (query_parts,))
    query_grad = lax.all_to_all(chunk, "label", 0, 0).reshape(rows, width)
    label_grad = jnp.sum(label_parts.astype(F32), axis=0)
    label_grad = label_grad.reshape(labels // BLOCK, BLOCK // planes, width).swapaxes(0, 1)
    return losses.reshape(rows), query_grad, label_grad


def solution(mesh):
    in_specs = (P("dp", None), P("label", None), P("dp", None), P("dp"))
    out_specs = (P("dp"), P("dp", None), P("dp", "label", None))
    return jax.shard_map(body, mesh=mesh, in_specs=in_specs, out_specs=out_specs, check_vma=False)
```

time: 310 us -> 117 us (0.38)
  the two profiles are of different devices: /device:TPU:1 before, /device:TPU:32 now
where the time goes in v1:
time: 117 us; the launch traced here: 116 us
  blocking collectives  52 us (44%)
  waiting for transfers between devices  39.3 us (34%)
  starting transfers between devices  15.2 us (13%)
  local copies, waits for them, and re-layouts  5.19 us (4%)
  Pallas kernels  3.68 us (3%)
    all_to_all x1, waiting for transfers between devices, body(): label_parts = lax.all_to_all(label_part, 'dp', 0, 0)  39.3 us
    all_to_all x1, blocking collectives, body(): lax.all_to_all(query_part.reshape(groups, rows // groups, width), 'label'...  18.1 us
    all_to_all x1, blocking collectives, body(): query_grad = lax.all_to_all(chunk, 'label', 0, 0).reshape(rows, width)  17.9 us
    all_to_all x1, blocking collectives, body(): stats = lax.all_to_all(stats, 'label', 0, 0)  16 us
    all_to_all x1, starting transfers between devices, body(): label_parts = lax.all_to_all(label_part, 'dp', 0, 0)  15.2 us
    unnamed x12, local copies, waits for them, and re-layouts  5.19 us
    pallas_call x4, Pallas kernels, call(): pl.pallas_call(kernel, out_shape=out_shape, in_specs=specs, out_specs=jax...  3.68 us
  transfers between devices with their start and end apart: 1, of which 1 were waited for; matrix products, arithmetic and copies ran while one was open for 0% of the time, Pallas kernels for 0%

profile of v1, /device:TPU:32, one launch (start us, length us, event | category | flops | bytes accessed | tf_op | source)
XLA Modules:
  0.0 116.1 jit_solution(568019450586054201)
XLA Ops:
  0.6 0.0 copy-start
  0.6 1.1 copy-done
  1.8 0.0 copy-start.2
  1.8 1.1 copy-done.2
  2.9 0.0 copy-start.3
  2.9 0.7 copy-done.3
  3.6 0.0 copy-start.4
  3.6 0.7 copy-done.4
  4.3 0.8 shard_map.67
  5.1 16.0 %all_to_all.20.stats_ref = f32[32,4,512]{2,1,0:T(4,128)S(1)} all-to-all(f32[32,4,512]{2,1,0:T(4,128)S(1)} %shard_map.67), channel_id=1, replica_groups=mesh['dp'=16,'label'=32] {'label'}, dimensions={0} | all-to-all | bytes 524288 | tf_op jit(solution)/shard_map/all_to_all | solution.py:115
  21.1 0.0 copy-start.1
  21.1 2.1 %shard_map.68 = (f32[1,512]{1,0:T(1,128)}, bf16[512,512]{1,0:T(8,128)(2,1)S(1)}, bf16[16,32,768]{2,1,0:T(8,128)(2,1)}) custom-call(s32[4,48]{1,0:T(4,128)S(1)} %copy-done.3, s32[1,512]{1,0:T(1,128)S(1)} %bitcast.9, f32[32,4,512]{2,1,0:T(4,128)S(1)} %all_to_all.20.stats_ref, bf16[512,768]{1,0:T(8,128)(2,1)S(1)} %copy-done.2, bf16[512,768]{1,0:T(8,128)(2,1)S(1)} %copy-done), custom_call_target="tpu_custom_call" | custom-call | flops 805306368 | bytes 2000000 | tf_op jit(solution)/shard_map/pallas_call | solution.py:20
  23.2 0.0 copy-done.1
  23.2 0.6 shard_map.69
  23.9 18.1 %all_to_all.21.parts_ref = bf16[32,16,768]{2,1,0:T(8,128)(2,1)S(1)} all-to-all(bf16[32,16,768]{2,1,0:T(8,128)(2,1)S(1)} %bitcast.7), channel_id=1, replica_groups=mesh['dp'=16,'label'=32] {'label'}, dimensions={0} | all-to-all | bytes 1572864 | tf_op jit(solution)/shard_map/all_to_all | solution.py:128
  42.0 0.1 shard_map.70
  42.1 17.9 %all_to_all.22 = bf16[32,16,768]{2,1,0:T(8,128)(2,1)S(1)} all-to-all(bf16[32,16,768]{2,1,0:T(8,128)(2,1)S(1)} %shard_map.70), channel_id=1, replica_groups=mesh['dp'=16,'label'=32] {'label'}, dimensions={0} | all-to-all | bytes 1572864 | tf_op jit(solution)/shard_map/all_to_all | solution.py:132
  60.0 15.2 %all-to-all-start.3 = ((bf16[16,32,768]{2,1,0:T(8,128)(2,1)}), bf16[16,32,768]{2,1,0:T(8,128)(2,1)S(1)}, u32[]{:S(2)}, u32[]{:S(2)}) async-start(bf16[16,32,768]{2,1,0:T(8,128)(2,1)} %get-tuple-element.8), calls=%async_computation.3 | async-start | bytes 1572864 | tf_op jit(solution)/shard_map/all_to_all | solution.py:126
  75.2 39.3 %all-to-all-done.3 = bf16[16,32,768]{2,1,0:T(8,128)(2,1)S(1)} async-done(((bf16[16,32,768]{2,1,0:T(8,128)(2,1)}), bf16[16,32,768]{2,1,0:T(8,128)(2,1)S(1)}, u32[]{:S(2)}, u32[]{:S(2)}) %all-to-all-start.3) | async-done | bytes 786464 | tf_op jit(solution)/shard_map/all_to_all | solution.py:126
  114.5 0.1 convert_reduce_fusion
  114.6 0.7 copy.7
  115.2 0.9 copy.9
Async XLA Ops:
  0.6 1.1 copy-start
  1.8 1.1 copy-start.2
  2.9 0.7 copy-start.3
  3.6 0.7 copy-start.4
  21.1 2.1 %copy-start.1 = (bf16[512,768]{1,0:T(8,128)(2,1)S(1)}, bf16[512,768]{1,0:T(8,128)(2,1)}, u32[]{:S(2)}) copy-start(bf16[512,768]{1,0:T(8,128)(2,1)} %embeddings_ref.5) | copy-start | bytes 2359300
  60.0 54.5 %all-to-all-start.3 = ((bf16[16,32,768]{2,1,0:T(8,128)(2,1)}), bf16[16,32,768]{2,1,0:T(8,128)(2,1)S(1)}, u32[]{:S(2)}, u32[]{:S(2)}) async-start(bf16[16,32,768]{2,1,0:T(8,128)(2,1)} %get-tuple-element.8), calls=%async_computation.3 | async-start | bytes 1572864 | tf_op jit(solution)/shard_map/all_to_all | solution.py:126

commit v2 on v1

v2 whole, which is shorter than its diff:
```python
import jax
import jax.numpy as jnp
from jax import lax
from jax.experimental import pallas as pl
from jax.experimental.pallas import tpu as pltpu
from jax.sharding import PartitionSpec as P

BLOCK = 128
LOWEST = -3.4028234e38
VMEM_LIMIT = 24 * 1024 * 1024
VMEM_MOST = 62_000_000
F32 = jnp.float32
BF16 = jnp.bfloat16


def call(kernel, out_shape, args, flops=0, scratch=(), any_inputs=0, vmem=VMEM_LIMIT):
    specs = [pl.BlockSpec(memory_space=pltpu.HBM)] * any_inputs
    specs += [pl.BlockSpec(memory_space=pltpu.VMEM)] * (len(args) - any_inputs)
    return pl.pallas_call(
        kernel,
        out_shape=out_shape,
        in_specs=specs,
        out_specs=jax.tree.map(lambda _: pl.BlockSpec(memory_space=pltpu.VMEM), out_shape),
        scratch_shapes=list(scratch),
        compiler_params=pltpu.CompilerParams(vmem_limit_bytes=vmem),
        cost_estimate=pl.CostEstimate(flops=flops, bytes_accessed=2_000_000, transcendentals=0),
    )(*args)


def local_scores(me, short_ref, positive_ref, queries_ref, embeddings_ref):
    labels, rows = embeddings_ref.shape[0], queries_ref.shape[0]
    label_blocks, query_blocks = labels // BLOCK, rows // BLOCK
    scores = lax.dot_general(
        embeddings_ref[...], queries_ref[...], (((1,), (1,)), ((), ())), preferred_element_type=F32
    )
    listed = short_ref[...]
    masked = []
    for b in range(label_blocks):
        hit = jnp.max(
            jnp.where(listed == me * label_blocks + b, 1.0, 0.0).astype(F32), axis=1, keepdims=True
        )
        row = jnp.concatenate(
            [jnp.broadcast_to(hit[q : q + 1], (1, BLOCK)) for q in range(query_blocks)], axis=1
        )
        masked.append(jnp.where(row > 0.5, scores[b * BLOCK : (b + 1) * BLOCK], -jnp.inf))
    masked = jnp.concatenate(masked, axis=0)
    place = positive_ref[...] - me * labels
    is_positive = lax.broadcasted_iota(jnp.int32, (labels, rows), 0) == place
    return scores, masked, is_positive


def stats_kernel(
    short_hbm, positive_hbm, queries_hbm, embeddings_hbm, out_ref,
    short_ref, positive_ref, queries_ref, embeddings_ref, sems,
):
    copies = [
        pltpu.make_async_copy(source, target, sems.at[i])
        for i, (source, target) in enumerate(
            [
                (queries_hbm, queries_ref),
                (embeddings_hbm, embeddings_ref),
                (short_hbm, short_ref),
                (positive_hbm, positive_ref),
            ]
        )
    ]
    for copy in copies:
        copy.start()
    for copy in copies:
        copy.wait()
    me = lax.axis_index("label")
    scores, masked, is_positive = local_scores(
        me, short_ref, positive_ref, queries_ref, embeddings_ref
    )
    top = jnp.maximum(jnp.max(masked, axis=0, keepdims=True), LOWEST)
    total = jnp.sum(jnp.exp(masked - top), axis=0, keepdims=True)
    positive = jnp.sum(jnp.where(is_positive, scores, 0.0), axis=0, keepdims=True)
    rows = jnp.concatenate([top + jnp.log(total), positive], axis=0)
    out_ref[...] = jnp.broadcast_to(rows[None], out_ref.shape)


def gradient_kernel(
    short_ref, positive_ref, stats_ref, queries_ref, embeddings_ref,
    loss_ref, grad_ref, keep_ref, right_ref, left_ref, far_ref, part_ref,
):
    me = lax.axis_index("label")
    logs = stats_ref[:, 0, :]
    top = jnp.max(logs, axis=0, keepdims=True)
    log_total = top + jnp.log(jnp.sum(jnp.exp(logs - top), axis=0, keepdims=True))
    positive = jnp.sum(stats_ref[:, 1, :], axis=0, keepdims=True)
    loss_ref[...] = log_total - positive
    _, masked, is_positive = local_scores(me, short_ref, positive_ref, queries_ref, embeddings_ref)
    weights = jnp.exp(masked - log_total)
    gradient = jnp.where(is_positive, weights - 1.0, weights).astype(BF16)
    grad_ref[...] = gradient
    part_ref[...] = jnp.dot(gradient, queries_ref[...], preferred_element_type=F32)
    plane = lax.axis_index("dp")
    labels = part_ref.shape[0]
    deep = BLOCK // lax.axis_size("dp")
    blocks = labels // BLOCK
    for ref, shift in ((keep_ref, 0), (right_ref, 1), (left_ref, 3), (far_ref, 2)):
        kind = lax.rem(plane + shift, 4)
        for m in range(ref.shape[0]):
            start = pl.multiple_of((4 * m + kind) * deep, deep)
            rows = [part_ref[pl.ds(b * BLOCK + start, deep), :] for b in range(blocks)]
            ref[m] = jnp.concatenate(rows, axis=0).astype(ref.dtype)


def query_kernel(grad_ref, embeddings_ref, out_ref):
    out_ref[...] = lax.dot_general(
        grad_ref[...], embeddings_ref[...], (((0,), (0,)), ((), ())), preferred_element_type=F32
    ).astype(BF16)


def middle_kernel(
    parts_ref, a_ref, b_ref, c_ref, d_ref, spread_ref, keep_ref, right_ref, left_ref, far_ref
):
    total = parts_ref[0].astype(F32)
    for i in range(1, parts_ref.shape[0]):
        total = total + parts_ref[i].astype(F32)
    spread_ref[...] = jnp.broadcast_to(total.astype(BF16)[None], spread_ref.shape)
    mine = lax.axis_index("dp") // 4
    for ref, shift in ((keep_ref, 0), (right_ref, 1), (left_ref, 3), (far_ref, 2)):
        m = lax.rem(mine + shift, 4)
        total = a_ref[m] + b_ref[m].astype(F32) + c_ref[m].astype(F32) + d_ref[m].astype(F32)
        ref[...] = total.astype(ref.dtype)


def last_kernel(a_ref, b_ref, c_ref, d_ref, out_ref):
    total = a_ref[...] + b_ref[...].astype(F32) + c_ref[...].astype(F32) + d_ref[...].astype(F32)
    deep, blocks = out_ref.shape[:2]
    for b in range(blocks):
        out_ref[:, b, :] = total[b * deep : (b + 1) * deep]


def moved_by(x, shift):
    planes = lax.axis_size("dp")
    return lax.ppermute(x, "dp", [(i, (i + shift) % planes) for i in range(planes)])


def body(queries, embeddings, shortlist, positive):
    rows, width = queries.shape
    labels = embeddings.shape[0]
    groups, planes = lax.axis_size("label"), lax.axis_size("dp")
    shape = jax.ShapeDtypeStruct
    positive = positive.reshape(1, rows)
    madds = rows * labels * width
    chunk = labels // planes

    given = (shortlist, positive, queries, embeddings)
    stats = call(
        stats_kernel,
        shape((groups, 2, rows), F32),
        given,
        flops=2 * madds,
        scratch=[pltpu.VMEM(x.shape, x.dtype) for x in given] + [pltpu.SemaphoreType.DMA((4,))],
        any_inputs=4,
        vmem=VMEM_MOST,
    )
    stats = lax.all_to_all(stats, "label", 0, 0)
    losses, gradient, keep, right, left, far = call(
        gradient_kernel,
        (
            shape((1, rows), F32),
            shape((labels, rows), BF16),
            shape((planes // 4, chunk, width), F32),
        )
        + (shape((planes // 4, chunk, width), BF16),) * 3,
        (shortlist, positive, stats, queries, embeddings),
        flops=4 * madds,
        scratch=(pltpu.VMEM((labels, width), F32),),
    )
    right, left, far = moved_by(right, 1), moved_by(left, -1), moved_by(far, 2)
    query_part = call(query_kernel, shape((rows, width), BF16), (gradient, embeddings), flops=2 * madds)
    query_parts = lax.all_to_all(
        query_part.reshape(groups, rows // groups, width), "label", 0, 0
    )
    spread, keep, right, left, far = call(
        middle_kernel,
        (shape(query_parts.shape, BF16), shape((chunk, width), F32))
        + (shape((chunk, width), BF16),) * 3,
        (query_parts, keep, right, left, far),
    )
    query_grad = lax.all_to_all(spread, "label", 0, 0).reshape(rows, width)
    right, left, far = moved_by(right, 4), moved_by(left, -4), moved_by(far, 8)
    label_grad = call(
        last_kernel,
        shape((BLOCK // planes, labels // BLOCK, width), F32),
        (keep, right, left, far),
    )
    return losses.reshape(rows), query_grad, label_grad


def solution(mesh):
    in_specs = (P("dp", None), P("label", None), P("dp", None), P("dp"))
    out_specs = (P("dp"), P("dp", None), P("dp", "label", None))
    return jax.shard_map(body, mesh=mesh, in_specs=in_specs, out_specs=out_specs, check_vma=False)
```

time: 117 us -> 90.2 us (0.77)
  the two profiles are of different devices: /device:TPU:32 before, /device:TPU:1 now
where the time goes in v2:
time: 90.2 us; the launch traced here: 88.9 us
  starting transfers between devices  41.9 us (46%)
  waiting for transfers between devices  19 us (21%)
  blocking collectives  18.1 us (20%)
  Pallas kernels  8.16 us (9%)
    ppermute x6, starting transfers between devices, moved_by(): lax.ppermute(x, 'dp', [(i, (i + shift) % planes) for i in range(planes)])  29.8 us
    ppermute x6, waiting for transfers between devices, moved_by(): lax.ppermute(x, 'dp', [(i, (i + shift) % planes) for i in range(planes)])  19 us
    all_to_all x1, blocking collectives, body(): stats = lax.all_to_all(stats, 'label', 0, 0)  18.1 us
    pallas_call x5, Pallas kernels, call(): pl.pallas_call(kernel, out_shape=out_shape, in_specs=specs, out_specs=jax...  8.16 us
    all_to_all x1, starting transfers between devices, body(): query_grad = lax.all_to_all(spread, 'label', 0, 0).reshape(rows, width)  8.13 us
    all_to_all x1, starting transfers between devices, body(): lax.all_to_all(query_part.reshape(groups, rows // groups, width), 'label'...  3.97 us
  transfers between devices with their start and end apart: 8, of which 4 were waited for; matrix products, arithmetic and copies ran while one was open for 0% of the time, Pallas kernels for 1%

profile of v2, /device:TPU:1, one launch (start us, length us, event | category | flops | bytes accessed | tf_op | source)
XLA Modules:
  0.0 88.9 jit_solution(12811800360496145477)
XLA Ops:
  0.6 0.0 copy-start
  0.6 0.0 copy-start.1
  0.6 3.0 %shard_map.67 = f32[32,2,512]{2,1,0:T(2,128)} custom-call(s32[4,48]{1,0:T(4,128)} %short_ref.1, s32[1,512]{1,0:T(1,128)} %bitcast.4, bf16[512,768]{1,0:T(8,128)(2,1)} %queries_ref.1, bf16[512,768]{1,0:T(8,128)(2,1)} %embeddings_ref.3), custom_call_target="tpu_custom_call" | custom-call | flops 402653184 | bytes 2000000 | tf_op jit(solution)/shard_map/pallas_call | solution.py:19
  3.7 0.0 copy-start.2
  3.7 0.0 copy-start.3
  3.7 18.1 %all_to_all.15.stats_ref = f32[32,2,512]{2,1,0:T(2,128)S(1)} all-to-all(f32[32,2,512]{2,1,0:T(2,128)} %shard_map.67), channel_id=1, replica_groups=mesh['dp'=16,'label'=32] {'label'}, dimensions={0} | all-to-all | bytes 262144 | tf_op jit(solution)/shard_map/all_to_all | solution.py:160
  21.8 0.0 copy-done
  21.8 0.0 copy-done.1
  21.8 0.0 copy-done.2
  21.9 0.0 copy-done.3
  21.9 1.9 %shard_map.68 = (f32[1,512]{1,0:T(1,128)}, bf16[512,512]{1,0:T(8,128)(2,1)S(1)}, f32[4,32,768]{2,1,0:T(8,128)S(1)}, bf16[4,32,768]{2,1,0:T(8,128)(2,1)S(1)}, bf1...) custom-call(s32[4,48]{1,0:T(4,128)S(1)} %copy-done.2, s32[1,512]{1,0:T(1,128)S(1)} %bitcast.5, ...), custom_call_target="tpu_custom_call" | custom-call | flops 805306368 | bytes 2000000 | tf_op jit(solution)/shard_map/pallas_call | solution.py:19
  23.8 1.5 %shard_map.69 = bf16[512,768]{1,0:T(8,128)(2,1)} custom-call(bf16[512,512]{1,0:T(8,128)(2,1)S(1)} %get-tuple-element.15.grad_ref, bf16[512,768]{1,0:T(8,128)(2,1)S(1)} %copy-done), custom_call_target="tpu_custom_call" | custom-call | flops 402653184 | bytes 2000000 | tf_op jit(solution)/shard_map/pallas_call | solution.py:19
  25.3 4.0 %all-to-all-start.1 = ((bf16[32,16,768]{2,1,0:T(8,128)(2,1)}), bf16[32,16,768]{2,1,0:T(8,128)(2,1)S(1)}, u32[]{:S(2)}, u32[]{:S(2)}) async-start(bf16[32,16,768]{2,1,0:T(8,128)(2,1)} %bitcast.2), calls=%async_computation.1 | async-start | bytes 1572864 | tf_op jit(solution)/shard_map/all_to_all | solution.py:175
  29.3 1.9 %collective-permute-start = (bf16[4,32,768]{2,1,0:T(8,128)(2,1)S(1)}, bf16[4,32,768]{2,1,0:T(8,128)(2,1)S(1)}, u32[]{:S(2)}, u32[]{:S(2)}) collective-permute-start(bf16[4,32,768]{2,1,0:T(8,128)(2,1)S(1)} %get-tuple-element.17), channel_id=1, source_target_pairs={{0,32},{32,64},{64,96},{96,128},{128,160},{160,192},{192,224},{224... | collective-permute-start | bytes 589832 | tf_op jit(solution)/shard_map/ppermute | solution.py:138
  31.2 9.3 %collective-permute-start.1 = (bf16[4,32,768]{2,1,0:T(8,128)(2,1)S(1)}, bf16[4,32,768]{2,1,0:T(8,128)(2,1)S(1)}, u32[]{:S(2)}, u32[]{:S(2)}) collective-permute-start(bf16[4,32,768]{2,1,0:T(8,128)(2,1)S(1)} %get-tuple-element.18), channel_id=1, source_target_pairs={{0,480},{32,0},{64,32},{96,64},{128,96},{160,128},{192,160},{224,1... | collective-permute-start | bytes 589832 | tf_op jit(solution)/shard_map/ppermute | solution.py:138
  40.5 1.9 %collective-permute-start.2 = (bf16[4,32,768]{2,1,0:T(8,128)(2,1)S(1)}, bf16[4,32,768]{2,1,0:T(8,128)(2,1)S(1)}, u32[]{:S(2)}, u32[]{:S(2)}) collective-permute-start(bf16[4,32,768]{2,1,0:T(8,128)(2,1)S(1)} %get-tuple-element.19), channel_id=1, source_target_pairs={{0,64},{32,96},{64,128},{96,160},{128,192},{160,224},{192,256},{22... | collective-permute-start | bytes 589832 | tf_op jit(solution)/shard_map/ppermute | solution.py:138
  42.4 1.1 %collective-permute-done.b_ref = bf16[4,32,768]{2,1,0:T(8,128)(2,1)S(1)} collective-permute-done((bf16[4,32,768]{2,1,0:T(8,128)(2,1)S(1)}, bf16[4,32,768]{2,1,0:T(8,128)(2,1)S(1)}, u32[]{:S(2)}, u32[]{:S(2)}) %collective-permute-start) | collective-permute-done | bytes 196640 | tf_op jit(solution)/shard_map/ppermute | solution.py:138
  43.5 0.9 collective-permute-done.1.c_ref
  44.4 10.5 %collective-permute-done.2.d_ref = bf16[4,32,768]{2,1,0:T(8,128)(2,1)S(1)} collective-permute-done((bf16[4,32,768]{2,1,0:T(8,128)(2,1)S(1)}, bf16[4,32,768]{2,1,0:T(8,128)(2,1)S(1)}, u32[]{:S(2)}, u32[]{:S(2)}) %collective-permute-start.2) | collective-permute-done | bytes 196640 | tf_op jit(solution)/shard_map/ppermute | solution.py:138
  54.9 0.0 all-to-all-done.1.parts_ref
  54.9 1.0 %shard_map.70 = (bf16[32,16,768]{2,1,0:T(8,128)(2,1)}, f32[32,768]{1,0:T(8,128)S(1)}, bf16[32,768]{1,0:T(8,128)(2,1)S(1)}, bf16[32,768]{1,0:T(8,128)(2,1)S(1)}, bf16[32,768]{1,0:T(8,128)(2,1)S(1)}) custom-call(bf16[32,16,768]{2,1,0:T(8,128)(2,1)S(1)} %all-to-all-done.1.parts_ref, f32[4,32,768]{2,1,0:T(8,128)S(1)} %get-tuple-element.16.a_ref, ...), custom_call_target="tpu_custom_call" | custom-call | bytes 2000000 | tf_op jit(solution)/shard_map/pallas_call | solution.py:19
  55.9 8.1 %all-to-all-start.2 = ((bf16[32,16,768]{2,1,0:T(8,128)(2,1)}), bf16[32,16,768]{2,1,0:T(8,128)(2,1)S(1)}, u32[]{:S(2)}, u32[]{:S(2)}) async-start(bf16[32,16,768]{2,1,0:T(8,128)(2,1)} %get-tuple-element.20), calls=%async_computation.2 | async-start | bytes 1572864 | tf_op jit(solution)/shard_map/all_to_all | solution.py:184
  64.0 1.9 %collective-permute-start.3 = (bf16[32,768]{1,0:T(8,128)(2,1)S(1)}, bf16[32,768]{1,0:T(8,128)(2,1)S(1)}, u32[]{:S(2)}, u32[]{:S(2)}) collective-permute-start(bf16[32,768]{1,0:T(8,128)(2,1)S(1)} %get-tuple-element.22), channel_id=1, source_target_pairs={{0,128},{32,160},{64,192},{96,224},{128,256},{160,288},{192,320},{... | collective-permute-start | bytes 147464 | tf_op jit(solution)/shard_map/ppermute | solution.py:138
  66.0 7.3 %collective-permute-start.4 = (bf16[32,768]{1,0:T(8,128)(2,1)S(1)}, bf16[32,768]{1,0:T(8,128)(2,1)S(1)}, u32[]{:S(2)}, u32[]{:S(2)}) collective-permute-start(bf16[32,768]{1,0:T(8,128)(2,1)S(1)} %get-tuple-element.23), channel_id=1, source_target_pairs={{0,384},{32,416},{64,448},{96,480},{128,0},{160,32},{192,64},{224,... | collective-permute-start | bytes 147464 | tf_op jit(solution)/shard_map/ppermute | solution.py:138
  73.2 7.6 %collective-permute-start.5 = (bf16[32,768]{1,0:T(8,128)(2,1)S(1)}, bf16[32,768]{1,0:T(8,128)(2,1)S(1)}, u32[]{:S(2)}, u32[]{:S(2)}) collective-permute-start(bf16[32,768]{1,0:T(8,128)(2,1)S(1)} %get-tuple-element.24), channel_id=1, source_target_pairs={{0,256},{32,288},{64,320},{96,352},{128,384},{160,416},{192,448},{... | collective-permute-start | bytes 147464 | tf_op jit(solution)/shard_map/ppermute | solution.py:138
  80.8 0.0 collective-permute-done.3.b_ref
  80.8 0.0 collective-permute-done.4.c_ref
  80.8 6.5 %collective-permute-done.5.d_ref = bf16[32,768]{1,0:T(8,128)(2,1)S(1)} collective-permute-done((bf16[32,768]{1,0:T(8,128)(2,1)S(1)}, bf16[32,768]{1,0:T(8,128)(2,1)S(1)}, u32[]{:S(2)}, u32[]{:S(2)}) %collective-permute-start.5) | collective-permute-done | bytes 49184 | tf_op jit(solution)/shard_map/ppermute | solution.py:138
  87.3 0.7 shard_map.71
  88.0 0.0 all-to-all-done.2
  88.0 0.9 copy.8
Async XLA Ops:
  0.6 21.2 %copy-start = (bf16[512,768]{1,0:T(8,128)(2,1)S(1)}, bf16[512,768]{1,0:T(8,128)(2,1)}, u32[]{:S(2)}) copy-start(bf16[512,768]{1,0:T(8,128)(2,1)} %embeddings_ref.3) | copy-start | bytes 2359300
  0.6 21.2 %copy-start.1 = (bf16[512,768]{1,0:T(8,128)(2,1)S(1)}, bf16[512,768]{1,0:T(8,128)(2,1)}, u32[]{:S(2)}) copy-start(bf16[512,768]{1,0:T(8,128)(2,1)} %queries_ref.1) | copy-start | bytes 2359300
  3.7 18.2 %copy-start.2 = (s32[4,48]{1,0:T(4,128)S(1)}, s32[4,48]{1,0:T(4,128)}, u32[]{:S(2)}) copy-start(s32[4,48]{1,0:T(4,128)} %short_ref.1) | copy-start | bytes 2308
  3.7 18.2 %copy-start.3 = (s32[512]{0:T(512)S(1)}, s32[512]{0:T(512)}, u32[]{:S(2)}) copy-start(s32[512]{0:T(512)} %param.7) | copy-start | bytes 6148
  25.3 29.6 %all-to-all-start.1 = ((bf16[32,16,768]{2,1,0:T(8,128)(2,1)}), bf16[32,16,768]{2,1,0:T(8,128)(2,1)S(1)}, u32[]{:S(2)}, u32[]{:S(2)}) async-start(bf16[32,16,768]{2,1,0:T(8,128)(2,1)} %bitcast.2), calls=%async_computation.1 | async-start | bytes 1572864 | tf_op jit(solution)/shard_map/all_to_all | solution.py:175
  29.3 14.2 %collective-permute-start = (bf16[4,32,768]{2,1,0:T(8,128)(2,1)S(1)}, bf16[4,32,768]{2,1,0:T(8,128)(2,1)S(1)}, u32[]{:S(2)}, u32[]{:S(2)}) collective-permute-start(bf16[4,32,768]{2,1,0:T(8,128)(2,1)S(1)} %get-tuple-element.17), channel_id=1, source_target_pairs={{0,32},{32,64},{64,96},{96,128},{128,160},{160,192},{192,224},{224... | collective-permute-start | bytes 589832 | tf_op jit(solution)/shard_map/ppermute | solution.py:138
  31.2 13.2 %collective-permute-start.1 = (bf16[4,32,768]{2,1,0:T(8,128)(2,1)S(1)}, bf16[4,32,768]{2,1,0:T(8,128)(2,1)S(1)}, u32[]{:S(2)}, u32[]{:S(2)}) collective-permute-start(bf16[4,32,768]{2,1,0:T(8,128)(2,1)S(1)} %get-tuple-element.18), channel_id=1, source_target_pairs={{0,480},{32,0},{64,32},{96,64},{128,96},{160,128},{192,160},{224,1... | collective-permute-start | bytes 589832 | tf_op jit(solution)/shard_map/ppermute | solution.py:138
  40.5 14.4 %collective-permute-start.2 = (bf16[4,32,768]{2,1,0:T(8,128)(2,1)S(1)}, bf16[4,32,768]{2,1,0:T(8,128)(2,1)S(1)}, u32[]{:S(2)}, u32[]{:S(2)}) collective-permute-start(bf16[4,32,768]{2,1,0:T(8,128)(2,1)S(1)} %get-tuple-element.19), channel_id=1, source_target_pairs={{0,64},{32,96},{64,128},{96,160},{128,192},{160,224},{192,256},{22... | collective-permute-start | bytes 589832 | tf_op jit(solution)/shard_map/ppermute | solution.py:138
  55.9 32.1 %all-to-all-start.2 = ((bf16[32,16,768]{2,1,0:T(8,128)(2,1)}), bf16[32,16,768]{2,1,0:T(8,128)(2,1)S(1)}, u32[]{:S(2)}, u32[]{:S(2)}) async-start(bf16[32,16,768]{2,1,0:T(8,128)(2,1)} %get-tuple-element.20), calls=%async_computation.2 | async-start | bytes 1572864 | tf_op jit(solution)/shard_map/all_to_all | solution.py:184
  64.0 16.8 %collective-permute-start.3 = (bf16[32,768]{1,0:T(8,128)(2,1)S(1)}, bf16[32,768]{1,0:T(8,128)(2,1)S(1)}, u32[]{:S(2)}, u32[]{:S(2)}) collective-permute-start(bf16[32,768]{1,0:T(8,128)(2,1)S(1)} %get-tuple-element.22), channel_id=1, source_target_pairs={{0,128},{32,160},{64,192},{96,224},{128,256},{160,288},{192,320},{... | collective-permute-start | bytes 147464 | tf_op jit(solution)/shard_map/ppermute | solution.py:138
  66.0 14.9 %collective-permute-start.4 = (bf16[32,768]{1,0:T(8,128)(2,1)S(1)}, bf16[32,768]{1,0:T(8,128)(2,1)S(1)}, u32[]{:S(2)}, u32[]{:S(2)}) collective-permute-start(bf16[32,768]{1,0:T(8,128)(2,1)S(1)} %get-tuple-element.23), channel_id=1, source_target_pairs={{0,384},{32,416},{64,448},{96,480},{128,0},{160,32},{192,64},{224,... | collective-permute-start | bytes 147464 | tf_op jit(solution)/shard_map/ppermute | solution.py:138
  73.2 14.1 %collective-permute-start.5 = (bf16[32,768]{1,0:T(8,128)(2,1)S(1)}, bf16[32,768]{1,0:T(8,128)(2,1)S(1)}, u32[]{:S(2)}, u32[]{:S(2)}) collective-permute-start(bf16[32,768]{1,0:T(8,128)(2,1)S(1)} %get-tuple-element.24), channel_id=1, source_target_pairs={{0,256},{32,288},{64,320},{96,352},{128,384},{160,416},{192,448},{... | collective-permute-start | bytes 147464 | tf_op jit(solution)/shard_map/ppermute | solution.py:138

commit v3 on v2

--- a/solution.py
+++ b/solution.py
@@ -13,14 +13,16 @@
 BF16 = jnp.bfloat16
 
 
-def call(kernel, out_shape, args, flops=0, scratch=(), any_inputs=0, vmem=VMEM_LIMIT):
+def call(kernel, out_shape, args, flops=0, scratch=(), any_inputs=0, any_outputs=0, vmem=VMEM_LIMIT):
     specs = [pl.BlockSpec(memory_space=pltpu.HBM)] * any_inputs
     specs += [pl.BlockSpec(memory_space=pltpu.VMEM)] * (len(args) - any_inputs)
+    results = [pl.BlockSpec(memory_space=pltpu.VMEM)] * (len(out_shape) - any_outputs)
+    results += [pl.BlockSpec(memory_space=pltpu.HBM)] * any_outputs
     return pl.pallas_call(
         kernel,
         out_shape=out_shape,
         in_specs=specs,
-        out_specs=jax.tree.map(lambda _: pl.BlockSpec(memory_space=pltpu.VMEM), out_shape),
+        out_specs=tuple(results),
         scratch_shapes=list(scratch),
         compiler_params=pltpu.CompilerParams(vmem_limit_bytes=vmem),
         cost_estimate=pl.CostEstimate(flops=flops, bytes_accessed=2_000_000, transcendentals=0),
@@ -81,7 +83,7 @@
 
 def gradient_kernel(
     short_ref, positive_ref, stats_ref, queries_ref, embeddings_ref,
-    loss_ref, grad_ref, keep_ref, right_ref, left_ref, far_ref, part_ref,
+    loss_ref, query_ref, keep_ref, right_ref, left_ref, far_ref, part_ref,
 ):
     me = lax.axis_index("label")
     logs = stats_ref[:, 0, :]
@@ -92,7 +94,6 @@
     _, masked, is_positive = local_scores(me, short_ref, positive_ref, queries_ref, embeddings_ref)
     weights = jnp.exp(masked - log_total)
     gradient = jnp.where(is_positive, weights - 1.0, weights).astype(BF16)
-    grad_ref[...] = gradient
     part_ref[...] = jnp.dot(gradient, queries_ref[...], preferred_element_type=F32)
     plane = lax.axis_index("dp")
     labels = part_ref.shape[0]
@@ -104,11 +105,8 @@
             start = pl.multiple_of((4 * m + kind) * deep, deep)
             rows = [part_ref[pl.ds(b * BLOCK + start, deep), :] for b in range(blocks)]
             ref[m] = jnp.concatenate(rows, axis=0).astype(ref.dtype)
-
-
-def query_kernel(grad_ref, embeddings_ref, out_ref):
-    out_ref[...] = lax.dot_general(
-        grad_ref[...], embeddings_ref[...], (((0,), (0,)), ((), ())), preferred_element_type=F32
+    query_ref[...] = lax.dot_general(
+        gradient, embeddings_ref[...], (((0,), (0,)), ((), ())), preferred_element_type=F32
     ).astype(BF16)
 
 
@@ -126,16 +124,24 @@
         ref[...] = total.astype(ref.dtype)
 
 
-def last_kernel(a_ref, b_ref, c_ref, d_ref, out_ref):
+def last_kernel(a_ref, b_ref, c_ref, d_ref, query_ref, label_ref, query_hbm, sem):
+    copy = pltpu.make_async_copy(query_ref, query_hbm, sem)
+    copy.start()
     total = a_ref[...] + b_ref[...].astype(F32) + c_ref[...].astype(F32) + d_ref[...].astype(F32)
-    deep, blocks = out_ref.shape[:2]
+    deep, blocks = label_ref.shape[:2]
     for b in range(blocks):
-        out_ref[:, b, :] = total[b * deep : (b + 1) * deep]
+        label_ref[:, b, :] = total[b * deep : (b + 1) * deep]
+    copy.wait()
 
 
 def moved_by(x, shift):
     planes = lax.axis_size("dp")
     return lax.ppermute(x, "dp", [(i, (i + shift) % planes) for i in range(planes)])
+
+
+def moved_by_two(x):
+    planes = lax.axis_size("dp")
+    return lax.ppermute(x, "dp", [(i, (i + 2 - i % 2 * 4) % planes) for i in range(planes)])
 
 
 def body(queries, embeddings, shortlist, positive):
@@ -148,9 +154,9 @@
     chunk = labels // planes
 
     given = (shortlist, positive, queries, embeddings)
-    stats = call(
+    (stats,) = call(
         stats_kernel,
-        shape((groups, 2, rows), F32),
+        (shape((groups, 2, rows), F32),),
         given,
         flops=2 * madds,
         scratch=[pltpu.VMEM(x.shape, x.dtype) for x in given] + [pltpu.SemaphoreType.DMA((4,))],
@@ -158,20 +164,19 @@
         vmem=VMEM_MOST,
     )
     stats = lax.all_to_all(stats, "label", 0, 0)
-    losses, gradient, keep, right, left, far = call(
+    losses, query_part, keep, right, left, far = call(
         gradient_kernel,
         (
             shape((1, rows), F32),
-            shape((labels, rows), BF16),
+            shape((rows, width), BF16),
             shape((planes // 4, chunk, width), F32),
         )
         + (shape((planes // 4, chunk, width), BF16),) * 3,
         (shortlist, positive, stats, queries, embeddings),
-        flops=4 * madds,
-        scratch=(pltpu.VMEM((labels, width), F32),),
-    )
-    right, left, far = moved_by(right, 1), moved_by(left, -1), moved_by(far, 2)
-    query_part = call(query_kernel, shape((rows, width), BF16), (gradient, embeddings), flops=2 * madds)
+        flops=6 * madds,
+        scratch=[pltpu.VMEM((labels, width), F32)],
+    )
+    far, right, left = moved_by_two(far), moved_by(right, 1), moved_by(left, -1)
     query_parts = lax.all_to_all(
         query_part.reshape(groups, rows // groups, width), "label", 0, 0
     )
@@ -181,12 +186,17 @@
         + (shape((chunk, width), BF16),) * 3,
         (query_parts, keep, right, left, far),
     )
+    far, right, left = moved_by(far, 8), moved_by(right, 4), moved_by(left, -4)
     query_grad = lax.all_to_all(spread, "label", 0, 0).reshape(rows, width)
-    right, left, far = moved_by(right, 4), moved_by(left, -4), moved_by(far, 8)
-    label_grad = call(
+    label_grad, query_grad = call(
         last_kernel,
-        shape((BLOCK // planes, labels // BLOCK, width), F32),
-        (keep, right, left, far),
+        (
+            shape((BLOCK // planes, labels // BLOCK, width), F32),
+            shape((rows, width), BF16),
+        ),
+        (keep, right, left, far, query_grad),
+        scratch=[pltpu.SemaphoreType.DMA],
+        any_outputs=1,
     )
     return losses.reshape(rows), query_grad, label_grad
 

time: 90.2 us -> 85.3 us (0.946)
  waiting for transfers between devices: 19 us -> 13.1 us
  starting transfers between devices: 41.9 us -> 43.7 us
    ppermute x6 -> x5, waiting for transfers between devices: 19 us -> 7.16 us  [moved_by(): lax.ppermute(x, 'dp', [(i, (i + shift) % planes) for i in range(planes)])]
    ppermute x0 -> x1, waiting for transfers between devices: none -> 5.91 us  [moved_by_two(): lax.ppermute(x, 'dp', [(i, (i + 2 - i % 2 * 4) % planes) for i in range(p...]
    ppermute x0 -> x1, starting transfers between devices: none -> 1.92 us  [moved_by_two(): lax.ppermute(x, 'dp', [(i, (i + 2 - i % 2 * 4) % planes) for i in range(p...]
    ppermute x6 -> x5, starting transfers between devices: 29.8 us -> 29.2 us  [moved_by(): lax.ppermute(x, 'dp', [(i, (i + shift) % planes) for i in range(planes)])]
    pallas_call x5 -> x4, Pallas kernels: 8.16 us -> 8.3 us  [call(): pl.pallas_call(kernel, out_shape=out_shape, in_specs=specs, out_specs=tup...]
  transfers between devices with their start and end apart: 8 -> 8, of which waited for: 4 -> 4; matrix products, arithmetic and copies ran while one was open for 0% -> 0% of each run, Pallas kernels for 1% -> 0%
where the time goes in v3:
time: 85.3 us; the launch traced here: 84 us
  starting transfers between devices  43.7 us (51%)
  blocking collectives  18.1 us (21%)
  waiting for transfers between devices  13.1 us (15%)
  Pallas kernels  8.3 us (10%)
    ppermute x5, starting transfers between devices, moved_by(): lax.ppermute(x, 'dp', [(i, (i + shift) % planes) for i in range(planes)])  29.2 us
    all_to_all x1, blocking collectives, body(): stats = lax.all_to_all(stats, 'label', 0, 0)  18.1 us
    all_to_all x1, starting transfers between devices, body(): query_grad = lax.all_to_all(spread, 'label', 0, 0).reshape(rows, width)  8.63 us
    pallas_call x4, Pallas kernels, call(): pl.pallas_call(kernel, out_shape=out_shape, in_specs=specs, out_specs=tup...  8.3 us
    ppermute x5, waiting for transfers between devices, moved_by(): lax.ppermute(x, 'dp', [(i, (i + shift) % planes) for i in range(planes)])  7.16 us
    ppermute x1, waiting for transfers between devices, moved_by_two(): lax.ppermute(x, 'dp', [(i, (i + 2 - i % 2 * 4) % planes) for i in range(p...  5.91 us
    all_to_all x1, starting transfers between devices, body(): lax.all_to_all(query_part.reshape(groups, rows // groups, width), 'label'...  3.97 us
    ppermute x1, starting transfers between devices, moved_by_two(): lax.ppermute(x, 'dp', [(i, (i + 2 - i % 2 * 4) % planes) for i in range(p...  1.92 us
  transfers between devices with their start and end apart: 8, of which 4 were waited for; matrix products, arithmetic and copies ran while one was open for 0% of the time, Pallas kernels for 0%

profile of v3, /device:TPU:1, one launch (start us, length us, event | category | flops | bytes accessed | tf_op | source)
XLA Modules:
  0.0 84.0 jit_solution(14405989134876311038)
XLA Ops:
  0.6 0.0 copy-start
  0.6 0.0 copy-start.1
  0.6 3.0 %shard_map.67 = f32[32,2,512]{2,1,0:T(2,128)} custom-call(s32[4,48]{1,0:T(4,128)} %short_ref.1, s32[1,512]{1,0:T(1,128)} %bitcast.5, bf16[512,768]{1,0:T(8,128)(2,1)} %queries_ref.1, bf16[512,768]{1,0:T(8,128)(2,1)} %embeddings_ref.1), custom_call_target="tpu_custom_call" | custom-call | flops 402653184 | bytes 2000000 | tf_op jit(solution)/shard_map/pallas_call | solution.py:21
  3.7 0.0 copy-start.2
  3.7 0.0 copy-start.3
  3.7 18.1 %all_to_all.15.stats_ref = f32[32,2,512]{2,1,0:T(2,128)S(1)} all-to-all(f32[32,2,512]{2,1,0:T(2,128)} %shard_map.67), channel_id=1, replica_groups=mesh['dp'=16,'label'=32] {'label'}, dimensions={0} | all-to-all | bytes 262144 | tf_op jit(solution)/shard_map/all_to_all | solution.py:166
  21.8 0.0 copy-done
  21.8 0.0 copy-done.1
  21.8 0.0 copy-done.2
  21.9 0.0 copy-done.3
  21.9 2.7 %shard_map.68 = (f32[1,512]{1,0:T(1,128)}, bf16[512,768]{1,0:T(8,128)(2,1)}, f32[4,32,768]{2,1,0:T(8,128)S(1)}, bf16[4,32,768]{2,1,0:T(8,128)(2,1)S(1)}, bf16[4,...) custom-call(s32[4,48]{1,0:T(4,128)S(1)} %copy-done.2, s32[1,512]{1,0:T(1,128)S(1)} %bitcast.6, ...), custom_call_target="tpu_custom_call" | custom-call | flops 1207959552 | bytes 2000000 | tf_op jit(solution)/shard_map/pallas_call | solution.py:21
  24.6 4.0 %all-to-all-start.1 = ((bf16[32,16,768]{2,1,0:T(8,128)(2,1)}), bf16[32,16,768]{2,1,0:T(8,128)(2,1)S(1)}, u32[]{:S(2)}, u32[]{:S(2)}) async-start(bf16[32,16,768]{2,1,0:T(8,128)(2,1)} %bitcast.2), calls=%async_computation.1 | async-start | bytes 1572864 | tf_op jit(solution)/shard_map/all_to_all | solution.py:180
  28.6 1.9 %collective-permute-start = (bf16[4,32,768]{2,1,0:T(8,128)(2,1)S(1)}, bf16[4,32,768]{2,1,0:T(8,128)(2,1)S(1)}, u32[]{:S(2)}, u32[]{:S(2)}) collective-permute-start(bf16[4,32,768]{2,1,0:T(8,128)(2,1)S(1)} %get-tuple-element.19), channel_id=1, source_target_pairs={{0,32},{32,64},{64,96},{96,128},{128,160},{160,192},{192,224},{224... | collective-permute-start | bytes 589832 | tf_op jit(solution)/shard_map/ppermute | solution.py:139
  30.5 9.2 %collective-permute-start.1 = (bf16[4,32,768]{2,1,0:T(8,128)(2,1)S(1)}, bf16[4,32,768]{2,1,0:T(8,128)(2,1)S(1)}, u32[]{:S(2)}, u32[]{:S(2)}) collective-permute-start(bf16[4,32,768]{2,1,0:T(8,128)(2,1)S(1)} %get-tuple-element.20), channel_id=1, source_target_pairs={{0,480},{32,0},{64,32},{96,64},{128,96},{160,128},{192,160},{224,1... | collective-permute-start | bytes 589832 | tf_op jit(solution)/shard_map/ppermute | solution.py:139
  39.7 1.9 %collective-permute-start.2 = (bf16[4,32,768]{2,1,0:T(8,128)(2,1)S(1)}, bf16[4,32,768]{2,1,0:T(8,128)(2,1)S(1)}, u32[]{:S(2)}, u32[]{:S(2)}) collective-permute-start(bf16[4,32,768]{2,1,0:T(8,128)(2,1)S(1)} %get-tuple-element.21), channel_id=1, source_target_pairs={{0,64},{32,480},{64,128},{96,32},{128,192},{160,96},{192,256},{224... | collective-permute-start | bytes 589832 | tf_op jit(solution)/shard_map/ppermute | solution.py:144
  41.7 1.1 %collective-permute-done.b_ref = bf16[4,32,768]{2,1,0:T(8,128)(2,1)S(1)} collective-permute-done((bf16[4,32,768]{2,1,0:T(8,128)(2,1)S(1)}, bf16[4,32,768]{2,1,0:T(8,128)(2,1)S(1)}, u32[]{:S(2)}, u32[]{:S(2)}) %collective-permute-start) | collective-permute-done | bytes 196640 | tf_op jit(solution)/shard_map/ppermute | solution.py:139
  42.8 0.9 %collective-permute-done.1.c_ref = bf16[4,32,768]{2,1,0:T(8,128)(2,1)S(1)} collective-permute-done((bf16[4,32,768]{2,1,0:T(8,128)(2,1)S(1)}, bf16[4,32,768]{2,1,0:T(8,128)(2,1)S(1)}, u32[]{:S(2)}, u32[]{:S(2)}) %collective-permute-start.1) | collective-permute-done | bytes 196640 | tf_op jit(solution)/shard_map/ppermute | solution.py:139
  43.7 5.9 %collective-permute-done.2.d_ref = bf16[4,32,768]{2,1,0:T(8,128)(2,1)S(1)} collective-permute-done((bf16[4,32,768]{2,1,0:T(8,128)(2,1)S(1)}, bf16[4,32,768]{2,1,0:T(8,128)(2,1)S(1)}, u32[]{:S(2)}, u32[]{:S(2)}) %collective-permute-start.2) | collective-permute-done | bytes 196640 | tf_op jit(solution)/shard_map/ppermute | solution.py:144
  49.6 0.0 all-to-all-done.1.parts_ref
  49.6 1.0 %shard_map.69 = (bf16[32,16,768]{2,1,0:T(8,128)(2,1)}, f32[32,768]{1,0:T(8,128)S(1)}, bf16[32,768]{1,0:T(8,128)(2,1)S(1)}, bf16[32,768]{1,0:T(8,128)(2,1)S(1)}, bf16[32,768]{1,0:T(8,128)(2,1)S(1)}) custom-call(bf16[32,16,768]{2,1,0:T(8,128)(2,1)S(1)} %all-to-all-done.1.parts_ref, f32[4,32,768]{2,1,0:T(8,128)S(1)} %get-tuple-element.18.a_ref, ...), custom_call_target="tpu_custom_call" | custom-call | bytes 2000000 | tf_op jit(solution)/shard_map/pallas_call | solution.py:21
  50.6 8.6 %all-to-all-start.2 = ((bf16[32,16,768]{2,1,0:T(8,128)(2,1)}), bf16[32,16,768]{2,1,0:T(8,128)(2,1)S(1)}, u32[]{:S(2)}, u32[]{:S(2)}) async-start(bf16[32,16,768]{2,1,0:T(8,128)(2,1)} %get-tuple-element.26), calls=%async_computation.2 | async-start | bytes 1572864 | tf_op jit(solution)/shard_map/all_to_all | solution.py:190
  59.2 2.2 %collective-permute-start.3 = (bf16[32,768]{1,0:T(8,128)(2,1)S(1)}, bf16[32,768]{1,0:T(8,128)(2,1)S(1)}, u32[]{:S(2)}, u32[]{:S(2)}) collective-permute-start(bf16[32,768]{1,0:T(8,128)(2,1)S(1)} %get-tuple-element.23), channel_id=1, source_target_pairs={{0,128},{32,160},{64,192},{96,224},{128,256},{160,288},{192,320},{... | collective-permute-start | bytes 147464 | tf_op jit(solution)/shard_map/ppermute | solution.py:139
  61.5 6.9 %collective-permute-start.4 = (bf16[32,768]{1,0:T(8,128)(2,1)S(1)}, bf16[32,768]{1,0:T(8,128)(2,1)S(1)}, u32[]{:S(2)}, u32[]{:S(2)}) collective-permute-start(bf16[32,768]{1,0:T(8,128)(2,1)S(1)} %get-tuple-element.24), channel_id=1, source_target_pairs={{0,384},{32,416},{64,448},{96,480},{128,0},{160,32},{192,64},{224,... | collective-permute-start | bytes 147464 | tf_op jit(solution)/shard_map/ppermute | solution.py:139
  68.4 8.9 %collective-permute-start.5 = (bf16[32,768]{1,0:T(8,128)(2,1)S(1)}, bf16[32,768]{1,0:T(8,128)(2,1)S(1)}, u32[]{:S(2)}, u32[]{:S(2)}) collective-permute-start(bf16[32,768]{1,0:T(8,128)(2,1)S(1)} %get-tuple-element.25), channel_id=1, source_target_pairs={{0,256},{32,288},{64,320},{96,352},{128,384},{160,416},{192,448},{... | collective-permute-start | bytes 147464 | tf_op jit(solution)/shard_map/ppermute | solution.py:139
  77.3 0.0 collective-permute-done.3.b_ref
  77.3 0.0 collective-permute-done.4.c_ref
  77.3 5.2 %collective-permute-done.5.d_ref = bf16[32,768]{1,0:T(8,128)(2,1)S(1)} collective-permute-done((bf16[32,768]{1,0:T(8,128)(2,1)S(1)}, bf16[32,768]{1,0:T(8,128)(2,1)S(1)}, u32[]{:S(2)}, u32[]{:S(2)}) %collective-permute-start.5) | collective-permute-done | bytes 49184 | tf_op jit(solution)/shard_map/ppermute | solution.py:139
  82.5 0.0 all-to-all-done.2
  82.5 1.5 %shard_map.70 = (f32[8,4,768]{2,1,0:T(4,128)}, bf16[512,768]{1,0:T(8,128)(2,1)}) custom-call(f32[32,768]{1,0:T(8,128)S(1)} %get-tuple-element.22.a_ref, bf16[32,768]{1,0:T(8,128)(2,1)S(1)} %collective-permute-done.3.b_ref, bf16[32,768]{1,0:T(8,128)(2,1)S(1)} %collective-permute-done.4.c_ref, bf16[32,768]{1,0:T(8,128)(2,1)S(1)} %collective-permute-done.5.d_ref, ...), custom_call_target="tpu_custom_call" | custom-call | bytes 2000000 | tf_op jit(solution)/shard_map/pallas_call | solution.py:21
Async XLA Ops:
  0.6 21.2 %copy-start = (bf16[512,768]{1,0:T(8,128)(2,1)S(1)}, bf16[512,768]{1,0:T(8,128)(2,1)}, u32[]{:S(2)}) copy-start(bf16[512,768]{1,0:T(8,128)(2,1)} %queries_ref.1) | copy-start | bytes 2359300
  0.6 21.2 %copy-start.1 = (bf16[512,768]{1,0:T(8,128)(2,1)S(1)}, bf16[512,768]{1,0:T(8,128)(2,1)}, u32[]{:S(2)}) copy-start(bf16[512,768]{1,0:T(8,128)(2,1)} %embeddings_ref.1) | copy-start | bytes 2359300
  3.7 18.2 %copy-start.2 = (s32[4,48]{1,0:T(4,128)S(1)}, s32[4,48]{1,0:T(4,128)}, u32[]{:S(2)}) copy-start(s32[4,48]{1,0:T(4,128)} %short_ref.1) | copy-start | bytes 2308
  3.7 18.2 %copy-start.3 = (s32[512]{0:T(512)S(1)}, s32[512]{0:T(512)}, u32[]{:S(2)}) copy-start(s32[512]{0:T(512)} %param.7) | copy-start | bytes 6148
  24.6 25.0 %all-to-all-start.1 = ((bf16[32,16,768]{2,1,0:T(8,128)(2,1)}), bf16[32,16,768]{2,1,0:T(8,128)(2,1)S(1)}, u32[]{:S(2)}, u32[]{:S(2)}) async-start(bf16[32,16,768]{2,1,0:T(8,128)(2,1)} %bitcast.2), calls=%async_computation.1 | async-start | bytes 1572864 | tf_op jit(solution)/shard_map/all_to_all | solution.py:180
  28.6 14.2 %collective-permute-start = (bf16[4,32,768]{2,1,0:T(8,128)(2,1)S(1)}, bf16[4,32,768]{2,1,0:T(8,128)(2,1)S(1)}, u32[]{:S(2)}, u32[]{:S(2)}) collective-permute-start(bf16[4,32,768]{2,1,0:T(8,128)(2,1)S(1)} %get-tuple-element.19), channel_id=1, source_target_pairs={{0,32},{32,64},{64,96},{96,128},{128,160},{160,192},{192,224},{224... | collective-permute-start | bytes 589832 | tf_op jit(solution)/shard_map/ppermute | solution.py:139
  30.5 13.2 %collective-permute-start.1 = (bf16[4,32,768]{2,1,0:T(8,128)(2,1)S(1)}, bf16[4,32,768]{2,1,0:T(8,128)(2,1)S(1)}, u32[]{:S(2)}, u32[]{:S(2)}) collective-permute-start(bf16[4,32,768]{2,1,0:T(8,128)(2,1)S(1)} %get-tuple-element.20), channel_id=1, source_target_pairs={{0,480},{32,0},{64,32},{96,64},{128,96},{160,128},{192,160},{224,1... | collective-permute-start | bytes 589832 | tf_op jit(solution)/shard_map/ppermute | solution.py:139
  39.7 9.8 %collective-permute-start.2 = (bf16[4,32,768]{2,1,0:T(8,128)(2,1)S(1)}, bf16[4,32,768]{2,1,0:T(8,128)(2,1)S(1)}, u32[]{:S(2)}, u32[]{:S(2)}) collective-permute-start(bf16[4,32,768]{2,1,0:T(8,128)(2,1)S(1)} %get-tuple-element.21), channel_id=1, source_target_pairs={{0,64},{32,480},{64,128},{96,32},{128,192},{160,96},{192,256},{224... | collective-permute-start | bytes 589832 | tf_op jit(solution)/shard_map/ppermute | solution.py:144
  50.6 31.9 %all-to-all-start.2 = ((bf16[32,16,768]{2,1,0:T(8,128)(2,1)}), bf16[32,16,768]{2,1,0:T(8,128)(2,1)S(1)}, u32[]{:S(2)}, u32[]{:S(2)}) async-start(bf16[32,16,768]{2,1,0:T(8,128)(2,1)} %get-tuple-element.26), calls=%async_computation.2 | async-start | bytes 1572864 | tf_op jit(solution)/shard_map/all_to_all | solution.py:190
  59.2 18.1 %collective-permute-start.3 = (bf16[32,768]{1,0:T(8,128)(2,1)S(1)}, bf16[32,768]{1,0:T(8,128)(2,1)S(1)}, u32[]{:S(2)}, u32[]{:S(2)}) collective-permute-start(bf16[32,768]{1,0:T(8,128)(2,1)S(1)} %get-tuple-element.23), channel_id=1, source_target_pairs={{0,128},{32,160},{64,192},{96,224},{128,256},{160,288},{192,320},{... | collective-permute-start | bytes 147464 | tf_op jit(solution)/shard_map/ppermute | solution.py:139
  61.5 15.8 %collective-permute-start.4 = (bf16[32,768]{1,0:T(8,128)(2,1)S(1)}, bf16[32,768]{1,0:T(8,128)(2,1)S(1)}, u32[]{:S(2)}, u32[]{:S(2)}) collective-permute-start(bf16[32,768]{1,0:T(8,128)(2,1)S(1)} %get-tuple-element.24), channel_id=1, source_target_pairs={{0,384},{32,416},{64,448},{96,480},{128,0},{160,32},{192,64},{224,... | collective-permute-start | bytes 147464 | tf_op jit(solution)/shard_map/ppermute | solution.py:139
  68.4 14.1 %collective-permute-start.5 = (bf16[32,768]{1,0:T(8,128)(2,1)S(1)}, bf16[32,768]{1,0:T(8,128)(2,1)S(1)}, u32[]{:S(2)}, u32[]{:S(2)}) collective-permute-start(bf16[32,768]{1,0:T(8,128)(2,1)S(1)} %get-tuple-element.25), channel_id=1, source_target_pairs={{0,256},{32,288},{64,320},{96,352},{128,384},{160,416},{192,448},{... | collective-permute-start | bytes 147464 | tf_op jit(solution)/shard_map/ppermute | solution.py:139

commit v4 on v3

--- a/solution.py
+++ b/solution.py
@@ -9,6 +9,7 @@
 LOWEST = -3.4028234e38
 VMEM_LIMIT = 24 * 1024 * 1024
 VMEM_MOST = 62_000_000
+LONG = 60_000_000_000
 F32 = jnp.float32
 BF16 = jnp.bfloat16
 
@@ -110,24 +111,25 @@
     ).astype(BF16)
 
 
-def middle_kernel(
-    parts_ref, a_ref, b_ref, c_ref, d_ref, spread_ref, keep_ref, right_ref, left_ref, far_ref
-):
+def spread_kernel(parts_ref, spread_ref):
     total = parts_ref[0].astype(F32)
     for i in range(1, parts_ref.shape[0]):
         total = total + parts_ref[i].astype(F32)
     spread_ref[...] = jnp.broadcast_to(total.astype(BF16)[None], spread_ref.shape)
+
+
+def middle_kernel(_, a_ref, b_ref, c_ref, d_ref, keep_ref, right_ref, left_ref, far_ref):
     mine = lax.axis_index("dp") // 4
-    for ref, shift in ((keep_ref, 0), (right_ref, 1), (left_ref, 3), (far_ref, 2)):
+    for ref, shift in ((far_ref, 2), (keep_ref, 0), (right_ref, 1), (left_ref, 3)):
         m = lax.rem(mine + shift, 4)
-        total = a_ref[m] + b_ref[m].astype(F32) + c_ref[m].astype(F32) + d_ref[m].astype(F32)
+        total = a_ref[m].astype(F32) + b_ref[m].astype(F32) + c_ref[m].astype(F32) + d_ref[m].astype(F32)
         ref[...] = total.astype(ref.dtype)
 
 
 def last_kernel(a_ref, b_ref, c_ref, d_ref, query_ref, label_ref, query_hbm, sem):
     copy = pltpu.make_async_copy(query_ref, query_hbm, sem)
     copy.start()
-    total = a_ref[...] + b_ref[...].astype(F32) + c_ref[...].astype(F32) + d_ref[...].astype(F32)
+    total = a_ref[...].astype(F32) + b_ref[...].astype(F32) + c_ref[...].astype(F32) + d_ref[...]
     deep, blocks = label_ref.shape[:2]
     for b in range(blocks):
         label_ref[:, b, :] = total[b * deep : (b + 1) * deep]
@@ -180,21 +182,25 @@
     query_parts = lax.all_to_all(
         query_part.reshape(groups, rows // groups, width), "label", 0, 0
     )
-    spread, keep, right, left, far = call(
+    (spread,) = call(
+        spread_kernel, (shape(query_parts.shape, BF16),), (query_parts,), flops=LONG
+    )
+    query_grad = lax.all_to_all(spread, "label", 0, 0).reshape(rows, width)
+    keep, right, left, far = call(
         middle_kernel,
-        (shape(query_parts.shape, BF16), shape((chunk, width), F32))
-        + (shape((chunk, width), BF16),) * 3,
-        (query_parts, keep, right, left, far),
+        (shape((chunk, width), F32),) + (shape((chunk, width), BF16),) * 3,
+        (spread, far, right, left, keep),
+        any_inputs=1,
+        flops=LONG,
     )
     far, right, left = moved_by(far, 8), moved_by(right, 4), moved_by(left, -4)
-    query_grad = lax.all_to_all(spread, "label", 0, 0).reshape(rows, width)
     label_grad, query_grad = call(
         last_kernel,
         (
             shape((BLOCK // planes, labels // BLOCK, width), F32),
             shape((rows, width), BF16),
         ),
-        (keep, right, left, far, query_grad),
+        (far, right, left, keep, query_grad),
         scratch=[pltpu.SemaphoreType.DMA],
         any_outputs=1,
     )

time: 85.3 us -> 78.7 us (0.923)
  the two profiles are of different devices: /device:TPU:1 before, /device:TPU:12 now
where the time goes in v4:
time: 78.7 us; the launch traced here: 78.1 us
  starting transfers between devices  49 us (62%)
  blocking collectives  14.1 us (18%)
  Pallas kernels  8.39 us (11%)
  waiting for transfers between devices  5.88 us (7%)
  between operations  0.79 us (1%)
    ppermute x5, starting transfers between devices, moved_by(): lax.ppermute(x, 'dp', [(i, (i + shift) % planes) for i in range(planes)])  31.3 us
    all_to_all x1, blocking collectives, body(): stats = lax.all_to_all(stats, 'label', 0, 0)  14.1 us
    pallas_call x5, Pallas kernels, call(): pl.pallas_call(kernel, out_shape=out_shape, in_specs=specs, out_specs=tup...  8.39 us
    all_to_all x1, starting transfers between devices, body(): query_grad = lax.all_to_all(spread, 'label', 0, 0).reshape(rows, width)  7.42 us
    all_to_all x1, starting transfers between devices, body(): lax.all_to_all(query_part.reshape(groups, rows // groups, width), 'label'...  7.01 us
    ppermute x5, waiting for transfers between devices, moved_by(): lax.ppermute(x, 'dp', [(i, (i + shift) % planes) for i in range(planes)])  5.87 us
    ppermute x1, starting transfers between devices, moved_by_two(): lax.ppermute(x, 'dp', [(i, (i + 2 - i % 2 * 4) % planes) for i in range(p...  3.28 us
  transfers between devices with their start and end apart: 8, of which 2 were waited for; matrix products, arithmetic and copies ran while one was open for 0% of the time, Pallas kernels for 1%

profile of v4, /device:TPU:12, one launch (start us, length us, event | category | flops | bytes accessed | tf_op | source)
XLA Modules:
  0.0 78.1 jit_solution(4255065569244388974)
XLA Ops:
  0.6 0.0 copy-start
  0.6 0.0 copy-start.1
  0.6 3.0 %shard_map.67 = f32[32,2,512]{2,1,0:T(2,128)} custom-call(s32[4,48]{1,0:T(4,128)} %short_ref.1, s32[1,512]{1,0:T(1,128)} %bitcast.5, bf16[512,768]{1,0:T(8,128)(2,1)} %queries_ref.1, bf16[512,768]{1,0:T(8,128)(2,1)} %embeddings_ref.1), custom_call_target="tpu_custom_call" | custom-call | flops 402653184 | bytes 2000000 | tf_op jit(solution)/shard_map/pallas_call | solution.py:22
  3.7 0.0 copy-start.2
  3.7 0.0 copy-start.3
  3.7 14.1 %all_to_all.15.stats_ref = f32[32,2,512]{2,1,0:T(2,128)S(1)} all-to-all(f32[32,2,512]{2,1,0:T(2,128)} %shard_map.67), channel_id=1, replica_groups=mesh['dp'=16,'label'=32] {'label'}, dimensions={0} | all-to-all | bytes 262144 | tf_op jit(solution)/shard_map/all_to_all | solution.py:168
  17.8 0.0 copy-done
  17.8 0.0 copy-done.1
  17.8 0.0 copy-done.2
  17.8 0.0 copy-done.3
  17.8 2.7 %shard_map.68 = (f32[1,512]{1,0:T(1,128)}, bf16[512,768]{1,0:T(8,128)(2,1)}, f32[4,32,768]{2,1,0:T(8,128)S(1)}, bf16[4,32,768]{2,1,0:T(8,128)(2,1)S(1)}, bf16[4,...) custom-call(s32[4,48]{1,0:T(4,128)S(1)} %copy-done.2, s32[1,512]{1,0:T(1,128)S(1)} %bitcast.6, ...), custom_call_target="tpu_custom_call" | custom-call | flops 1207959552 | bytes 2000000 | tf_op jit(solution)/shard_map/pallas_call | solution.py:22
  20.5 7.0 %all-to-all-start.1 = ((bf16[32,16,768]{2,1,0:T(8,128)(2,1)}), bf16[32,16,768]{2,1,0:T(8,128)(2,1)S(1)}, u32[]{:S(2)}, u32[]{:S(2)}) async-start(bf16[32,16,768]{2,1,0:T(8,128)(2,1)} %bitcast.2), calls=%async_computation.1 | async-start | bytes 1572864 | tf_op jit(solution)/shard_map/all_to_all | solution.py:182
  27.5 3.3 %collective-permute-start = (bf16[4,32,768]{2,1,0:T(8,128)(2,1)S(1)}, bf16[4,32,768]{2,1,0:T(8,128)(2,1)S(1)}, u32[]{:S(2)}, u32[]{:S(2)}) collective-permute-start(bf16[4,32,768]{2,1,0:T(8,128)(2,1)S(1)} %get-tuple-element.17), channel_id=1, source_target_pairs={{0,64},{32,480},{64,128},{96,32},{128,192},{160,96},{192,256},{224... | collective-permute-start | bytes 589832 | tf_op jit(solution)/shard_map/ppermute | solution.py:146
  30.8 9.6 %collective-permute-start.1 = (bf16[4,32,768]{2,1,0:T(8,128)(2,1)S(1)}, bf16[4,32,768]{2,1,0:T(8,128)(2,1)S(1)}, u32[]{:S(2)}, u32[]{:S(2)}) collective-permute-start(bf16[4,32,768]{2,1,0:T(8,128)(2,1)S(1)} %get-tuple-element.18), channel_id=1, source_target_pairs={{0,32},{32,64},{64,96},{96,128},{128,160},{160,192},{192,224},{224... | collective-permute-start | bytes 589832 | tf_op jit(solution)/shard_map/ppermute | solution.py:141
  40.4 1.9 %collective-permute-start.2 = (bf16[4,32,768]{2,1,0:T(8,128)(2,1)S(1)}, bf16[4,32,768]{2,1,0:T(8,128)(2,1)S(1)}, u32[]{:S(2)}, u32[]{:S(2)}) collective-permute-start(bf16[4,32,768]{2,1,0:T(8,128)(2,1)S(1)} %get-tuple-element.19), channel_id=1, source_target_pairs={{0,480},{32,0},{64,32},{96,64},{128,96},{160,128},{192,160},{224,1... | collective-permute-start | bytes 589832 | tf_op jit(solution)/shard_map/ppermute | solution.py:141
  42.4 0.0 all-to-all-done.1.parts_ref
  42.4 1.0 %shard_map.69._ = bf16[32,16,768]{2,1,0:T(8,128)(2,1)} custom-call(bf16[32,16,768]{2,1,0:T(8,128)(2,1)S(1)} %all-to-all-done.1.parts_ref), custom_call_target="tpu_custom_call" | custom-call | flops 60000002048 | bytes 2000000 | tf_op jit(solution)/shard_map/pallas_call | solution.py:22
  43.4 7.4 %all-to-all-start.2 = ((bf16[32,16,768]{2,1,0:T(8,128)(2,1)}), bf16[32,16,768]{2,1,0:T(8,128)(2,1)S(1)}, u32[]{:S(2)}, u32[]{:S(2)}) async-start(bf16[32,16,768]{2,1,0:T(8,128)(2,1)} %shard_map.69._), calls=%async_computation.2 | async-start | bytes 1572864 | tf_op jit(solution)/shard_map/all_to_all | solution.py:188
  50.8 0.0 collective-permute-done.a_ref
  50.8 0.0 collective-permute-done.1.b_ref
  50.8 0.0 collective-permute-done.2.c_ref
  50.8 0.1 shard_map.70
  50.9 10.0 %collective-permute-start.3 = (bf16[32,768]{1,0:T(8,128)(2,1)S(1)}, bf16[32,768]{1,0:T(8,128)(2,1)S(1)}, u32[]{:S(2)}, u32[]{:S(2)}) collective-permute-start(bf16[32,768]{1,0:T(8,128)(2,1)S(1)} %get-tuple-element.21), channel_id=1, source_target_pairs={{0,256},{32,288},{64,320},{96,352},{128,384},{160,416},{192,448},{... | collective-permute-start | bytes 147464 | tf_op jit(solution)/shard_map/ppermute | solution.py:141
  61.0 4.3 %collective-permute-start.4 = (bf16[32,768]{1,0:T(8,128)(2,1)S(1)}, bf16[32,768]{1,0:T(8,128)(2,1)S(1)}, u32[]{:S(2)}, u32[]{:S(2)}) collective-permute-start(bf16[32,768]{1,0:T(8,128)(2,1)S(1)} %get-tuple-element.22), channel_id=1, source_target_pairs={{0,128},{32,160},{64,192},{96,224},{128,256},{160,288},{192,320},{... | collective-permute-start | bytes 147464 | tf_op jit(solution)/shard_map/ppermute | solution.py:141
  65.3 5.5 %collective-permute-start.5 = (bf16[32,768]{1,0:T(8,128)(2,1)S(1)}, bf16[32,768]{1,0:T(8,128)(2,1)S(1)}, u32[]{:S(2)}, u32[]{:S(2)}) collective-permute-start(bf16[32,768]{1,0:T(8,128)(2,1)S(1)} %get-tuple-element.23), channel_id=1, source_target_pairs={{0,384},{32,416},{64,448},{96,480},{128,0},{160,32},{192,64},{224,... | collective-permute-start | bytes 147464 | tf_op jit(solution)/shard_map/ppermute | solution.py:141
  70.7 0.0 collective-permute-done.3.a_ref
  70.8 1.3 %collective-permute-done.4.b_ref = bf16[32,768]{1,0:T(8,128)(2,1)S(1)} collective-permute-done((bf16[32,768]{1,0:T(8,128)(2,1)S(1)}, bf16[32,768]{1,0:T(8,128)(2,1)S(1)}, u32[]{:S(2)}, u32[]{:S(2)}) %collective-permute-start.4) | collective-permute-done | bytes 49184 | tf_op jit(solution)/shard_map/ppermute | solution.py:141
  72.0 4.6 %collective-permute-done.5.c_ref = bf16[32,768]{1,0:T(8,128)(2,1)S(1)} collective-permute-done((bf16[32,768]{1,0:T(8,128)(2,1)S(1)}, bf16[32,768]{1,0:T(8,128)(2,1)S(1)}, u32[]{:S(2)}, u32[]{:S(2)}) %collective-permute-start.5) | collective-permute-done | bytes 49184 | tf_op jit(solution)/shard_map/ppermute | solution.py:141
  76.6 0.0 all-to-all-done.2
  76.6 1.5 %shard_map.71 = (f32[8,4,768]{2,1,0:T(4,128)}, bf16[512,768]{1,0:T(8,128)(2,1)}) custom-call(bf16[32,768]{1,0:T(8,128)(2,1)S(1)} %collective-permute-done.3.a_ref, bf16[32,768]{1,0:T(8,128)(2,1)S(1)} %collective-permute-done.4.b_ref, bf16[32,768]{1,0:T(8,128)(2,1)S(1)} %collective-permute-done.5.c_ref, f32[32,768]{1,0:T(8,128)S(1)} %get-tuple-element.24.d_ref, ...), custom_call_target="tpu_custom_call" | custom-call | bytes 2000000 | tf_op jit(solution)/shard_map/pallas_call | solution.py:22
Async XLA Ops:
  0.6 17.1 %copy-start = (bf16[512,768]{1,0:T(8,128)(2,1)S(1)}, bf16[512,768]{1,0:T(8,128)(2,1)}, u32[]{:S(2)}) copy-start(bf16[512,768]{1,0:T(8,128)(2,1)} %queries_ref.1) | copy-start | bytes 2359300
  0.6 17.1 %copy-start.1 = (bf16[512,768]{1,0:T(8,128)(2,1)S(1)}, bf16[512,768]{1,0:T(8,128)(2,1)}, u32[]{:S(2)}) copy-start(bf16[512,768]{1,0:T(8,128)(2,1)} %embeddings_ref.1) | copy-start | bytes 2359300
  3.7 14.1 %copy-start.2 = (s32[4,48]{1,0:T(4,128)S(1)}, s32[4,48]{1,0:T(4,128)}, u32[]{:S(2)}) copy-start(s32[4,48]{1,0:T(4,128)} %short_ref.1) | copy-start | bytes 2308
  3.7 14.1 %copy-start.3 = (s32[512]{0:T(512)S(1)}, s32[512]{0:T(512)}, u32[]{:S(2)}) copy-start(s32[512]{0:T(512)} %param.7) | copy-start | bytes 6148
  20.5 21.8 %all-to-all-start.1 = ((bf16[32,16,768]{2,1,0:T(8,128)(2,1)}), bf16[32,16,768]{2,1,0:T(8,128)(2,1)S(1)}, u32[]{:S(2)}, u32[]{:S(2)}) async-start(bf16[32,16,768]{2,1,0:T(8,128)(2,1)} %bitcast.2), calls=%async_computation.1 | async-start | bytes 1572864 | tf_op jit(solution)/shard_map/all_to_all | solution.py:182
  27.5 23.3 %collective-permute-start = (bf16[4,32,768]{2,1,0:T(8,128)(2,1)S(1)}, bf16[4,32,768]{2,1,0:T(8,128)(2,1)S(1)}, u32[]{:S(2)}, u32[]{:S(2)}) collective-permute-start(bf16[4,32,768]{2,1,0:T(8,128)(2,1)S(1)} %get-tuple-element.17), channel_id=1, source_target_pairs={{0,64},{32,480},{64,128},{96,32},{128,192},{160,96},{192,256},{224... | collective-permute-start | bytes 589832 | tf_op jit(solution)/shard_map/ppermute | solution.py:146
  30.8 20.0 %collective-permute-start.1 = (bf16[4,32,768]{2,1,0:T(8,128)(2,1)S(1)}, bf16[4,32,768]{2,1,0:T(8,128)(2,1)S(1)}, u32[]{:S(2)}, u32[]{:S(2)}) collective-permute-start(bf16[4,32,768]{2,1,0:T(8,128)(2,1)S(1)} %get-tuple-element.18), channel_id=1, source_target_pairs={{0,32},{32,64},{64,96},{96,128},{128,160},{160,192},{192,224},{224... | collective-permute-start | bytes 589832 | tf_op jit(solution)/shard_map/ppermute | solution.py:141
  40.4 10.4 %collective-permute-start.2 = (bf16[4,32,768]{2,1,0:T(8,128)(2,1)S(1)}, bf16[4,32,768]{2,1,0:T(8,128)(2,1)S(1)}, u32[]{:S(2)}, u32[]{:S(2)}) collective-permute-start(bf16[4,32,768]{2,1,0:T(8,128)(2,1)S(1)} %get-tuple-element.19), channel_id=1, source_target_pairs={{0,480},{32,0},{64,32},{96,64},{128,96},{160,128},{192,160},{224,1... | collective-permute-start | bytes 589832 | tf_op jit(solution)/shard_map/ppermute | solution.py:141
  43.4 33.3 %all-to-all-start.2 = ((bf16[32,16,768]{2,1,0:T(8,128)(2,1)}), bf16[32,16,768]{2,1,0:T(8,128)(2,1)S(1)}, u32[]{:S(2)}, u32[]{:S(2)}) async-start(bf16[32,16,768]{2,1,0:T(8,128)(2,1)} %shard_map.69._), calls=%async_computation.2 | async-start | bytes 1572864 | tf_op jit(solution)/shard_map/all_to_all | solution.py:188
  50.9 19.8 %collective-permute-start.3 = (bf16[32,768]{1,0:T(8,128)(2,1)S(1)}, bf16[32,768]{1,0:T(8,128)(2,1)S(1)}, u32[]{:S(2)}, u32[]{:S(2)}) collective-permute-start(bf16[32,768]{1,0:T(8,128)(2,1)S(1)} %get-tuple-element.21), channel_id=1, source_target_pairs={{0,256},{32,288},{64,320},{96,352},{128,384},{160,416},{192,448},{... | collective-permute-start | bytes 147464 | tf_op jit(solution)/shard_map/ppermute | solution.py:141
  61.0 11.0 %collective-permute-start.4 = (bf16[32,768]{1,0:T(8,128)(2,1)S(1)}, bf16[32,768]{1,0:T(8,128)(2,1)S(1)}, u32[]{:S(2)}, u32[]{:S(2)}) collective-permute-start(bf16[32,768]{1,0:T(8,128)(2,1)S(1)} %get-tuple-element.22), channel_id=1, source_target_pairs={{0,128},{32,160},{64,192},{96,224},{128,256},{160,288},{192,320},{... | collective-permute-start | bytes 147464 | tf_op jit(solution)/shard_map/ppermute | solution.py:141
  65.3 11.3 %collective-permute-start.5 = (bf16[32,768]{1,0:T(8,128)(2,1)S(1)}, bf16[32,768]{1,0:T(8,128)(2,1)S(1)}, u32[]{:S(2)}, u32[]{:S(2)}) collective-permute-start(bf16[32,768]{1,0:T(8,128)(2,1)S(1)} %get-tuple-element.23), channel_id=1, source_target_pairs={{0,384},{32,416},{64,448},{96,480},{128,0},{160,32},{192,64},{224,... | collective-permute-start | bytes 147464 | tf_op jit(solution)/shard_map/ppermute | solution.py:141

commit v5 on v4

v5 whole, which is shorter than its diff:
```python
import jax
import jax.numpy as jnp
from jax import lax
from jax.experimental import pallas as pl
from jax.experimental.pallas import tpu as pltpu
from jax.sharding import PartitionSpec as P

BLOCK = 128
LOWEST = -3.4028234e38
VMEM_LIMIT = 24 * 1024 * 1024
VMEM_MOST = 62_000_000
LONG = 60_000_000_000
PART = 512
F32 = jnp.float32
BF16 = jnp.bfloat16


def call(kernel, out_shape, args, flops=0, scratch=(), any_inputs=0, any_outputs=0, vmem=VMEM_LIMIT):
    specs = [pl.BlockSpec(memory_space=pltpu.HBM)] * any_inputs
    specs += [pl.BlockSpec(memory_space=pltpu.VMEM)] * (len(args) - any_inputs)
    results = [pl.BlockSpec(memory_space=pltpu.VMEM)] * (len(out_shape) - any_outputs)
    results += [pl.BlockSpec(memory_space=pltpu.HBM)] * any_outputs
    return pl.pallas_call(
        kernel,
        out_shape=out_shape,
        in_specs=specs,
        out_specs=tuple(results),
        scratch_shapes=list(scratch),
        compiler_params=pltpu.CompilerParams(vmem_limit_bytes=vmem),
        cost_estimate=pl.CostEstimate(flops=flops, bytes_accessed=2_000_000, transcendentals=0),
    )(*args)


def part_scores(part, short_ref, positive_ref, queries_ref, embeddings_ref):
    columns = slice(part * PART, (part + 1) * PART)
    scores = lax.dot_general(
        embeddings_ref[...], queries_ref[columns, :], (((1,), (1,)), ((), ())), preferred_element_type=F32
    )
    labels = scores.shape[0]
    label_blocks = labels // BLOCK
    first = lax.axis_index("label") * label_blocks
    listed = short_ref[...]
    masked = []
    for b in range(label_blocks):
        hit = jnp.max(jnp.where(listed == first + b, 1.0, 0.0).astype(F32), axis=1, keepdims=True)
        hit = [
            jnp.broadcast_to(hit[q : q + 1], (1, BLOCK))
            for q in range(columns.start // BLOCK, columns.stop // BLOCK)
        ]
        block = scores[b * BLOCK : (b + 1) * BLOCK]
        masked.append(jnp.where(jnp.concatenate(hit, axis=1) > 0.5, block, -jnp.inf))
    place = positive_ref[:, columns] - first * BLOCK
    is_positive = lax.broadcasted_iota(jnp.int32, scores.shape, 0) == place
    return scores, jnp.concatenate(masked, axis=0), is_positive


def stats_kernel(
    short_hbm, positive_hbm, queries_hbm, embeddings_hbm, out_ref,
    short_ref, positive_ref, queries_ref, embeddings_ref, sems,
):
    parts = [slice(q, q + PART) for q in range(0, queries_ref.shape[0], PART)]
    pairs = [(embeddings_hbm, embeddings_ref), (short_hbm, short_ref), (positive_hbm, positive_ref)]
    pairs += [(queries_hbm.at[rows, :], queries_ref.at[rows, :]) for rows in parts]
    copies = [pltpu.make_async_copy(*pair, sems.at[i]) for i, pair in enumerate(pairs)]
    for copy in copies:
        copy.start()
    for copy in copies[:3]:
        copy.wait()
    for i, columns in enumerate(parts):
        copies[3 + i].wait()
        scores, masked, is_positive = part_scores(
            i, short_ref, positive_ref, queries_ref, embeddings_ref
        )
        top = jnp.maximum(jnp.max(masked, axis=0, keepdims=True), LOWEST)
        total = jnp.sum(jnp.exp(masked - top), axis=0, keepdims=True)
        positive = jnp.sum(jnp.where(is_positive, scores, 0.0), axis=0, keepdims=True)
        rows = jnp.concatenate([top + jnp.log(total), positive], axis=0)
        out_ref[:, :, columns] = jnp.broadcast_to(rows[None], (out_ref.shape[0], 2, PART))


def gradient_kernel(
    short_ref, positive_ref, stats_ref, queries_ref, embeddings_ref,
    loss_ref, keep_ref, right_ref, left_ref, far_ref, query_ref, part_ref,
):
    logs = stats_ref[:, 0, :]
    top = jnp.max(logs, axis=0, keepdims=True)
    log_total = top + jnp.log(jnp.sum(jnp.exp(logs - top), axis=0, keepdims=True))
    positive = jnp.sum(stats_ref[:, 1, :], axis=0, keepdims=True)
    loss_ref[...] = log_total - positive
    _, masked, is_positive = part_scores(0, short_ref, positive_ref, queries_ref, embeddings_ref)
    weights = jnp.exp(masked - log_total)
    gradient = jnp.where(is_positive, weights - 1.0, weights)
    part_ref[...] = gradient
    gradient = gradient.astype(BF16)
    plane = lax.axis_index("dp")
    deep = BLOCK // lax.axis_size("dp")
    blocks = part_ref.shape[0] // BLOCK
    odd = 2 * lax.rem(plane, 2)
    results = ((keep_ref, 0), (right_ref, 1 + odd), (left_ref, 3 - odd), (far_ref, 2))
    pieces = []
    for ref, shift in results:
        kind = lax.rem(plane + shift, 4)
        for m in range(ref.shape[0]):
            start = pl.multiple_of((4 * m + kind) * deep, deep)
            pieces += [part_ref[pl.ds(b * BLOCK + start, deep), :] for b in range(blocks)]
    sorted_rows = jnp.concatenate(pieces, axis=0).astype(BF16)
    terms = jnp.dot(sorted_rows, queries_ref[...], preferred_element_type=F32)
    size = terms.shape[0] // 4
    for i, (ref, _) in enumerate(results):
        ref[...] = terms[i * size : (i + 1) * size].reshape(ref.shape).astype(ref.dtype)
    query_ref[...] = lax.dot_general(
        gradient, embeddings_ref[...], (((0,), (0,)), ((), ())), preferred_element_type=F32
    ).astype(BF16)


def spread_kernel(parts_ref, spread_ref):
    total = parts_ref[0].astype(F32)
    for i in range(1, parts_ref.shape[0]):
        total = total + parts_ref[i].astype(F32)
    spread_ref[...] = jnp.broadcast_to(total.astype(BF16)[None], spread_ref.shape)


def middle_kernel(_, a_ref, b_ref, c_ref, d_ref, keep_ref, right_ref, left_ref, far_ref):
    mine = lax.axis_index("dp") // 4
    for ref, flip in ((far_ref, 2), (keep_ref, 0), (right_ref, 1), (left_ref, 3)):
        m = mine ^ flip
        total = a_ref[m].astype(F32) + b_ref[m].astype(F32) + c_ref[m].astype(F32) + d_ref[m].astype(F32)
        ref[...] = total.astype(ref.dtype)


def copy_kernel(from_ref, token_ref, to_hbm, sem):
    copy = pltpu.make_async_copy(from_ref, to_hbm, sem)
    copy.start()
    token_ref[...] = jnp.zeros_like(token_ref)
    copy.wait()


def last_kernel(_, a_ref, b_ref, c_ref, d_ref, label_ref):
    total = a_ref[...].astype(F32) + b_ref[...].astype(F32) + c_ref[...].astype(F32) + d_ref[...]
    deep, blocks = label_ref.shape[:2]
    for b in range(blocks):
        label_ref[:, b, :] = total[b * deep : (b + 1) * deep]


def moved_by(x, shift):
    planes = lax.axis_size("dp")
    return lax.ppermute(x, "dp", [(i, (i + shift) % planes) for i in range(planes)])


def exchanged(x, flip):
    planes = lax.axis_size("dp")
    return lax.ppermute(x, "dp", [(i, i ^ flip) for i in range(planes)])


def beside(x):
    planes = lax.axis_size("dp")
    return lax.ppermute(x, "dp", [(i, (i - 1 + i % 2 * 2) % planes) for i in range(planes)])


def moved_by_two(x):
    planes = lax.axis_size("dp")
    return lax.ppermute(x, "dp", [(i, (i + 2 - i % 2 * 4) % planes) for i in range(planes)])


def body(queries, embeddings, shortlist, positive):
    rows, width = queries.shape
    labels = embeddings.shape[0]
    groups, planes = lax.axis_size("label"), lax.axis_size("dp")
    shape = jax.ShapeDtypeStruct
    positive = positive.reshape(1, rows)
    madds = rows * labels * width
    chunk = labels // planes

    given = (shortlist, positive, queries, embeddings)
    (stats,) = call(
        stats_kernel,
        (shape((groups, 2, rows), F32),),
        given,
        flops=2 * madds,
        scratch=[pltpu.VMEM(x.shape, x.dtype) for x in given] + [pltpu.SemaphoreType.DMA((3 + rows // PART,))],
        any_inputs=4,
        vmem=VMEM_MOST,
    )
    stats = lax.all_to_all(stats, "label", 0, 0)
    losses, keep, right, left, far, query_part = call(
        gradient_kernel,
        (shape((1, rows), F32), shape((planes // 4, chunk, width), F32))
        + (shape((planes // 4, chunk, width), BF16),) * 3
        + (shape((rows, width), BF16),),
        (shortlist, positive, stats, queries, embeddings),
        flops=6 * madds,
        scratch=[
            pltpu.VMEM((labels, rows), F32),
        ],
    )
    far, right, left = moved_by_two(far), exchanged(right, 1), beside(left)
    query_parts = lax.all_to_all(
        query_part.reshape(groups, rows // groups, width), "label", 0, 0
    )
    (spread,) = call(
        spread_kernel, (shape(query_parts.shape, BF16),), (query_parts,), flops=LONG
    )
    query_grad = lax.all_to_all(spread, "label", 0, 0).reshape(rows, width)
    keep, right, left, far = call(
        middle_kernel,
        (shape((chunk, width), F32),) + (shape((chunk, width), BF16),) * 3,
        (spread, far, right, left, keep),
        any_inputs=1,
        flops=LONG,
    )
    far, right, left = exchanged(far, 8), exchanged(right, 4), exchanged(left, 12)
    token, query_grad = call(
        copy_kernel,
        (shape((8, BLOCK), F32), shape((rows, width), BF16)),
        (query_grad,),
        scratch=[pltpu.SemaphoreType.DMA],
        any_outputs=1,
        flops=LONG,
    )
    (label_grad,) = call(
        last_kernel,
        (shape((BLOCK // planes, labels // BLOCK, width), F32),),
        (token, far, right, left, keep),
    )
    return losses.reshape(rows), query_grad, label_grad


def solution(mesh):
    in_specs = (P("dp", None), P("label", None), P("dp", None), P("dp"))
    out_specs = (P("dp"), P("dp", None), P("dp", "label", None))
    return jax.shard_map(body, mesh=mesh, in_specs=in_specs, out_specs=out_specs, check_vma=False)
```

time: 78.7 us -> 76.9 us (0.977)
  the two profiles are of different devices: /device:TPU:12 before, /device:TPU:1 now
where the time goes in v5:
time: 76.9 us; the launch traced here: 75.8 us
  starting transfers between devices  42.4 us (55%)
  blocking collectives  18.1 us (24%)
  Pallas kernels  8.38 us (11%)
  waiting for transfers between devices  6.11 us (8%)
  between operations  0.8 us (1%)
    ppermute x4, starting transfers between devices, exchanged(): return lax.ppermute(x, 'dp', [(i, i ^ flip) for i in range(planes)])  25.5 us
    all_to_all x1, blocking collectives, body(): stats = lax.all_to_all(stats, 'label', 0, 0)  18.1 us
    pallas_call x6, Pallas kernels, call(): pl.pallas_call(kernel, out_shape=out_shape, in_specs=specs, out_specs=tup...  8.38 us
    all_to_all x1, starting transfers between devices, body(): query_grad = lax.all_to_all(spread, 'label', 0, 0).reshape(rows, width)  7.99 us
    ppermute x4, waiting for transfers between devices, exchanged(): return lax.ppermute(x, 'dp', [(i, i ^ flip) for i in range(planes)])  6.03 us
    all_to_all x1, starting transfers between devices, body(): lax.all_to_all(query_part.reshape(groups, rows // groups, width), 'label'...  3.96 us
    ppermute x1, starting transfers between devices, moved_by_two(): lax.ppermute(x, 'dp', [(i, (i + 2 - i % 2 * 4) % planes) for i in range(p...  3 us
    ppermute x1, starting transfers between devices, beside(): lax.ppermute(x, 'dp', [(i, (i - 1 + i % 2 * 2) % planes) for i in range(p...  1.92 us
  transfers between devices with their start and end apart: 8, of which 3 were waited for; matrix products, arithmetic and copies ran while one was open for 0% of the time, Pallas kernels for 3%

profile of v5, /device:TPU:1, one launch (start us, length us, event | category | flops | bytes accessed | tf_op | source)
XLA Modules:
  0.0 75.8 jit_solution(16577666930745348127)
XLA Ops:
  0.6 0.0 copy-start
  0.6 0.0 copy-start.1
  0.6 3.1 %shard_map.67 = f32[32,2,512]{2,1,0:T(2,128)} custom-call(s32[4,48]{1,0:T(4,128)} %short_ref.1, s32[1,512]{1,0:T(1,128)} %bitcast.5, bf16[512,768]{1,0:T(8,128)(2,1)} %queries_ref.1, bf16[512,768]{1,0:T(8,128)(2,1)} %embeddings_ref.1), custom_call_target="tpu_custom_call" | custom-call | flops 402653184 | bytes 2000000 | tf_op jit(solution)/shard_map/pallas_call | solution.py:23
  3.7 0.0 copy-start.2
  3.7 0.0 copy-start.3
  3.7 18.1 %all_to_all.15.stats_ref = f32[32,2,512]{2,1,0:T(2,128)S(1)} all-to-all(f32[32,2,512]{2,1,0:T(2,128)} %shard_map.67), channel_id=1, replica_groups=mesh['dp'=16,'label'=32] {'label'}, dimensions={0} | all-to-all | bytes 262144 | tf_op jit(solution)/shard_map/all_to_all | solution.py:184
  21.9 0.0 copy-done
  21.9 0.0 copy-done.1
  21.9 0.0 copy-done.2
  21.9 0.0 copy-done.3
  21.9 2.6 %shard_map.68 = (f32[1,512]{1,0:T(1,128)}, f32[4,32,768]{2,1,0:T(8,128)S(1)}, bf16[4,32,768]{2,1,0:T(8,128)(2,1)S(1)}, bf16[4,32,768]{2,1,0:T(8,128)(2,1)S(1)}, ...) custom-call(s32[4,48]{1,0:T(4,128)S(1)} %copy-done.2, s32[1,512]{1,0:T(1,128)S(1)} %bitcast.6, ...), custom_call_target="tpu_custom_call" | custom-call | flops 1207959552 | bytes 2000000 | tf_op jit(solution)/shard_map/pallas_call | solution.py:23
  24.5 4.0 %all-to-all-start.1 = ((bf16[32,16,768]{2,1,0:T(8,128)(2,1)}), bf16[32,16,768]{2,1,0:T(8,128)(2,1)S(1)}, u32[]{:S(2)}, u32[]{:S(2)}) async-start(bf16[32,16,768]{2,1,0:T(8,128)(2,1)} %bitcast.2), calls=%async_computation.1 | async-start | bytes 1572864 | tf_op jit(solution)/shard_map/all_to_all | solution.py:197
  28.5 3.0 %collective-permute-start = (bf16[4,32,768]{2,1,0:T(8,128)(2,1)S(1)}, bf16[4,32,768]{2,1,0:T(8,128)(2,1)S(1)}, u32[]{:S(2)}, u32[]{:S(2)}) collective-permute-start(bf16[4,32,768]{2,1,0:T(8,128)(2,1)S(1)} %get-tuple-element.19), channel_id=1, source_target_pairs={{0,64},{32,480},{64,128},{96,32},{128,192},{160,96},{192,256},{224... | collective-permute-start | bytes 589832 | tf_op jit(solution)/shard_map/ppermute | solution.py:162
  31.5 9.3 %collective-permute-start.1 = (bf16[4,32,768]{2,1,0:T(8,128)(2,1)S(1)}, bf16[4,32,768]{2,1,0:T(8,128)(2,1)S(1)}, u32[]{:S(2)}, u32[]{:S(2)}) collective-permute-start(bf16[4,32,768]{2,1,0:T(8,128)(2,1)S(1)} %get-tuple-element.20), channel_id=1, source_target_pairs={{0,32},{32,0},{64,96},{96,64},{128,160},{160,128},{192,224},{224,1... | collective-permute-start | bytes 589832 | tf_op jit(solution)/shard_map/ppermute | solution.py:152
  40.8 1.9 %collective-permute-start.2 = (bf16[4,32,768]{2,1,0:T(8,128)(2,1)S(1)}, bf16[4,32,768]{2,1,0:T(8,128)(2,1)S(1)}, u32[]{:S(2)}, u32[]{:S(2)}) collective-permute-start(bf16[4,32,768]{2,1,0:T(8,128)(2,1)S(1)} %get-tuple-element.21), channel_id=1, source_target_pairs={{0,480},{32,64},{64,32},{96,128},{128,96},{160,192},{192,160},{224... | collective-permute-start | bytes 589832 | tf_op jit(solution)/shard_map/ppermute | solution.py:157
  42.8 0.1 all-to-all-done.1.parts_ref
  42.8 1.0 %shard_map.69._ = bf16[32,16,768]{2,1,0:T(8,128)(2,1)} custom-call(bf16[32,16,768]{2,1,0:T(8,128)(2,1)S(1)} %all-to-all-done.1.parts_ref), custom_call_target="tpu_custom_call" | custom-call | flops 60000002048 | bytes 2000000 | tf_op jit(solution)/shard_map/pallas_call | solution.py:23
  43.8 8.0 %all-to-all-start.2 = ((bf16[32,16,768]{2,1,0:T(8,128)(2,1)}), bf16[32,16,768]{2,1,0:T(8,128)(2,1)S(1)}, u32[]{:S(2)}, u32[]{:S(2)}) async-start(bf16[32,16,768]{2,1,0:T(8,128)(2,1)} %shard_map.69._), calls=%async_computation.2 | async-start | bytes 1572864 | tf_op jit(solution)/shard_map/all_to_all | solution.py:203
  51.8 0.0 collective-permute-done.a_ref
  51.9 0.0 collective-permute-done.1.b_ref
  51.9 0.0 collective-permute-done.2.c_ref
  51.9 0.1 shard_map.71
  52.0 9.7 %collective-permute-start.3 = (bf16[32,768]{1,0:T(8,128)(2,1)S(1)}, bf16[32,768]{1,0:T(8,128)(2,1)S(1)}, u32[]{:S(2)}, u32[]{:S(2)}) collective-permute-start(bf16[32,768]{1,0:T(8,128)(2,1)S(1)} %get-tuple-element.23), channel_id=1, source_target_pairs={{0,256},{32,288},{64,320},{96,352},{128,384},{160,416},{192,448},{... | collective-permute-start | bytes 147464 | tf_op jit(solution)/shard_map/ppermute | solution.py:152
  61.7 4.0 %collective-permute-start.4 = (bf16[32,768]{1,0:T(8,128)(2,1)S(1)}, bf16[32,768]{1,0:T(8,128)(2,1)S(1)}, u32[]{:S(2)}, u32[]{:S(2)}) collective-permute-start(bf16[32,768]{1,0:T(8,128)(2,1)S(1)} %get-tuple-element.24), channel_id=1, source_target_pairs={{0,128},{32,160},{64,192},{96,224},{128,0},{160,32},{192,64},{224,... | collective-permute-start | bytes 147464 | tf_op jit(solution)/shard_map/ppermute | solution.py:152
  65.7 2.5 %collective-permute-start.5 = (bf16[32,768]{1,0:T(8,128)(2,1)S(1)}, bf16[32,768]{1,0:T(8,128)(2,1)S(1)}, u32[]{:S(2)}, u32[]{:S(2)}) collective-permute-start(bf16[32,768]{1,0:T(8,128)(2,1)S(1)} %get-tuple-element.25), channel_id=1, source_target_pairs={{0,384},{32,416},{64,448},{96,480},{128,256},{160,288},{192,320},{... | collective-permute-start | bytes 147464 | tf_op jit(solution)/shard_map/ppermute | solution.py:152
  68.2 0.0 all-to-all-done.2
  68.2 0.9 %shard_map.70 = (f32[8,128]{1,0:T(8,128)S(1)}, bf16[512,768]{1,0:T(8,128)(2,1)}) custom-call(bf16[512,768]{1,0:T(8,128)(2,1)S(1)} %bitcast.4), custom_call_target="tpu_custom_call" | custom-call | flops 60000002048 | bytes 2000000 | tf_op jit(solution)/shard_map/pallas_call | solution.py:23
  69.1 0.0 collective-permute-done.3.a_ref
  69.1 1.4 %collective-permute-done.4.b_ref = bf16[32,768]{1,0:T(8,128)(2,1)S(1)} collective-permute-done((bf16[32,768]{1,0:T(8,128)(2,1)S(1)}, bf16[32,768]{1,0:T(8,128)(2,1)S(1)}, u32[]{:S(2)}, u32[]{:S(2)}) %collective-permute-start.4) | collective-permute-done | bytes 49184 | tf_op jit(solution)/shard_map/ppermute | solution.py:152
  70.6 4.6 %collective-permute-done.5.c_ref = bf16[32,768]{1,0:T(8,128)(2,1)S(1)} collective-permute-done((bf16[32,768]{1,0:T(8,128)(2,1)S(1)}, bf16[32,768]{1,0:T(8,128)(2,1)S(1)}, u32[]{:S(2)}, u32[]{:S(2)}) %collective-permute-start.5) | collective-permute-done | bytes 49184 | tf_op jit(solution)/shard_map/ppermute | solution.py:152
  75.1 0.7 shard_map.72
Async XLA Ops:
  0.6 21.2 %copy-start = (bf16[512,768]{1,0:T(8,128)(2,1)S(1)}, bf16[512,768]{1,0:T(8,128)(2,1)}, u32[]{:S(2)}) copy-start(bf16[512,768]{1,0:T(8,128)(2,1)} %queries_ref.1) | copy-start | bytes 2359300
  0.6 21.2 %copy-start.1 = (bf16[512,768]{1,0:T(8,128)(2,1)S(1)}, bf16[512,768]{1,0:T(8,128)(2,1)}, u32[]{:S(2)}) copy-start(bf16[512,768]{1,0:T(8,128)(2,1)} %embeddings_ref.1) | copy-start | bytes 2359300
  3.7 18.2 %copy-start.2 = (s32[4,48]{1,0:T(4,128)S(1)}, s32[4,48]{1,0:T(4,128)}, u32[]{:S(2)}) copy-start(s32[4,48]{1,0:T(4,128)} %short_ref.1) | copy-start | bytes 2308
  3.7 18.2 %copy-start.3 = (s32[512]{0:T(512)S(1)}, s32[512]{0:T(512)}, u32[]{:S(2)}) copy-start(s32[512]{0:T(512)} %param.7) | copy-start | bytes 6148
  24.5 18.3 %all-to-all-start.1 = ((bf16[32,16,768]{2,1,0:T(8,128)(2,1)}), bf16[32,16,768]{2,1,0:T(8,128)(2,1)S(1)}, u32[]{:S(2)}, u32[]{:S(2)}) async-start(bf16[32,16,768]{2,1,0:T(8,128)(2,1)} %bitcast.2), calls=%async_computation.1 | async-start | bytes 1572864 | tf_op jit(solution)/shard_map/all_to_all | solution.py:197
  28.5 23.3 %collective-permute-start = (bf16[4,32,768]{2,1,0:T(8,128)(2,1)S(1)}, bf16[4,32,768]{2,1,0:T(8,128)(2,1)S(1)}, u32[]{:S(2)}, u32[]{:S(2)}) collective-permute-start(bf16[4,32,768]{2,1,0:T(8,128)(2,1)S(1)} %get-tuple-element.19), channel_id=1, source_target_pairs={{0,64},{32,480},{64,128},{96,32},{128,192},{160,96},{192,256},{224... | collective-permute-start | bytes 589832 | tf_op jit(solution)/shard_map/ppermute | solution.py:162
  31.5 20.3 %collective-permute-start.1 = (bf16[4,32,768]{2,1,0:T(8,128)(2,1)S(1)}, bf16[4,32,768]{2,1,0:T(8,128)(2,1)S(1)}, u32[]{:S(2)}, u32[]{:S(2)}) collective-permute-start(bf16[4,32,768]{2,1,0:T(8,128)(2,1)S(1)} %get-tuple-element.20), channel_id=1, source_target_pairs={{0,32},{32,0},{64,96},{96,64},{128,160},{160,128},{192,224},{224,1... | collective-permute-start | bytes 589832 | tf_op jit(solution)/shard_map/ppermute | solution.py:152
  40.8 11.0 %collective-permute-start.2 = (bf16[4,32,768]{2,1,0:T(8,128)(2,1)S(1)}, bf16[4,32,768]{2,1,0:T(8,128)(2,1)S(1)}, u32[]{:S(2)}, u32[]{:S(2)}) collective-permute-start(bf16[4,32,768]{2,1,0:T(8,128)(2,1)S(1)} %get-tuple-element.21), channel_id=1, source_target_pairs={{0,480},{32,64},{64,32},{96,128},{128,96},{160,192},{192,160},{224... | collective-permute-start | bytes 589832 | tf_op jit(solution)/shard_map/ppermute | solution.py:157
  43.8 24.4 %all-to-all-start.2 = ((bf16[32,16,768]{2,1,0:T(8,128)(2,1)}), bf16[32,16,768]{2,1,0:T(8,128)(2,1)S(1)}, u32[]{:S(2)}, u32[]{:S(2)}) async-start(bf16[32,16,768]{2,1,0:T(8,128)(2,1)} %shard_map.69._), calls=%async_computation.2 | async-start | bytes 1572864 | tf_op jit(solution)/shard_map/all_to_all | solution.py:203
  52.0 17.1 %collective-permute-start.3 = (bf16[32,768]{1,0:T(8,128)(2,1)S(1)}, bf16[32,768]{1,0:T(8,128)(2,1)S(1)}, u32[]{:S(2)}, u32[]{:S(2)}) collective-permute-start(bf16[32,768]{1,0:T(8,128)(2,1)S(1)} %get-tuple-element.23), channel_id=1, source_target_pairs={{0,256},{32,288},{64,320},{96,352},{128,384},{160,416},{192,448},{... | collective-permute-start | bytes 147464 | tf_op jit(solution)/shard_map/ppermute | solution.py:152
  61.7 8.9 %collective-permute-start.4 = (bf16[32,768]{1,0:T(8,128)(2,1)S(1)}, bf16[32,768]{1,0:T(8,128)(2,1)S(1)}, u32[]{:S(2)}, u32[]{:S(2)}) collective-permute-start(bf16[32,768]{1,0:T(8,128)(2,1)S(1)} %get-tuple-element.24), channel_id=1, source_target_pairs={{0,128},{32,160},{64,192},{96,224},{128,0},{160,32},{192,64},{224,... | collective-permute-start | bytes 147464 | tf_op jit(solution)/shard_map/ppermute | solution.py:152
  65.7 9.4 %collective-permute-start.5 = (bf16[32,768]{1,0:T(8,128)(2,1)S(1)}, bf16[32,768]{1,0:T(8,128)(2,1)S(1)}, u32[]{:S(2)}, u32[]{:S(2)}) collective-permute-start(bf16[32,768]{1,0:T(8,128)(2,1)S(1)} %get-tuple-element.25), channel_id=1, source_target_pairs={{0,384},{32,416},{64,448},{96,480},{128,256},{160,288},{192,320},{... | collective-permute-start | bytes 147464 | tf_op jit(solution)/shard_map/ppermute | solution.py:152

commit v6 on v5

--- a/solution.py
+++ b/solution.py
@@ -10,7 +10,7 @@
 VMEM_LIMIT = 24 * 1024 * 1024
 VMEM_MOST = 62_000_000
 LONG = 60_000_000_000
-PART = 512
+PIECE = 512
 F32 = jnp.float32
 BF16 = jnp.bfloat16
 
@@ -31,51 +31,60 @@
     )(*args)
 
 
-def part_scores(part, short_ref, positive_ref, queries_ref, embeddings_ref):
-    columns = slice(part * PART, (part + 1) * PART)
+def local_scores(short_ref, positive_ref, queries_ref, embeddings_ref):
     scores = lax.dot_general(
-        embeddings_ref[...], queries_ref[columns, :], (((1,), (1,)), ((), ())), preferred_element_type=F32
-    )
-    labels = scores.shape[0]
+        embeddings_ref[...], queries_ref[...], (((1,), (1,)), ((), ())), preferred_element_type=F32
+    )
+    labels, rows = scores.shape
     label_blocks = labels // BLOCK
     first = lax.axis_index("label") * label_blocks
     listed = short_ref[...]
     masked = []
     for b in range(label_blocks):
         hit = jnp.max(jnp.where(listed == first + b, 1.0, 0.0).astype(F32), axis=1, keepdims=True)
-        hit = [
-            jnp.broadcast_to(hit[q : q + 1], (1, BLOCK))
-            for q in range(columns.start // BLOCK, columns.stop // BLOCK)
-        ]
+        hit = [jnp.broadcast_to(hit[q : q + 1], (1, BLOCK)) for q in range(rows // BLOCK)]
         block = scores[b * BLOCK : (b + 1) * BLOCK]
         masked.append(jnp.where(jnp.concatenate(hit, axis=1) > 0.5, block, -jnp.inf))
-    place = positive_ref[:, columns] - first * BLOCK
+    place = positive_ref[...] - first * BLOCK
     is_positive = lax.broadcasted_iota(jnp.int32, scores.shape, 0) == place
     return scores, jnp.concatenate(masked, axis=0), is_positive
+
+
+def copies_of(pairs, sems):
+    cut = []
+    for source, target in pairs:
+        rows = source.shape[0]
+        if rows <= PIECE:
+            cut.append((source, target))
+        else:
+            at = [pl.ds(r, PIECE) for r in range(0, rows, PIECE)]
+            cut += [(source.at[rows, :], target.at[rows, :]) for rows in at]
+    return [pltpu.make_async_copy(*pair, sems.at[i]) for i, pair in enumerate(cut)]
 
 
 def stats_kernel(
     short_hbm, positive_hbm, queries_hbm, embeddings_hbm, out_ref,
     short_ref, positive_ref, queries_ref, embeddings_ref, sems,
 ):
-    parts = [slice(q, q + PART) for q in range(0, queries_ref.shape[0], PART)]
-    pairs = [(embeddings_hbm, embeddings_ref), (short_hbm, short_ref), (positive_hbm, positive_ref)]
-    pairs += [(queries_hbm.at[rows, :], queries_ref.at[rows, :]) for rows in parts]
-    copies = [pltpu.make_async_copy(*pair, sems.at[i]) for i, pair in enumerate(pairs)]
+    copies = copies_of(
+        [
+            (queries_hbm, queries_ref),
+            (embeddings_hbm, embeddings_ref),
+            (short_hbm, short_ref),
+            (positive_hbm, positive_ref),
+        ],
+        sems,
+    )
     for copy in copies:
         copy.start()
-    for copy in copies[:3]:
+    for copy in copies:
         copy.wait()
-    for i, columns in enumerate(parts):
-        copies[3 + i].wait()
-        scores, masked, is_positive = part_scores(
-            i, short_ref, positive_ref, queries_ref, embeddings_ref
-        )
-        top = jnp.maximum(jnp.max(masked, axis=0, keepdims=True), LOWEST)
-        total = jnp.sum(jnp.exp(masked - top), axis=0, keepdims=True)
-        positive = jnp.sum(jnp.where(is_positive, scores, 0.0), axis=0, keepdims=True)
-        rows = jnp.concatenate([top + jnp.log(total), positive], axis=0)
-        out_ref[:, :, columns] = jnp.broadcast_to(rows[None], (out_ref.shape[0], 2, PART))
+    scores, masked, is_positive = local_scores(short_ref, positive_ref, queries_ref, embeddings_ref)
+    top = jnp.maximum(jnp.max(masked, axis=0, keepdims=True), LOWEST)
+    total = jnp.sum(jnp.exp(masked - top), axis=0, keepdims=True)
+    positive = jnp.sum(jnp.where(is_positive, scores, 0.0), axis=0, keepdims=True)
+    rows = jnp.concatenate([top + jnp.log(total), positive], axis=0)
+    out_ref[...] = jnp.broadcast_to(rows[None], out_ref.shape)
 
 
 def gradient_kernel(
@@ -87,7 +96,7 @@
     log_total = top + jnp.log(jnp.sum(jnp.exp(logs - top), axis=0, keepdims=True))
     positive = jnp.sum(stats_ref[:, 1, :], axis=0, keepdims=True)
     loss_ref[...] = log_total - positive
-    _, masked, is_positive = part_scores(0, short_ref, positive_ref, queries_ref, embeddings_ref)
+    _, masked, is_positive = local_scores(short_ref, positive_ref, queries_ref, embeddings_ref)
     weights = jnp.exp(masked - log_total)
     gradient = jnp.where(is_positive, weights - 1.0, weights)
     part_ref[...] = gradient
@@ -120,12 +129,19 @@
     spread_ref[...] = jnp.broadcast_to(total.astype(BF16)[None], spread_ref.shape)
 
 
-def middle_kernel(_, a_ref, b_ref, c_ref, d_ref, keep_ref, right_ref, left_ref, far_ref):
-    mine = lax.axis_index("dp") // 4
-    for ref, flip in ((far_ref, 2), (keep_ref, 0), (right_ref, 1), (left_ref, 3)):
-        m = mine ^ flip
-        total = a_ref[m].astype(F32) + b_ref[m].astype(F32) + c_ref[m].astype(F32) + d_ref[m].astype(F32)
-        ref[...] = total.astype(ref.dtype)
+def middle_kernel(_, a_ref, b_ref, c_ref, d_ref, send_ref, keep_ref):
+    plane = lax.axis_index("dp")
+    mine, first = plane // 4, 1 + 2 * lax.rem(plane, 2)
+    for ref, masks in ((send_ref, (first, 2)), (keep_ref, (0, 4 - first))):
+        for i, mask in enumerate(masks):
+            m = mine ^ mask
+            total = a_ref[m].astype(F32) + b_ref[m].astype(F32) + c_ref[m].astype(F32) + d_ref[m].astype(F32)
+            ref[i] = total.astype(ref.dtype)
+
+
+def join_kernel(received_ref, keep_ref, send_ref, own_ref):
+    own_ref[...] = received_ref[0].astype(F32) + keep_ref[0]
+    send_ref[...] = (received_ref[1].astype(F32) + keep_ref[1]).astype(BF16)
 
 
 def copy_kernel(from_ref, token_ref, to_hbm, sem):
@@ -135,21 +151,16 @@
     copy.wait()
 
 
-def last_kernel(_, a_ref, b_ref, c_ref, d_ref, label_ref):
-    total = a_ref[...].astype(F32) + b_ref[...].astype(F32) + c_ref[...].astype(F32) + d_ref[...]
+def last_kernel(_, received_ref, own_ref, label_ref):
+    total = received_ref[...].astype(F32) + own_ref[...]
     deep, blocks = label_ref.shape[:2]
     for b in range(blocks):
         label_ref[:, b, :] = total[b * deep : (b + 1) * deep]
 
 
-def moved_by(x, shift):
+def exchanged(x, even, odd):
     planes = lax.axis_size("dp")
-    return lax.ppermute(x, "dp", [(i, (i + shift) % planes) for i in range(planes)])
-
-
-def exchanged(x, flip):
-    planes = lax.axis_size("dp")
-    return lax.ppermute(x, "dp", [(i, i ^ flip) for i in range(planes)])
+    return lax.ppermute(x, "dp", [(i, i ^ (odd if i % 2 else even)) for i in range(planes)])
 
 
 def beside(x):
@@ -177,7 +188,7 @@
         (shape((groups, 2, rows), F32),),
         given,
         flops=2 * madds,
-        scratch=[pltpu.VMEM(x.shape, x.dtype) for x in given] + [pltpu.SemaphoreType.DMA((3 + rows // PART,))],
+        scratch=[pltpu.VMEM(x.shape, x.dtype) for x in given] + [pltpu.SemaphoreType.DMA((2 + (rows + labels) // PIECE,))],
         any_inputs=4,
         vmem=VMEM_MOST,
     )
@@ -193,7 +204,7 @@
             pltpu.VMEM((labels, rows), F32),
         ],
     )
-    far, right, left = moved_by_two(far), exchanged(right, 1), beside(left)
+    far, right, left = moved_by_two(far), exchanged(right, 1, 1), beside(left)
     query_parts = lax.all_to_all(
         query_part.reshape(groups, rows // groups, width), "label", 0, 0
     )
@@ -201,14 +212,19 @@
         spread_kernel, (shape(query_parts.shape, BF16),), (query_parts,), flops=LONG
     )
     query_grad = lax.all_to_all(spread, "label", 0, 0).reshape(rows, width)
-    keep, right, left, far = call(
+    send, keep = call(
         middle_kernel,
-        (shape((chunk, width), F32),) + (shape((chunk, width), BF16),) * 3,
+        (shape((2, chunk, width), BF16), shape((2, chunk, width), F32)),
         (spread, far, right, left, keep),
         any_inputs=1,
         flops=LONG,
     )
-    far, right, left = exchanged(far, 8), exchanged(right, 4), exchanged(left, 12)
+    send, own = call(
+        join_kernel,
+        (shape((chunk, width), BF16), shape((chunk, width), F32)),
+        (exchanged(send, 4, 12), keep),
+    )
+    received = exchanged(send, 12, 4)
     token, query_grad = call(
         copy_kernel,
         (shape((8, BLOCK), F32), shape((rows, width), BF16)),
@@ -220,7 +236,7 @@
     (label_grad,) = call(
         last_kernel,
         (shape((BLOCK // planes, labels // BLOCK, width), F32),),
-        (token, far, right, left, keep),
+        (token, received, own),
     )
     return losses.reshape(rows), query_grad, label_grad
 

time: 76.9 us -> 75.9 us (0.987)
  the two profiles are of different devices: /device:TPU:1 before, /device:TPU:2 now
where the time goes in v6:
time: 75.9 us; the launch traced here: 75.3 us
  starting transfers between devices  39.4 us (52%)
  blocking collectives  16.2 us (21%)
  waiting for transfers between devices  10.7 us (14%)
  Pallas kernels  8.36 us (11%)
  between operations  0.8 us (1%)
    ppermute x3, starting transfers between devices, exchanged(): lax.ppermute(x, 'dp', [(i, i ^ (odd if i % 2 else even)) for i in range(p...  21.7 us
    all_to_all x1, blocking collectives, body(): stats = lax.all_to_all(stats, 'label', 0, 0)  16.2 us
    ppermute x3, waiting for transfers between devices, exchanged(): lax.ppermute(x, 'dp', [(i, i ^ (odd if i % 2 else even)) for i in range(p...  10.6 us
    pallas_call x7, Pallas kernels, call(): pl.pallas_call(kernel, out_shape=out_shape, in_specs=specs, out_specs=tup...  8.36 us
    all_to_all x1, starting transfers between devices, body(): query_grad = lax.all_to_all(spread, 'label', 0, 0).reshape(rows, width)  7.49 us
    all_to_all x1, starting transfers between devices, body(): lax.all_to_all(query_part.reshape(groups, rows // groups, width), 'label'...  4.98 us
    ppermute x1, starting transfers between devices, moved_by_two(): lax.ppermute(x, 'dp', [(i, (i + 2 - i % 2 * 4) % planes) for i in range(p...  3.27 us
    ppermute x1, starting transfers between devices, beside(): lax.ppermute(x, 'dp', [(i, (i - 1 + i % 2 * 2) % planes) for i in range(p...  1.92 us
  transfers between devices with their start and end apart: 7, of which 2 were waited for; matrix products, arithmetic and copies ran while one was open for 0% of the time, Pallas kernels for 3%

profile of v6, /device:TPU:2, one launch (start us, length us, event | category | flops | bytes accessed | tf_op | source)
XLA Modules:
  0.0 75.3 jit_solution(10225827876907957396)
XLA Ops:
  0.6 0.0 copy-start
  0.6 0.0 copy-start.1
  0.6 3.0 %shard_map.67 = f32[32,2,512]{2,1,0:T(2,128)} custom-call(s32[4,48]{1,0:T(4,128)} %short_ref.1, s32[1,512]{1,0:T(1,128)} %bitcast.5, bf16[512,768]{1,0:T(8,128)(2,1)} %queries_ref.1, bf16[512,768]{1,0:T(8,128)(2,1)} %embeddings_ref.1), custom_call_target="tpu_custom_call" | custom-call | flops 402653184 | bytes 2000000 | tf_op jit(solution)/shard_map/pallas_call | solution.py:23
  3.7 0.0 copy-start.2
  3.7 0.0 copy-start.3
  3.7 16.2 %all_to_all.15.stats_ref = f32[32,2,512]{2,1,0:T(2,128)S(1)} all-to-all(f32[32,2,512]{2,1,0:T(2,128)} %shard_map.67), channel_id=1, replica_groups=mesh['dp'=16,'label'=32] {'label'}, dimensions={0} | all-to-all | bytes 262144 | tf_op jit(solution)/shard_map/all_to_all | solution.py:195
  19.9 0.0 copy-done
  19.9 0.0 copy-done.1
  19.9 0.0 copy-done.2
  19.9 0.0 copy-done.3
  19.9 2.6 %shard_map.68 = (f32[1,512]{1,0:T(1,128)}, f32[4,32,768]{2,1,0:T(8,128)S(1)}, bf16[4,32,768]{2,1,0:T(8,128)(2,1)S(1)}, bf16[4,32,768]{2,1,0:T(8,128)(2,1)S(1)}, ...) custom-call(s32[4,48]{1,0:T(4,128)S(1)} %copy-done.2, s32[1,512]{1,0:T(1,128)S(1)} %bitcast.6, ...), custom_call_target="tpu_custom_call" | custom-call | flops 1207959552 | bytes 2000000 | tf_op jit(solution)/shard_map/pallas_call | solution.py:23
  22.5 5.0 %all-to-all-start.1 = ((bf16[32,16,768]{2,1,0:T(8,128)(2,1)}), bf16[32,16,768]{2,1,0:T(8,128)(2,1)S(1)}, u32[]{:S(2)}, u32[]{:S(2)}) async-start(bf16[32,16,768]{2,1,0:T(8,128)(2,1)} %bitcast.2), calls=%async_computation.1 | async-start | bytes 1572864 | tf_op jit(solution)/shard_map/all_to_all | solution.py:208
  27.5 3.3 %collective-permute-start = (bf16[4,32,768]{2,1,0:T(8,128)(2,1)S(1)}, bf16[4,32,768]{2,1,0:T(8,128)(2,1)S(1)}, u32[]{:S(2)}, u32[]{:S(2)}) collective-permute-start(bf16[4,32,768]{2,1,0:T(8,128)(2,1)S(1)} %get-tuple-element.19), channel_id=1, source_target_pairs={{0,64},{32,480},{64,128},{96,32},{128,192},{160,96},{192,256},{224... | collective-permute-start | bytes 589832 | tf_op jit(solution)/shard_map/ppermute | solution.py:173
  30.8 9.6 %collective-permute-start.1 = (bf16[4,32,768]{2,1,0:T(8,128)(2,1)S(1)}, bf16[4,32,768]{2,1,0:T(8,128)(2,1)S(1)}, u32[]{:S(2)}, u32[]{:S(2)}) collective-permute-start(bf16[4,32,768]{2,1,0:T(8,128)(2,1)S(1)} %get-tuple-element.20), channel_id=1, source_target_pairs={{0,32},{32,0},{64,96},{96,64},{128,160},{160,128},{192,224},{224,1... | collective-permute-start | bytes 589832 | tf_op jit(solution)/shard_map/ppermute | solution.py:163
  40.4 1.9 %collective-permute-start.2 = (bf16[4,32,768]{2,1,0:T(8,128)(2,1)S(1)}, bf16[4,32,768]{2,1,0:T(8,128)(2,1)S(1)}, u32[]{:S(2)}, u32[]{:S(2)}) collective-permute-start(bf16[4,32,768]{2,1,0:T(8,128)(2,1)S(1)} %get-tuple-element.21), channel_id=1, source_target_pairs={{0,480},{32,64},{64,32},{96,128},{128,96},{160,192},{192,160},{224... | collective-permute-start | bytes 589832 | tf_op jit(solution)/shard_map/ppermute | solution.py:168
  42.3 0.0 all-to-all-done.1.parts_ref
  42.3 1.0 %shard_map.69._ = bf16[32,16,768]{2,1,0:T(8,128)(2,1)} custom-call(bf16[32,16,768]{2,1,0:T(8,128)(2,1)S(1)} %all-to-all-done.1.parts_ref), custom_call_target="tpu_custom_call" | custom-call | flops 60000002048 | bytes 2000000 | tf_op jit(solution)/shard_map/pallas_call | solution.py:23
  43.3 7.5 %all-to-all-start.2 = ((bf16[32,16,768]{2,1,0:T(8,128)(2,1)}), bf16[32,16,768]{2,1,0:T(8,128)(2,1)S(1)}, u32[]{:S(2)}, u32[]{:S(2)}) async-start(bf16[32,16,768]{2,1,0:T(8,128)(2,1)} %shard_map.69._), calls=%async_computation.2 | async-start | bytes 1572864 | tf_op jit(solution)/shard_map/all_to_all | solution.py:214
  50.8 0.0 collective-permute-done.a_ref
  50.9 0.0 collective-permute-done.1.b_ref
  50.9 0.0 collective-permute-done.2.c_ref
  50.9 0.1 shard_map.71
  51.0 3.3 %collective-permute-start.3 = (bf16[2,32,768]{2,1,0:T(8,128)(2,1)S(1)}, bf16[2,32,768]{2,1,0:T(8,128)(2,1)S(1)}, u32[]{:S(2)}, u32[]{:S(2)}) collective-permute-start(bf16[2,32,768]{2,1,0:T(8,128)(2,1)S(1)} %get-tuple-element.23), channel_id=1, source_target_pairs={{0,128},{32,416},{64,192},{96,480},{128,0},{160,288},{192,64},{224... | collective-permute-start | bytes 294920 | tf_op jit(solution)/shard_map/ppermute | solution.py:163
  54.3 9.5 %collective-permute-done.3.received_ref = bf16[2,32,768]{2,1,0:T(8,128)(2,1)S(1)} collective-permute-done((bf16[2,32,768]{2,1,0:T(8,128)(2,1)S(1)}, bf16[2,32,768]{2,1,0:T(8,128)(2,1)S(1)}, u32[]{:S(2)}, u32[]{:S(2)}) %collective-permute-start.3) | collective-permute-done | bytes 98336 | tf_op jit(solution)/shard_map/ppermute | solution.py:163
  63.9 8.7 %collective-permute-start.4 = (bf16[32,768]{1,0:T(8,128)(2,1)S(1)}, bf16[32,768]{1,0:T(8,128)(2,1)S(1)}, u32[]{:S(2)}, u32[]{:S(2)}) collective-permute-start(bf16[32,768]{1,0:T(8,128)(2,1)S(1)} %get-tuple-element.25), channel_id=1, source_target_pairs={{0,384},{32,160},{64,448},{96,224},{128,256},{160,32},{192,320},{2... | collective-permute-start | bytes 147464 | tf_op jit(solution)/shard_map/ppermute | solution.py:163
  72.6 0.0 all-to-all-done.2
  72.6 0.9 %shard_map.70 = (f32[8,128]{1,0:T(8,128)S(1)}, bf16[512,768]{1,0:T(8,128)(2,1)}) custom-call(bf16[512,768]{1,0:T(8,128)(2,1)S(1)} %bitcast.4), custom_call_target="tpu_custom_call" | custom-call | flops 60000002048 | bytes 2000000 | tf_op jit(solution)/shard_map/pallas_call | solution.py:23
  73.5 1.1 %collective-permute-done.4.received_ref = bf16[32,768]{1,0:T(8,128)(2,1)S(1)} collective-permute-done((bf16[32,768]{1,0:T(8,128)(2,1)S(1)}, bf16[32,768]{1,0:T(8,128)(2,1)S(1)}, u32[]{:S(2)}, u32[]{:S(2)}) %collective-permute-start.4) | collective-permute-done | bytes 49184 | tf_op jit(solution)/shard_map/ppermute | solution.py:163
  74.7 0.7 shard_map.73
  (1 shorter events, 0.0 us)
Async XLA Ops:
  0.6 19.2 %copy-start = (bf16[512,768]{1,0:T(8,128)(2,1)S(1)}, bf16[512,768]{1,0:T(8,128)(2,1)}, u32[]{:S(2)}) copy-start(bf16[512,768]{1,0:T(8,128)(2,1)} %queries_ref.1) | copy-start | bytes 2359300
  0.6 19.2 %copy-start.1 = (bf16[512,768]{1,0:T(8,128)(2,1)S(1)}, bf16[512,768]{1,0:T(8,128)(2,1)}, u32[]{:S(2)}) copy-start(bf16[512,768]{1,0:T(8,128)(2,1)} %embeddings_ref.1) | copy-start | bytes 2359300
  3.7 16.2 %copy-start.2 = (s32[4,48]{1,0:T(4,128)S(1)}, s32[4,48]{1,0:T(4,128)}, u32[]{:S(2)}) copy-start(s32[4,48]{1,0:T(4,128)} %short_ref.1) | copy-start | bytes 2308
  3.7 16.2 %copy-start.3 = (s32[512]{0:T(512)S(1)}, s32[512]{0:T(512)}, u32[]{:S(2)}) copy-start(s32[512]{0:T(512)} %param.7) | copy-start | bytes 6148
  22.5 19.8 %all-to-all-start.1 = ((bf16[32,16,768]{2,1,0:T(8,128)(2,1)}), bf16[32,16,768]{2,1,0:T(8,128)(2,1)S(1)}, u32[]{:S(2)}, u32[]{:S(2)}) async-start(bf16[32,16,768]{2,1,0:T(8,128)(2,1)} %bitcast.2), calls=%async_computation.1 | async-start | bytes 1572864 | tf_op jit(solution)/shard_map/all_to_all | solution.py:208
  27.5 23.3 %collective-permute-start = (bf16[4,32,768]{2,1,0:T(8,128)(2,1)S(1)}, bf16[4,32,768]{2,1,0:T(8,128)(2,1)S(1)}, u32[]{:S(2)}, u32[]{:S(2)}) collective-permute-start(bf16[4,32,768]{2,1,0:T(8,128)(2,1)S(1)} %get-tuple-element.19), channel_id=1, source_target_pairs={{0,64},{32,480},{64,128},{96,32},{128,192},{160,96},{192,256},{224... | collective-permute-start | bytes 589832 | tf_op jit(solution)/shard_map/ppermute | solution.py:173
  30.8 20.1 %collective-permute-start.1 = (bf16[4,32,768]{2,1,0:T(8,128)(2,1)S(1)}, bf16[4,32,768]{2,1,0:T(8,128)(2,1)S(1)}, u32[]{:S(2)}, u32[]{:S(2)}) collective-permute-start(bf16[4,32,768]{2,1,0:T(8,128)(2,1)S(1)} %get-tuple-element.20), channel_id=1, source_target_pairs={{0,32},{32,0},{64,96},{96,64},{128,160},{160,128},{192,224},{224,1... | collective-permute-start | bytes 589832 | tf_op jit(solution)/shard_map/ppermute | solution.py:163
  40.4 10.5 %collective-permute-start.2 = (bf16[4,32,768]{2,1,0:T(8,128)(2,1)S(1)}, bf16[4,32,768]{2,1,0:T(8,128)(2,1)S(1)}, u32[]{:S(2)}, u32[]{:S(2)}) collective-permute-start(bf16[4,32,768]{2,1,0:T(8,128)(2,1)S(1)} %get-tuple-element.21), channel_id=1, source_target_pairs={{0,480},{32,64},{64,32},{96,128},{128,96},{160,192},{192,160},{224... | collective-permute-start | bytes 589832 | tf_op jit(solution)/shard_map/ppermute | solution.py:168
  43.3 29.3 %all-to-all-start.2 = ((bf16[32,16,768]{2,1,0:T(8,128)(2,1)}), bf16[32,16,768]{2,1,0:T(8,128)(2,1)S(1)}, u32[]{:S(2)}, u32[]{:S(2)}) async-start(bf16[32,16,768]{2,1,0:T(8,128)(2,1)} %shard_map.69._), calls=%async_computation.2 | async-start | bytes 1572864 | tf_op jit(solution)/shard_map/all_to_all | solution.py:214
  51.0 12.9 %collective-permute-start.3 = (bf16[2,32,768]{2,1,0:T(8,128)(2,1)S(1)}, bf16[2,32,768]{2,1,0:T(8,128)(2,1)S(1)}, u32[]{:S(2)}, u32[]{:S(2)}) collective-permute-start(bf16[2,32,768]{2,1,0:T(8,128)(2,1)S(1)} %get-tuple-element.23), channel_id=1, source_target_pairs={{0,128},{32,416},{64,192},{96,480},{128,0},{160,288},{192,64},{224... | collective-permute-start | bytes 294920 | tf_op jit(solution)/shard_map/ppermute | solution.py:163
  63.9 10.8 %collective-permute-start.4 = (bf16[32,768]{1,0:T(8,128)(2,1)S(1)}, bf16[32,768]{1,0:T(8,128)(2,1)S(1)}, u32[]{:S(2)}, u32[]{:S(2)}) collective-permute-start(bf16[32,768]{1,0:T(8,128)(2,1)S(1)} %get-tuple-element.25), channel_id=1, source_target_pairs={{0,384},{32,160},{64,448},{96,224},{128,256},{160,32},{192,320},{2... | collective-permute-start | bytes 147464 | tf_op jit(solution)/shard_map/ppermute | solution.py:163

commit v7 on v6

--- a/solution.py
+++ b/solution.py
@@ -89,7 +89,7 @@
 
 def gradient_kernel(
     short_ref, positive_ref, stats_ref, queries_ref, embeddings_ref,
-    loss_ref, keep_ref, right_ref, left_ref, far_ref, query_ref, part_ref,
+    loss_ref, grad_ref, keep_ref, right_ref, left_ref, far_ref, part_ref,
 ):
     logs = stats_ref[:, 0, :]
     top = jnp.max(logs, axis=0, keepdims=True)
@@ -100,15 +100,14 @@
     weights = jnp.exp(masked - log_total)
     gradient = jnp.where(is_positive, weights - 1.0, weights)
     part_ref[...] = gradient
-    gradient = gradient.astype(BF16)
+    grad_ref[...] = gradient.astype(BF16)
     plane = lax.axis_index("dp")
     deep = BLOCK // lax.axis_size("dp")
     blocks = part_ref.shape[0] // BLOCK
-    odd = 2 * lax.rem(plane, 2)
-    results = ((keep_ref, 0), (right_ref, 1 + odd), (left_ref, 3 - odd), (far_ref, 2))
+    results = ((keep_ref, 0), (right_ref, 1), (left_ref, 3), (far_ref, 2))
     pieces = []
     for ref, shift in results:
-        kind = lax.rem(plane + shift, 4)
+        kind = lax.rem(plane, 4) ^ shift
         for m in range(ref.shape[0]):
             start = pl.multiple_of((4 * m + kind) * deep, deep)
             pieces += [part_ref[pl.ds(b * BLOCK + start, deep), :] for b in range(blocks)]
@@ -117,29 +116,31 @@
     size = terms.shape[0] // 4
     for i, (ref, _) in enumerate(results):
         ref[...] = terms[i * size : (i + 1) * size].reshape(ref.shape).astype(ref.dtype)
+
+
+def query_kernel(grad_ref, embeddings_ref, query_ref):
     query_ref[...] = lax.dot_general(
-        gradient, embeddings_ref[...], (((0,), (0,)), ((), ())), preferred_element_type=F32
+        grad_ref[...], embeddings_ref[...], (((0,), (0,)), ((), ())), preferred_element_type=F32
     ).astype(BF16)
 
 
-def spread_kernel(parts_ref, spread_ref):
+def spread_kernel(_, parts_ref, spread_ref):
     total = parts_ref[0].astype(F32)
     for i in range(1, parts_ref.shape[0]):
         total = total + parts_ref[i].astype(F32)
     spread_ref[...] = jnp.broadcast_to(total.astype(BF16)[None], spread_ref.shape)
 
 
-def middle_kernel(_, a_ref, b_ref, c_ref, d_ref, send_ref, keep_ref):
-    plane = lax.axis_index("dp")
-    mine, first = plane // 4, 1 + 2 * lax.rem(plane, 2)
-    for ref, masks in ((send_ref, (first, 2)), (keep_ref, (0, 4 - first))):
+def middle_kernel(a_ref, b_ref, c_ref, d_ref, send_ref, keep_ref):
+    mine = lax.axis_index("dp") // 4
+    for ref, masks in ((send_ref, (1, 2)), (keep_ref, (0, 3))):
         for i, mask in enumerate(masks):
             m = mine ^ mask
             total = a_ref[m].astype(F32) + b_ref[m].astype(F32) + c_ref[m].astype(F32) + d_ref[m].astype(F32)
             ref[i] = total.astype(ref.dtype)
 
 
-def join_kernel(received_ref, keep_ref, send_ref, own_ref):
+def join_kernel(_, received_ref, keep_ref, send_ref, own_ref):
     own_ref[...] = received_ref[0].astype(F32) + keep_ref[0]
     send_ref[...] = (received_ref[1].astype(F32) + keep_ref[1]).astype(BF16)
 
@@ -158,19 +159,8 @@
         label_ref[:, b, :] = total[b * deep : (b + 1) * deep]
 
 
-def exchanged(x, even, odd):
-    planes = lax.axis_size("dp")
-    return lax.ppermute(x, "dp", [(i, i ^ (odd if i % 2 else even)) for i in range(planes)])
-
-
-def beside(x):
-    planes = lax.axis_size("dp")
-    return lax.ppermute(x, "dp", [(i, (i - 1 + i % 2 * 2) % planes) for i in range(planes)])
-
-
-def moved_by_two(x):
-    planes = lax.axis_size("dp")
-    return lax.ppermute(x, "dp", [(i, (i + 2 - i % 2 * 4) % planes) for i in range(planes)])
+def exchanged(x, flip):
+    return lax.ppermute(x, "dp", [(i, i ^ flip) for i in range(lax.axis_size("dp"))])
 
 
 def body(queries, embeddings, shortlist, positive):
@@ -193,38 +183,43 @@
         vmem=VMEM_MOST,
     )
     stats = lax.all_to_all(stats, "label", 0, 0)
-    losses, keep, right, left, far, query_part = call(
+    losses, gradient, keep, right, left, far = call(
         gradient_kernel,
-        (shape((1, rows), F32), shape((planes // 4, chunk, width), F32))
-        + (shape((planes // 4, chunk, width), BF16),) * 3
-        + (shape((rows, width), BF16),),
+        (
+            shape((1, rows), F32),
+            shape((labels, rows), BF16),
+            shape((planes // 4, chunk, width), F32),
+        )
+        + (shape((planes // 4, chunk, width), BF16),) * 3,
         (shortlist, positive, stats, queries, embeddings),
-        flops=6 * madds,
-        scratch=[
-            pltpu.VMEM((labels, rows), F32),
-        ],
-    )
-    far, right, left = moved_by_two(far), exchanged(right, 1, 1), beside(left)
+        flops=4 * madds,
+        scratch=[pltpu.VMEM((labels, rows), F32)],
+    )
+    (query_part,) = call(
+        query_kernel, (shape((rows, width), BF16),), (gradient, embeddings), flops=LONG
+    )
+    far, right, left = exchanged(far, 2), exchanged(right, 1), exchanged(left, 3)
     query_parts = lax.all_to_all(
         query_part.reshape(groups, rows // groups, width), "label", 0, 0
     )
-    (spread,) = call(
-        spread_kernel, (shape(query_parts.shape, BF16),), (query_parts,), flops=LONG
-    )
-    query_grad = lax.all_to_all(spread, "label", 0, 0).reshape(rows, width)
     send, keep = call(
         middle_kernel,
         (shape((2, chunk, width), BF16), shape((2, chunk, width), F32)),
-        (spread, far, right, left, keep),
-        any_inputs=1,
+        (far, right, left, keep),
         flops=LONG,
     )
+    (spread,) = call(
+        spread_kernel, (shape(query_parts.shape, BF16),), (send, query_parts), any_inputs=1, flops=LONG
+    )
+    query_grad = lax.all_to_all(spread, "label", 0, 0).reshape(rows, width)
     send, own = call(
         join_kernel,
         (shape((chunk, width), BF16), shape((chunk, width), F32)),
-        (exchanged(send, 4, 12), keep),
-    )
-    received = exchanged(send, 12, 4)
+        (spread, exchanged(send, 4), keep),
+        any_inputs=1,
+        flops=LONG,
+    )
+    received = exchanged(send, 12)
     token, query_grad = call(
         copy_kernel,
         (shape((8, BLOCK), F32), shape((rows, width), BF16)),

time: 75.9 us -> 75.4 us (level)
  the two profiles are of different devices: /device:TPU:2 before, /device:TPU:1 now
where the time goes in v7:
time: 75.4 us; the launch traced here: 74.8 us
  starting transfers between devices  36.1 us (48%)
  blocking collectives  18.1 us (24%)
  waiting for transfers between devices  10.6 us (14%)
  Pallas kernels  9.18 us (12%)
  between operations  0.78 us (1%)
    ppermute x5, starting transfers between devices, exchanged(): lax.ppermute(x, 'dp', [(i, i ^ flip) for i in range(lax.axis_size('dp'))])  27.1 us
    all_to_all x1, blocking collectives, body(): stats = lax.all_to_all(stats, 'label', 0, 0)  18.1 us
    pallas_call x8, Pallas kernels, call(): pl.pallas_call(kernel, out_shape=out_shape, in_specs=specs, out_specs=tup...  9.18 us
    all_to_all x1, starting transfers between devices, body(): lax.all_to_all(query_part.reshape(groups, rows // groups, width), 'label'...  4.81 us
    all_to_all x1, starting transfers between devices, body(): query_grad = lax.all_to_all(spread, 'label', 0, 0).reshape(rows, width)  4.13 us
    all_to_all x1, waiting for transfers between devices, body(): query_grad = lax.all_to_all(spread, 'label', 0, 0).reshape(rows, width)  3.74 us
    ppermute x5, waiting for transfers between devices, exchanged(): lax.ppermute(x, 'dp', [(i, i ^ flip) for i in range(lax.axis_size('dp'))])  3.67 us
    all_to_all x1, waiting for transfers between devices, body(): lax.all_to_all(query_part.reshape(groups, rows // groups, width), 'label'...  3.24 us
  transfers between devices with their start and end apart: 7, of which 3 were waited for; matrix products, arithmetic and copies ran while one was open for 0% of the time, Pallas kernels for 5%

profile of v7, /device:TPU:1, one launch (start us, length us, event | category | flops | bytes accessed | tf_op | source)
XLA Modules:
  0.0 74.8 jit_solution(16112777235505835901)
XLA Ops:
  0.6 0.0 copy-start
  0.6 0.0 copy-start.1
  0.6 3.0 %shard_map.67 = f32[32,2,512]{2,1,0:T(2,128)} custom-call(s32[4,48]{1,0:T(4,128)} %short_ref.1, s32[1,512]{1,0:T(1,128)} %bitcast.5, bf16[512,768]{1,0:T(8,128)(2,1)} %queries_ref.1, bf16[512,768]{1,0:T(8,128)(2,1)} %embeddings_ref.3), custom_call_target="tpu_custom_call" | custom-call | flops 402653184 | bytes 2000000 | tf_op jit(solution)/shard_map/pallas_call | solution.py:23
  3.7 0.0 copy-start.2
  3.7 0.0 copy-start.3
  3.7 18.1 %all_to_all.15.stats_ref = f32[32,2,512]{2,1,0:T(2,128)S(1)} all-to-all(f32[32,2,512]{2,1,0:T(2,128)} %shard_map.67), channel_id=1, replica_groups=mesh['dp'=16,'label'=32] {'label'}, dimensions={0} | all-to-all | bytes 262144 | tf_op jit(solution)/shard_map/all_to_all | solution.py:185
  21.8 0.0 copy-done
  21.8 0.0 copy-done.1
  21.8 0.0 copy-done.2
  21.9 0.0 copy-done.3
  21.9 2.0 %shard_map.68 = (f32[1,512]{1,0:T(1,128)}, bf16[512,512]{1,0:T(8,128)(2,1)S(1)}, f32[4,32,768]{2,1,0:T(8,128)S(1)}, bf16[4,32,768]{2,1,0:T(8,128)(2,1)S(1)}, bf1...) custom-call(s32[4,48]{1,0:T(4,128)S(1)} %copy-done.2, s32[1,512]{1,0:T(1,128)S(1)} %bitcast.6, ...), custom_call_target="tpu_custom_call" | custom-call | flops 805306368 | bytes 2000000 | tf_op jit(solution)/shard_map/pallas_call | solution.py:23
  23.9 3.0 %collective-permute-start = (bf16[4,32,768]{2,1,0:T(8,128)(2,1)S(1)}, bf16[4,32,768]{2,1,0:T(8,128)(2,1)S(1)}, u32[]{:S(2)}, u32[]{:S(2)}) collective-permute-start(bf16[4,32,768]{2,1,0:T(8,128)(2,1)S(1)} %get-tuple-element.16), channel_id=1, source_target_pairs={{0,64},{32,96},{64,0},{96,32},{128,192},{160,224},{192,128},{224,1... | collective-permute-start | bytes 589832 | tf_op jit(solution)/shard_map/ppermute | solution.py:163
  26.8 3.5 %collective-permute-start.1 = (bf16[4,32,768]{2,1,0:T(8,128)(2,1)S(1)}, bf16[4,32,768]{2,1,0:T(8,128)(2,1)S(1)}, u32[]{:S(2)}, u32[]{:S(2)}) collective-permute-start(bf16[4,32,768]{2,1,0:T(8,128)(2,1)S(1)} %get-tuple-element.17), channel_id=1, source_target_pairs={{0,32},{32,0},{64,96},{96,64},{128,160},{160,128},{192,224},{224,1... | collective-permute-start | bytes 589832 | tf_op jit(solution)/shard_map/ppermute | solution.py:163
  30.4 2.7 %collective-permute-start.2 = (bf16[4,32,768]{2,1,0:T(8,128)(2,1)S(1)}, bf16[4,32,768]{2,1,0:T(8,128)(2,1)S(1)}, u32[]{:S(2)}, u32[]{:S(2)}) collective-permute-start(bf16[4,32,768]{2,1,0:T(8,128)(2,1)S(1)} %get-tuple-element.18), channel_id=1, source_target_pairs={{0,96},{32,64},{64,32},{96,0},{128,224},{160,192},{192,160},{224,1... | collective-permute-start | bytes 589832 | tf_op jit(solution)/shard_map/ppermute | solution.py:163
  33.1 1.5 %shard_map.70 = bf16[512,768]{1,0:T(8,128)(2,1)} custom-call(bf16[512,512]{1,0:T(8,128)(2,1)S(1)} %get-tuple-element.21.grad_ref, bf16[512,768]{1,0:T(8,128)(2,1)S(1)} %copy-done.1), custom_call_target="tpu_custom_call" | custom-call | flops 60000002048 | bytes 2000000 | tf_op jit(solution)/shard_map/pallas_call | solution.py:23
  34.6 4.8 %all-to-all-start.1 = ((bf16[32,16,768]{2,1,0:T(8,128)(2,1)}), bf16[32,16,768]{2,1,0:T(8,128)(2,1)S(1)}, u32[]{:S(2)}, u32[]{:S(2)}) async-start(bf16[32,16,768]{2,1,0:T(8,128)(2,1)} %bitcast.2), calls=%async_computation.1 | async-start | bytes 1572864 | tf_op jit(solution)/shard_map/all_to_all | solution.py:202
  39.5 0.0 collective-permute-done.a_ref
  39.5 3.7 %collective-permute-done.1.b_ref = bf16[4,32,768]{2,1,0:T(8,128)(2,1)S(1)} collective-permute-done((bf16[4,32,768]{2,1,0:T(8,128)(2,1)S(1)}, bf16[4,32,768]{2,1,0:T(8,128)(2,1)S(1)}, u32[]{:S(2)}, u32[]{:S(2)}) %collective-permute-start.1) | collective-permute-done | bytes 196640 | tf_op jit(solution)/shard_map/ppermute | solution.py:163
  43.1 0.0 collective-permute-done.2.c_ref
  43.1 0.1 shard_map.69
  43.2 7.3 %collective-permute-start.3 = (bf16[2,32,768]{2,1,0:T(8,128)(2,1)S(1)}, bf16[2,32,768]{2,1,0:T(8,128)(2,1)S(1)}, u32[]{:S(2)}, u32[]{:S(2)}) collective-permute-start(bf16[2,32,768]{2,1,0:T(8,128)(2,1)S(1)} %get-tuple-element.20._), channel_id=1, source_target_pairs={{0,128},{32,160},{64,192},{96,224},{128,0},{160,32},{192,64},{224,... | collective-permute-start | bytes 294920 | tf_op jit(solution)/shard_map/ppermute | solution.py:163
  50.5 3.2 %all-to-all-done.1.parts_ref = bf16[32,16,768]{2,1,0:T(8,128)(2,1)S(1)} async-done(((bf16[32,16,768]{2,1,0:T(8,128)(2,1)}), bf16[32,16,768]{2,1,0:T(8,128)(2,1)S(1)}, u32[]{:S(2)}, u32[]{:S(2)}) %all-to-all-start.1) | async-done | bytes 786464 | tf_op jit(solution)/shard_map/all_to_all | solution.py:202
  53.8 1.0 %shard_map.71._ = bf16[32,16,768]{2,1,0:T(8,128)(2,1)} custom-call(bf16[2,32,768]{2,1,0:T(8,128)(2,1)S(1)} %get-tuple-element.20._, bf16[32,16,768]{2,1,0:T(8,128)(2,1)S(1)} %all-to-all-done.1.parts_ref), custom_call_target="tpu_custom_call" | custom-call | flops 60000002048 | bytes 2000000 | tf_op jit(solution)/shard_map/pallas_call | solution.py:23
  54.8 4.1 %all-to-all-start.2 = ((bf16[32,16,768]{2,1,0:T(8,128)(2,1)}), bf16[32,16,768]{2,1,0:T(8,128)(2,1)S(1)}, u32[]{:S(2)}, u32[]{:S(2)}) async-start(bf16[32,16,768]{2,1,0:T(8,128)(2,1)} %shard_map.71._), calls=%async_computation.2 | async-start | bytes 1572864 | tf_op jit(solution)/shard_map/all_to_all | solution.py:214
  58.9 0.0 collective-permute-done.3.received_ref
  59.0 10.6 %collective-permute-start.4 = (bf16[32,768]{1,0:T(8,128)(2,1)S(1)}, bf16[32,768]{1,0:T(8,128)(2,1)S(1)}, u32[]{:S(2)}, u32[]{:S(2)}) collective-permute-start(bf16[32,768]{1,0:T(8,128)(2,1)S(1)} %get-tuple-element.25), channel_id=1, source_target_pairs={{0,384},{32,416},{64,448},{96,480},{128,256},{160,288},{192,320},{... | collective-permute-start | bytes 147464 | tf_op jit(solution)/shard_map/ppermute | solution.py:163
  69.5 3.7 %all-to-all-done.2 = bf16[32,16,768]{2,1,0:T(8,128)(2,1)S(1)} async-done(((bf16[32,16,768]{2,1,0:T(8,128)(2,1)}), bf16[32,16,768]{2,1,0:T(8,128)(2,1)S(1)}, u32[]{:S(2)}, u32[]{:S(2)}) %all-to-all-start.2) | async-done | bytes 786464 | tf_op jit(solution)/shard_map/all_to_all | solution.py:214
  73.3 0.9 %shard_map.72 = (f32[8,128]{1,0:T(8,128)S(1)}, bf16[512,768]{1,0:T(8,128)(2,1)}) custom-call(bf16[512,768]{1,0:T(8,128)(2,1)S(1)} %bitcast.4), custom_call_target="tpu_custom_call" | custom-call | flops 60000002048 | bytes 2000000 | tf_op jit(solution)/shard_map/pallas_call | solution.py:23
  74.2 0.0 collective-permute-done.4.received_ref
  74.2 0.7 shard_map.74
  (1 shorter events, 0.0 us)
Async XLA Ops:
  0.6 21.2 %copy-start = (bf16[512,768]{1,0:T(8,128)(2,1)S(1)}, bf16[512,768]{1,0:T(8,128)(2,1)}, u32[]{:S(2)}) copy-start(bf16[512,768]{1,0:T(8,128)(2,1)} %queries_ref.1) | copy-start | bytes 2359300
  0.6 21.2 %copy-start.1 = (bf16[512,768]{1,0:T(8,128)(2,1)S(1)}, bf16[512,768]{1,0:T(8,128)(2,1)}, u32[]{:S(2)}) copy-start(bf16[512,768]{1,0:T(8,128)(2,1)} %embeddings_ref.3) | copy-start | bytes 2359300
  3.7 18.2 %copy-start.2 = (s32[4,48]{1,0:T(4,128)S(1)}, s32[4,48]{1,0:T(4,128)}, u32[]{:S(2)}) copy-start(s32[4,48]{1,0:T(4,128)} %short_ref.1) | copy-start | bytes 2308
  3.7 18.2 %copy-start.3 = (s32[512]{0:T(512)S(1)}, s32[512]{0:T(512)}, u32[]{:S(2)}) copy-start(s32[512]{0:T(512)} %param.7) | copy-start | bytes 6148
  23.9 15.6 %collective-permute-start = (bf16[4,32,768]{2,1,0:T(8,128)(2,1)S(1)}, bf16[4,32,768]{2,1,0:T(8,128)(2,1)S(1)}, u32[]{:S(2)}, u32[]{:S(2)}) collective-permute-start(bf16[4,32,768]{2,1,0:T(8,128)(2,1)S(1)} %get-tuple-element.16), channel_id=1, source_target_pairs={{0,64},{32,96},{64,0},{96,32},{128,192},{160,224},{192,128},{224,1... | collective-permute-start | bytes 589832 | tf_op jit(solution)/shard_map/ppermute | solution.py:163
  26.8 16.3 %collective-permute-start.1 = (bf16[4,32,768]{2,1,0:T(8,128)(2,1)S(1)}, bf16[4,32,768]{2,1,0:T(8,128)(2,1)S(1)}, u32[]{:S(2)}, u32[]{:S(2)}) collective-permute-start(bf16[4,32,768]{2,1,0:T(8,128)(2,1)S(1)} %get-tuple-element.17), channel_id=1, source_target_pairs={{0,32},{32,0},{64,96},{96,64},{128,160},{160,128},{192,224},{224,1... | collective-permute-start | bytes 589832 | tf_op jit(solution)/shard_map/ppermute | solution.py:163
  30.4 12.7 %collective-permute-start.2 = (bf16[4,32,768]{2,1,0:T(8,128)(2,1)S(1)}, bf16[4,32,768]{2,1,0:T(8,128)(2,1)S(1)}, u32[]{:S(2)}, u32[]{:S(2)}) collective-permute-start(bf16[4,32,768]{2,1,0:T(8,128)(2,1)S(1)} %get-tuple-element.18), channel_id=1, source_target_pairs={{0,96},{32,64},{64,32},{96,0},{128,224},{160,192},{192,160},{224,1... | collective-permute-start | bytes 589832 | tf_op jit(solution)/shard_map/ppermute | solution.py:163
  34.6 19.2 %all-to-all-start.1 = ((bf16[32,16,768]{2,1,0:T(8,128)(2,1)}), bf16[32,16,768]{2,1,0:T(8,128)(2,1)S(1)}, u32[]{:S(2)}, u32[]{:S(2)}) async-start(bf16[32,16,768]{2,1,0:T(8,128)(2,1)} %bitcast.2), calls=%async_computation.1 | async-start | bytes 1572864 | tf_op jit(solution)/shard_map/all_to_all | solution.py:202
  43.2 15.7 %collective-permute-start.3 = (bf16[2,32,768]{2,1,0:T(8,128)(2,1)S(1)}, bf16[2,32,768]{2,1,0:T(8,128)(2,1)S(1)}, u32[]{:S(2)}, u32[]{:S(2)}) collective-permute-start(bf16[2,32,768]{2,1,0:T(8,128)(2,1)S(1)} %get-tuple-element.20._), channel_id=1, source_target_pairs={{0,128},{32,160},{64,192},{96,224},{128,0},{160,32},{192,64},{224,... | collective-permute-start | bytes 294920 | tf_op jit(solution)/shard_map/ppermute | solution.py:163
  54.8 18.5 %all-to-all-start.2 = ((bf16[32,16,768]{2,1,0:T(8,128)(2,1)}), bf16[32,16,768]{2,1,0:T(8,128)(2,1)S(1)}, u32[]{:S(2)}, u32[]{:S(2)}) async-start(bf16[32,16,768]{2,1,0:T(8,128)(2,1)} %shard_map.71._), calls=%async_computation.2 | async-start | bytes 1572864 | tf_op jit(solution)/shard_map/all_to_all | solution.py:214
  59.0 15.2 %collective-permute-start.4 = (bf16[32,768]{1,0:T(8,128)(2,1)S(1)}, bf16[32,768]{1,0:T(8,128)(2,1)S(1)}, u32[]{:S(2)}, u32[]{:S(2)}) collective-permute-start(bf16[32,768]{1,0:T(8,128)(2,1)S(1)} %get-tuple-element.25), channel_id=1, source_target_pairs={{0,384},{32,416},{64,448},{96,480},{128,256},{160,288},{192,320},{... | collective-permute-start | bytes 147464 | tf_op jit(solution)/shard_map/ppermute | solution.py:163

commit v8 on v7

--- a/solution.py
+++ b/solution.py
@@ -87,15 +87,17 @@
     out_ref[...] = jnp.broadcast_to(rows[None], out_ref.shape)
 
 
+def log_total_of(stats_ref):
+    logs = stats_ref[:, 0, :]
+    top = jnp.max(logs, axis=0, keepdims=True)
+    return top + jnp.log(jnp.sum(jnp.exp(logs - top), axis=0, keepdims=True))
+
+
 def gradient_kernel(
     short_ref, positive_ref, stats_ref, queries_ref, embeddings_ref,
-    loss_ref, grad_ref, keep_ref, right_ref, left_ref, far_ref, part_ref,
+    grad_ref, keep_ref, right_ref, left_ref, far_ref, part_ref,
 ):
-    logs = stats_ref[:, 0, :]
-    top = jnp.max(logs, axis=0, keepdims=True)
-    log_total = top + jnp.log(jnp.sum(jnp.exp(logs - top), axis=0, keepdims=True))
-    positive = jnp.sum(stats_ref[:, 1, :], axis=0, keepdims=True)
-    loss_ref[...] = log_total - positive
+    log_total = log_total_of(stats_ref)
     _, masked, is_positive = local_scores(short_ref, positive_ref, queries_ref, embeddings_ref)
     weights = jnp.exp(masked - log_total)
     gradient = jnp.where(is_positive, weights - 1.0, weights)
@@ -118,7 +120,8 @@
         ref[...] = terms[i * size : (i + 1) * size].reshape(ref.shape).astype(ref.dtype)
 
 
-def query_kernel(grad_ref, embeddings_ref, query_ref):
+def query_kernel(grad_ref, embeddings_ref, stats_ref, query_ref, loss_ref):
+    loss_ref[...] = log_total_of(stats_ref) - jnp.sum(stats_ref[:, 1, :], axis=0, keepdims=True)
     query_ref[...] = lax.dot_general(
         grad_ref[...], embeddings_ref[...], (((0,), (0,)), ((), ())), preferred_element_type=F32
     ).astype(BF16)
@@ -183,10 +186,9 @@
         vmem=VMEM_MOST,
     )
     stats = lax.all_to_all(stats, "label", 0, 0)
-    losses, gradient, keep, right, left, far = call(
+    gradient, keep, right, left, far = call(
         gradient_kernel,
         (
-            shape((1, rows), F32),
             shape((labels, rows), BF16),
             shape((planes // 4, chunk, width), F32),
         )
@@ -195,8 +197,11 @@
         flops=4 * madds,
         scratch=[pltpu.VMEM((labels, rows), F32)],
     )
-    (query_part,) = call(
-        query_kernel, (shape((rows, width), BF16),), (gradient, embeddings), flops=LONG
+    query_part, losses = call(
+        query_kernel,
+        (shape((rows, width), BF16), shape((1, rows), F32)),
+        (gradient, embeddings, stats),
+        flops=LONG,
     )
     far, right, left = exchanged(far, 2), exchanged(right, 1), exchanged(left, 3)
     query_parts = lax.all_to_all(

time: 75.4 us -> 74.8 us (level)
  no operation moved by 1% of the time
where the time goes in v8:
time: 74.8 us; the launch traced here: 74.3 us
  starting transfers between devices  36.1 us (48%)
  blocking collectives  18.1 us (24%)
  waiting for transfers between devices  10.6 us (14%)
  Pallas kernels  8.65 us (12%)
  between operations  0.79 us (1%)
    ppermute x5, starting transfers between devices, exchanged(): lax.ppermute(x, 'dp', [(i, i ^ flip) for i in range(lax.axis_size('dp'))])  27.2 us
    all_to_all x1, blocking collectives, body(): stats = lax.all_to_all(stats, 'label', 0, 0)  18.1 us
    pallas_call x8, Pallas kernels, call(): pl.pallas_call(kernel, out_shape=out_shape, in_specs=specs, out_specs=tup...  8.65 us
    all_to_all x1, starting transfers between devices, body(): lax.all_to_all(query_part.reshape(groups, rows // groups, width), 'label'...  4.81 us
    all_to_all x1, starting transfers between devices, body(): query_grad = lax.all_to_all(spread, 'label', 0, 0).reshape(rows, width)  4.13 us
    all_to_all x1, waiting for transfers between devices, body(): query_grad = lax.all_to_all(spread, 'label', 0, 0).reshape(rows, width)  3.74 us
    ppermute x5, waiting for transfers between devices, exchanged(): lax.ppermute(x, 'dp', [(i, i ^ flip) for i in range(lax.axis_size('dp'))])  3.66 us
    all_to_all x1, waiting for transfers between devices, body(): lax.all_to_all(query_part.reshape(groups, rows // groups, width), 'label'...  3.25 us
  transfers between devices with their start and end apart: 7, of which 3 were waited for; matrix products, arithmetic and copies ran while one was open for 0% of the time, Pallas kernels for 5%

profile of v8, /device:TPU:1, one launch (start us, length us, event | category | flops | bytes accessed | tf_op | source)
XLA Modules:
  0.0 74.3 jit_solution(15771117132006963629)
XLA Ops:
  0.6 0.0 copy-start
  0.6 0.0 copy-start.1
  0.6 3.0 %shard_map.67 = f32[32,2,512]{2,1,0:T(2,128)} custom-call(s32[4,48]{1,0:T(4,128)} %short_ref.1, s32[1,512]{1,0:T(1,128)} %bitcast.5, bf16[512,768]{1,0:T(8,128)(2,1)} %queries_ref.1, bf16[512,768]{1,0:T(8,128)(2,1)} %embeddings_ref.3), custom_call_target="tpu_custom_call" | custom-call | flops 402653184 | bytes 2000000 | tf_op jit(solution)/shard_map/pallas_call | solution.py:23
  3.7 0.0 copy-start.2
  3.7 0.0 copy-start.3
  3.7 18.1 %all_to_all.15.stats_ref = f32[32,2,512]{2,1,0:T(2,128)S(1)} all-to-all(f32[32,2,512]{2,1,0:T(2,128)} %shard_map.67), channel_id=1, replica_groups=mesh['dp'=16,'label'=32] {'label'}, dimensions={0} | all-to-all | bytes 262144 | tf_op jit(solution)/shard_map/all_to_all | solution.py:188
  21.8 0.0 copy-done
  21.8 0.0 copy-done.1
  21.8 0.0 copy-done.2
  21.9 0.0 copy-done.3
  21.9 1.5 %shard_map.68 = (bf16[512,512]{1,0:T(8,128)(2,1)S(1)}, f32[4,32,768]{2,1,0:T(8,128)S(1)}, bf16[4,32,768]{2,1,0:T(8,128)(2,1)S(1)}, bf16[4,32,768]{2,1,0:T(8,128)(2,1)S(1)}, bf16[4,32,768]{2,1,0:T(8,128)(2,1)S(1)}) custom-call(s32[4,48]{1,0:T(4,128)S(1)} %copy-done.2, s32[1,512]{1,0:T(1,128)S(1)} %bitcast.6, f32[32,2,512]{2,1,0:T(2,128)S(1)} %all_to_all.15.stats_ref, ...), custom_call_target="tpu_custom_call" | custom-call | flops 805306368 | bytes 2000000 | tf_op jit(solution)/shard_map/pallas_call | solution.py:23
  23.3 3.0 %collective-permute-start = (bf16[4,32,768]{2,1,0:T(8,128)(2,1)S(1)}, bf16[4,32,768]{2,1,0:T(8,128)(2,1)S(1)}, u32[]{:S(2)}, u32[]{:S(2)}) collective-permute-start(bf16[4,32,768]{2,1,0:T(8,128)(2,1)S(1)} %get-tuple-element.18), channel_id=1, source_target_pairs={{0,64},{32,96},{64,0},{96,32},{128,192},{160,224},{192,128},{224,1... | collective-permute-start | bytes 589832 | tf_op jit(solution)/shard_map/ppermute | solution.py:166
  26.3 3.5 %collective-permute-start.1 = (bf16[4,32,768]{2,1,0:T(8,128)(2,1)S(1)}, bf16[4,32,768]{2,1,0:T(8,128)(2,1)S(1)}, u32[]{:S(2)}, u32[]{:S(2)}) collective-permute-start(bf16[4,32,768]{2,1,0:T(8,128)(2,1)S(1)} %get-tuple-element.19), channel_id=1, source_target_pairs={{0,32},{32,0},{64,96},{96,64},{128,160},{160,128},{192,224},{224,1... | collective-permute-start | bytes 589832 | tf_op jit(solution)/shard_map/ppermute | solution.py:166
  29.9 2.7 %collective-permute-start.2 = (bf16[4,32,768]{2,1,0:T(8,128)(2,1)S(1)}, bf16[4,32,768]{2,1,0:T(8,128)(2,1)S(1)}, u32[]{:S(2)}, u32[]{:S(2)}) collective-permute-start(bf16[4,32,768]{2,1,0:T(8,128)(2,1)S(1)} %get-tuple-element.20), channel_id=1, source_target_pairs={{0,96},{32,64},{64,32},{96,0},{128,224},{160,192},{192,160},{224,1... | collective-permute-start | bytes 589832 | tf_op jit(solution)/shard_map/ppermute | solution.py:166
  32.6 1.5 %shard_map.69 = (bf16[512,768]{1,0:T(8,128)(2,1)}, f32[1,512]{1,0:T(1,128)}) custom-call(bf16[512,512]{1,0:T(8,128)(2,1)S(1)} %get-tuple-element.16.grad_ref, bf16[512,768]{1,0:T(8,128)(2,1)S(1)} %copy-done.1, f32[32,2,512]{2,1,0:T(2,128)S(1)} %all_to_all.15.stats_ref), custom_call_target="tpu_custom_call" | custom-call | flops 60000002048 | bytes 2000000 | tf_op jit(solution)/shard_map/pallas_call | solution.py:23
  34.1 4.8 %all-to-all-start.1 = ((bf16[32,16,768]{2,1,0:T(8,128)(2,1)}), bf16[32,16,768]{2,1,0:T(8,128)(2,1)S(1)}, u32[]{:S(2)}, u32[]{:S(2)}) async-start(bf16[32,16,768]{2,1,0:T(8,128)(2,1)} %bitcast.2), calls=%async_computation.1 | async-start | bytes 1572864 | tf_op jit(solution)/shard_map/all_to_all | solution.py:207
  38.9 0.0 collective-permute-done.a_ref
  39.0 3.6 %collective-permute-done.1.b_ref = bf16[4,32,768]{2,1,0:T(8,128)(2,1)S(1)} collective-permute-done((bf16[4,32,768]{2,1,0:T(8,128)(2,1)S(1)}, bf16[4,32,768]{2,1,0:T(8,128)(2,1)S(1)}, u32[]{:S(2)}, u32[]{:S(2)}) %collective-permute-start.1) | collective-permute-done | bytes 196640 | tf_op jit(solution)/shard_map/ppermute | solution.py:166
  42.6 0.0 collective-permute-done.2.c_ref
  42.6 0.1 shard_map.70
  42.7 7.3 %collective-permute-start.3 = (bf16[2,32,768]{2,1,0:T(8,128)(2,1)S(1)}, bf16[2,32,768]{2,1,0:T(8,128)(2,1)S(1)}, u32[]{:S(2)}, u32[]{:S(2)}) collective-permute-start(bf16[2,32,768]{2,1,0:T(8,128)(2,1)S(1)} %get-tuple-element.22._), channel_id=1, source_target_pairs={{0,128},{32,160},{64,192},{96,224},{128,0},{160,32},{192,64},{224,... | collective-permute-start | bytes 294920 | tf_op jit(solution)/shard_map/ppermute | solution.py:166
  50.0 3.2 %all-to-all-done.1.parts_ref = bf16[32,16,768]{2,1,0:T(8,128)(2,1)S(1)} async-done(((bf16[32,16,768]{2,1,0:T(8,128)(2,1)}), bf16[32,16,768]{2,1,0:T(8,128)(2,1)S(1)}, u32[]{:S(2)}, u32[]{:S(2)}) %all-to-all-start.1) | async-done | bytes 786464 | tf_op jit(solution)/shard_map/all_to_all | solution.py:207
  53.3 1.0 %shard_map.71._ = bf16[32,16,768]{2,1,0:T(8,128)(2,1)} custom-call(bf16[2,32,768]{2,1,0:T(8,128)(2,1)S(1)} %get-tuple-element.22._, bf16[32,16,768]{2,1,0:T(8,128)(2,1)S(1)} %all-to-all-done.1.parts_ref), custom_call_target="tpu_custom_call" | custom-call | flops 60000002048 | bytes 2000000 | tf_op jit(solution)/shard_map/pallas_call | solution.py:23
  54.3 4.1 %all-to-all-start.2 = ((bf16[32,16,768]{2,1,0:T(8,128)(2,1)}), bf16[32,16,768]{2,1,0:T(8,128)(2,1)S(1)}, u32[]{:S(2)}, u32[]{:S(2)}) async-start(bf16[32,16,768]{2,1,0:T(8,128)(2,1)} %shard_map.71._), calls=%async_computation.2 | async-start | bytes 1572864 | tf_op jit(solution)/shard_map/all_to_all | solution.py:219
  58.4 0.0 collective-permute-done.3.received_ref
  58.5 10.6 %collective-permute-start.4 = (bf16[32,768]{1,0:T(8,128)(2,1)S(1)}, bf16[32,768]{1,0:T(8,128)(2,1)S(1)}, u32[]{:S(2)}, u32[]{:S(2)}) collective-permute-start(bf16[32,768]{1,0:T(8,128)(2,1)S(1)} %get-tuple-element.27), channel_id=1, source_target_pairs={{0,384},{32,416},{64,448},{96,480},{128,256},{160,288},{192,320},{... | collective-permute-start | bytes 147464 | tf_op jit(solution)/shard_map/ppermute | solution.py:166
  69.0 3.7 %all-to-all-done.2 = bf16[32,16,768]{2,1,0:T(8,128)(2,1)S(1)} async-done(((bf16[32,16,768]{2,1,0:T(8,128)(2,1)}), bf16[32,16,768]{2,1,0:T(8,128)(2,1)S(1)}, u32[]{:S(2)}, u32[]{:S(2)}) %all-to-all-start.2) | async-done | bytes 786464 | tf_op jit(solution)/shard_map/all_to_all | solution.py:219
  72.8 0.9 %shard_map.72 = (f32[8,128]{1,0:T(8,128)S(1)}, bf16[512,768]{1,0:T(8,128)(2,1)}) custom-call(bf16[512,768]{1,0:T(8,128)(2,1)S(1)} %bitcast.4), custom_call_target="tpu_custom_call" | custom-call | flops 60000002048 | bytes 2000000 | tf_op jit(solution)/shard_map/pallas_call | solution.py:23
  73.7 0.0 collective-permute-done.4.received_ref
  73.7 0.7 shard_map.74
  (1 shorter events, 0.0 us)
Async XLA Ops:
  0.6 21.2 %copy-start = (bf16[512,768]{1,0:T(8,128)(2,1)S(1)}, bf16[512,768]{1,0:T(8,128)(2,1)}, u32[]{:S(2)}) copy-start(bf16[512,768]{1,0:T(8,128)(2,1)} %queries_ref.1) | copy-start | bytes 2359300
  0.6 21.2 %copy-start.1 = (bf16[512,768]{1,0:T(8,128)(2,1)S(1)}, bf16[512,768]{1,0:T(8,128)(2,1)}, u32[]{:S(2)}) copy-start(bf16[512,768]{1,0:T(8,128)(2,1)} %embeddings_ref.3) | copy-start | bytes 2359300
  3.7 18.2 %copy-start.2 = (s32[4,48]{1,0:T(4,128)S(1)}, s32[4,48]{1,0:T(4,128)}, u32[]{:S(2)}) copy-start(s32[4,48]{1,0:T(4,128)} %short_ref.1) | copy-start | bytes 2308
  3.7 18.2 %copy-start.3 = (s32[512]{0:T(512)S(1)}, s32[512]{0:T(512)}, u32[]{:S(2)}) copy-start(s32[512]{0:T(512)} %param.7) | copy-start | bytes 6148
  23.3 15.6 %collective-permute-start = (bf16[4,32,768]{2,1,0:T(8,128)(2,1)S(1)}, bf16[4,32,768]{2,1,0:T(8,128)(2,1)S(1)}, u32[]{:S(2)}, u32[]{:S(2)}) collective-permute-start(bf16[4,32,768]{2,1,0:T(8,128)(2,1)S(1)} %get-tuple-element.18), channel_id=1, source_target_pairs={{0,64},{32,96},{64,0},{96,32},{128,192},{160,224},{192,128},{224,1... | collective-permute-start | bytes 589832 | tf_op jit(solution)/shard_map/ppermute | solution.py:166
  26.3 16.3 %collective-permute-start.1 = (bf16[4,32,768]{2,1,0:T(8,128)(2,1)S(1)}, bf16[4,32,768]{2,1,0:T(8,128)(2,1)S(1)}, u32[]{:S(2)}, u32[]{:S(2)}) collective-permute-start(bf16[4,32,768]{2,1,0:T(8,128)(2,1)S(1)} %get-tuple-element.19), channel_id=1, source_target_pairs={{0,32},{32,0},{64,96},{96,64},{128,160},{160,128},{192,224},{224,1... | collective-permute-start | bytes 589832 | tf_op jit(solution)/shard_map/ppermute | solution.py:166
  29.9 12.7 %collective-permute-start.2 = (bf16[4,32,768]{2,1,0:T(8,128)(2,1)S(1)}, bf16[4,32,768]{2,1,0:T(8,128)(2,1)S(1)}, u32[]{:S(2)}, u32[]{:S(2)}) collective-permute-start(bf16[4,32,768]{2,1,0:T(8,128)(2,1)S(1)} %get-tuple-element.20), channel_id=1, source_target_pairs={{0,96},{32,64},{64,32},{96,0},{128,224},{160,192},{192,160},{224,1... | collective-permute-start | bytes 589832 | tf_op jit(solution)/shard_map/ppermute | solution.py:166
  34.1 19.2 %all-to-all-start.1 = ((bf16[32,16,768]{2,1,0:T(8,128)(2,1)}), bf16[32,16,768]{2,1,0:T(8,128)(2,1)S(1)}, u32[]{:S(2)}, u32[]{:S(2)}) async-start(bf16[32,16,768]{2,1,0:T(8,128)(2,1)} %bitcast.2), calls=%async_computation.1 | async-start | bytes 1572864 | tf_op jit(solution)/shard_map/all_to_all | solution.py:207
  42.7 15.7 %collective-permute-start.3 = (bf16[2,32,768]{2,1,0:T(8,128)(2,1)S(1)}, bf16[2,32,768]{2,1,0:T(8,128)(2,1)S(1)}, u32[]{:S(2)}, u32[]{:S(2)}) collective-permute-start(bf16[2,32,768]{2,1,0:T(8,128)(2,1)S(1)} %get-tuple-element.22._), channel_id=1, source_target_pairs={{0,128},{32,160},{64,192},{96,224},{128,0},{160,32},{192,64},{224,... | collective-permute-start | bytes 294920 | tf_op jit(solution)/shard_map/ppermute | solution.py:166
  54.3 18.5 %all-to-all-start.2 = ((bf16[32,16,768]{2,1,0:T(8,128)(2,1)}), bf16[32,16,768]{2,1,0:T(8,128)(2,1)S(1)}, u32[]{:S(2)}, u32[]{:S(2)}) async-start(bf16[32,16,768]{2,1,0:T(8,128)(2,1)} %shard_map.71._), calls=%async_computation.2 | async-start | bytes 1572864 | tf_op jit(solution)/shard_map/all_to_all | solution.py:219
  58.5 15.2 %collective-permute-start.4 = (bf16[32,768]{1,0:T(8,128)(2,1)S(1)}, bf16[32,768]{1,0:T(8,128)(2,1)S(1)}, u32[]{:S(2)}, u32[]{:S(2)}) collective-permute-start(bf16[32,768]{1,0:T(8,128)(2,1)S(1)} %get-tuple-element.27), channel_id=1, source_target_pairs={{0,384},{32,416},{64,448},{96,480},{128,256},{160,288},{192,320},{... | collective-permute-start | bytes 147464 | tf_op jit(solution)/shard_map/ppermute | solution.py:166

commit v9 on v8

--- a/solution.py
+++ b/solution.py
@@ -148,18 +148,17 @@
     send_ref[...] = (received_ref[1].astype(F32) + keep_ref[1]).astype(BF16)
 
 
-def copy_kernel(from_ref, token_ref, to_hbm, sem):
-    copy = pltpu.make_async_copy(from_ref, to_hbm, sem)
-    copy.start()
-    token_ref[...] = jnp.zeros_like(token_ref)
-    copy.wait()
-
-
-def last_kernel(_, received_ref, own_ref, label_ref):
+def last_kernel(query_ref, received_ref, own_ref, query_hbm, label_hbm, label_ref, sems):
+    query_copy = pltpu.make_async_copy(query_ref, query_hbm, sems.at[0])
+    query_copy.start()
     total = received_ref[...].astype(F32) + own_ref[...]
     deep, blocks = label_ref.shape[:2]
     for b in range(blocks):
         label_ref[:, b, :] = total[b * deep : (b + 1) * deep]
+    label_copy = pltpu.make_async_copy(label_ref, label_hbm, sems.at[1])
+    label_copy.start()
+    label_copy.wait()
+    query_copy.wait()
 
 
 def exchanged(x, flip):
@@ -225,18 +224,13 @@
         flops=LONG,
     )
     received = exchanged(send, 12)
-    token, query_grad = call(
-        copy_kernel,
-        (shape((8, BLOCK), F32), shape((rows, width), BF16)),
-        (query_grad,),
-        scratch=[pltpu.SemaphoreType.DMA],
-        any_outputs=1,
-        flops=LONG,
-    )
-    (label_grad,) = call(
+    label_shape = (BLOCK // planes, labels // BLOCK, width)
+    query_grad, label_grad = call(
         last_kernel,
-        (shape((BLOCK // planes, labels // BLOCK, width), F32),),
-        (token, received, own),
+        (shape((rows, width), BF16), shape(label_shape, F32)),
+        (query_grad, received, own),
+        scratch=[pltpu.VMEM(label_shape, F32), pltpu.SemaphoreType.DMA((2,))],
+        any_outputs=2,
     )
     return losses.reshape(rows), query_grad, label_grad
 

time: 74.8 us -> 74.3 us (level)
    ppermute x5, waiting for transfers between devices: 3.66 us -> 7.48 us  [exchanged(): lax.ppermute(x, 'dp', [(i, i ^ flip) for i in range(lax.axis_size('dp'))])]
    all_to_all x1, waiting for transfers between devices: 3.74 us -> 0.01 us  [body(): query_grad = lax.all_to_all(spread, 'label', 0, 0).reshape(rows, width)]
    pallas_call x8 -> x7, Pallas kernels: 8.65 us -> 8.01 us  [call(): pl.pallas_call(kernel, out_shape=out_shape, in_specs=specs, out_specs=tup...]
  transfers between devices with their start and end apart: 7 -> 7, of which waited for: 3 -> 3; matrix products, arithmetic and copies ran while one was open for 0% -> 0% of each run, Pallas kernels for 5% -> 4%
where the time goes in v9:
time: 74.3 us; the launch traced here: 73.8 us
  starting transfers between devices  36.1 us (49%)
  blocking collectives  18.1 us (24%)
  waiting for transfers between devices  10.7 us (14%)
  Pallas kernels  8.01 us (11%)
  between operations  0.78 us (1%)
    ppermute x5, starting transfers between devices, exchanged(): lax.ppermute(x, 'dp', [(i, i ^ flip) for i in range(lax.axis_size('dp'))])  27.2 us
    all_to_all x1, blocking collectives, body(): stats = lax.all_to_all(stats, 'label', 0, 0)  18.1 us
    pallas_call x7, Pallas kernels, call(): pl.pallas_call(kernel, out_shape=out_shape, in_specs=specs, out_specs=tup...  8.01 us
    ppermute x5, waiting for transfers between devices, exchanged(): lax.ppermute(x, 'dp', [(i, i ^ flip) for i in range(lax.axis_size('dp'))])  7.48 us
    all_to_all x1, starting transfers between devices, body(): lax.all_to_all(query_part.reshape(groups, rows // groups, width), 'label'...  4.81 us
    all_to_all x1, starting transfers between devices, body(): query_grad = lax.all_to_all(spread, 'label', 0, 0).reshape(rows, width)  4.13 us
    all_to_all x1, waiting for transfers between devices, body(): lax.all_to_all(query_part.reshape(groups, rows // groups, width), 'label'...  3.24 us
  transfers between devices with their start and end apart: 7, of which 3 were waited for; matrix products, arithmetic and copies ran while one was open for 0% of the time, Pallas kernels for 4%

profile of v9, /device:TPU:1, one launch (start us, length us, event | category | flops | bytes accessed | tf_op | source)
XLA Modules:
  0.0 73.8 jit_solution(16398078896539697406)
XLA Ops:
  0.6 0.0 copy-start
  0.6 0.0 copy-start.1
  0.6 3.0 %shard_map.67 = f32[32,2,512]{2,1,0:T(2,128)} custom-call(s32[4,48]{1,0:T(4,128)} %short_ref.1, s32[1,512]{1,0:T(1,128)} %bitcast.5, bf16[512,768]{1,0:T(8,128)(2,1)} %queries_ref.1, bf16[512,768]{1,0:T(8,128)(2,1)} %embeddings_ref.3), custom_call_target="tpu_custom_call" | custom-call | flops 402653184 | bytes 2000000 | tf_op jit(solution)/shard_map/pallas_call | solution.py:23
  3.7 0.0 copy-start.2
  3.7 0.0 copy-start.3
  3.7 18.1 %all_to_all.15.stats_ref = f32[32,2,512]{2,1,0:T(2,128)S(1)} all-to-all(f32[32,2,512]{2,1,0:T(2,128)} %shard_map.67), channel_id=1, replica_groups=mesh['dp'=16,'label'=32] {'label'}, dimensions={0} | all-to-all | bytes 262144 | tf_op jit(solution)/shard_map/all_to_all | solution.py:187
  21.8 0.0 copy-done
  21.8 0.0 copy-done.1
  21.8 0.0 copy-done.2
  21.9 0.0 copy-done.3
  21.9 1.5 %shard_map.68 = (bf16[512,512]{1,0:T(8,128)(2,1)S(1)}, f32[4,32,768]{2,1,0:T(8,128)S(1)}, bf16[4,32,768]{2,1,0:T(8,128)(2,1)S(1)}, bf16[4,32,768]{2,1,0:T(8,128)(2,1)S(1)}, bf16[4,32,768]{2,1,0:T(8,128)(2,1)S(1)}) custom-call(s32[4,48]{1,0:T(4,128)S(1)} %copy-done.2, s32[1,512]{1,0:T(1,128)S(1)} %bitcast.6, f32[32,2,512]{2,1,0:T(2,128)S(1)} %all_to_all.15.stats_ref, ...), custom_call_target="tpu_custom_call" | custom-call | flops 805306368 | bytes 2000000 | tf_op jit(solution)/shard_map/pallas_call | solution.py:23
  23.3 3.0 %collective-permute-start = (bf16[4,32,768]{2,1,0:T(8,128)(2,1)S(1)}, bf16[4,32,768]{2,1,0:T(8,128)(2,1)S(1)}, u32[]{:S(2)}, u32[]{:S(2)}) collective-permute-start(bf16[4,32,768]{2,1,0:T(8,128)(2,1)S(1)} %get-tuple-element.18), channel_id=1, source_target_pairs={{0,64},{32,96},{64,0},{96,32},{128,192},{160,224},{192,128},{224,1... | collective-permute-start | bytes 589832 | tf_op jit(solution)/shard_map/ppermute | solution.py:165
  26.3 3.5 %collective-permute-start.1 = (bf16[4,32,768]{2,1,0:T(8,128)(2,1)S(1)}, bf16[4,32,768]{2,1,0:T(8,128)(2,1)S(1)}, u32[]{:S(2)}, u32[]{:S(2)}) collective-permute-start(bf16[4,32,768]{2,1,0:T(8,128)(2,1)S(1)} %get-tuple-element.19), channel_id=1, source_target_pairs={{0,32},{32,0},{64,96},{96,64},{128,160},{160,128},{192,224},{224,1... | collective-permute-start | bytes 589832 | tf_op jit(solution)/shard_map/ppermute | solution.py:165
  29.9 2.7 %collective-permute-start.2 = (bf16[4,32,768]{2,1,0:T(8,128)(2,1)S(1)}, bf16[4,32,768]{2,1,0:T(8,128)(2,1)S(1)}, u32[]{:S(2)}, u32[]{:S(2)}) collective-permute-start(bf16[4,32,768]{2,1,0:T(8,128)(2,1)S(1)} %get-tuple-element.20), channel_id=1, source_target_pairs={{0,96},{32,64},{64,32},{96,0},{128,224},{160,192},{192,160},{224,1... | collective-permute-start | bytes 589832 | tf_op jit(solution)/shard_map/ppermute | solution.py:165
  32.6 1.5 %shard_map.69 = (bf16[512,768]{1,0:T(8,128)(2,1)}, f32[1,512]{1,0:T(1,128)}) custom-call(bf16[512,512]{1,0:T(8,128)(2,1)S(1)} %get-tuple-element.16.grad_ref, bf16[512,768]{1,0:T(8,128)(2,1)S(1)} %copy-done.1, f32[32,2,512]{2,1,0:T(2,128)S(1)} %all_to_all.15.stats_ref), custom_call_target="tpu_custom_call" | custom-call | flops 60000002048 | bytes 2000000 | tf_op jit(solution)/shard_map/pallas_call | solution.py:23
  34.1 4.8 %all-to-all-start.1 = ((bf16[32,16,768]{2,1,0:T(8,128)(2,1)}), bf16[32,16,768]{2,1,0:T(8,128)(2,1)S(1)}, u32[]{:S(2)}, u32[]{:S(2)}) async-start(bf16[32,16,768]{2,1,0:T(8,128)(2,1)} %bitcast.2), calls=%async_computation.1 | async-start | bytes 1572864 | tf_op jit(solution)/shard_map/all_to_all | solution.py:206
  38.9 0.0 collective-permute-done.a_ref
  38.9 3.6 %collective-permute-done.1.b_ref = bf16[4,32,768]{2,1,0:T(8,128)(2,1)S(1)} collective-permute-done((bf16[4,32,768]{2,1,0:T(8,128)(2,1)S(1)}, bf16[4,32,768]{2,1,0:T(8,128)(2,1)S(1)}, u32[]{:S(2)}, u32[]{:S(2)}) %collective-permute-start.1) | collective-permute-done | bytes 196640 | tf_op jit(solution)/shard_map/ppermute | solution.py:165
  42.6 0.0 collective-permute-done.2.c_ref
  42.6 0.1 shard_map.70
  42.7 7.3 %collective-permute-start.3 = (bf16[2,32,768]{2,1,0:T(8,128)(2,1)S(1)}, bf16[2,32,768]{2,1,0:T(8,128)(2,1)S(1)}, u32[]{:S(2)}, u32[]{:S(2)}) collective-permute-start(bf16[2,32,768]{2,1,0:T(8,128)(2,1)S(1)} %get-tuple-element.22._), channel_id=1, source_target_pairs={{0,128},{32,160},{64,192},{96,224},{128,0},{160,32},{192,64},{224,... | collective-permute-start | bytes 294920 | tf_op jit(solution)/shard_map/ppermute | solution.py:165
  50.0 3.2 %all-to-all-done.1.parts_ref = bf16[32,16,768]{2,1,0:T(8,128)(2,1)S(1)} async-done(((bf16[32,16,768]{2,1,0:T(8,128)(2,1)}), bf16[32,16,768]{2,1,0:T(8,128)(2,1)S(1)}, u32[]{:S(2)}, u32[]{:S(2)}) %all-to-all-start.1) | async-done | bytes 786464 | tf_op jit(solution)/shard_map/all_to_all | solution.py:206
  53.3 1.0 %shard_map.71._ = bf16[32,16,768]{2,1,0:T(8,128)(2,1)} custom-call(bf16[2,32,768]{2,1,0:T(8,128)(2,1)S(1)} %get-tuple-element.22._, bf16[32,16,768]{2,1,0:T(8,128)(2,1)S(1)} %all-to-all-done.1.parts_ref), custom_call_target="tpu_custom_call" | custom-call | flops 60000002048 | bytes 2000000 | tf_op jit(solution)/shard_map/pallas_call | solution.py:23
  54.3 4.1 %all-to-all-start.2 = ((bf16[32,16,768]{2,1,0:T(8,128)(2,1)}), bf16[32,16,768]{2,1,0:T(8,128)(2,1)S(1)}, u32[]{:S(2)}, u32[]{:S(2)}) async-start(bf16[32,16,768]{2,1,0:T(8,128)(2,1)} %shard_map.71._), calls=%async_computation.2 | async-start | bytes 1572864 | tf_op jit(solution)/shard_map/all_to_all | solution.py:218
  58.4 0.0 collective-permute-done.3.received_ref
  58.5 10.6 %collective-permute-start.4 = (bf16[32,768]{1,0:T(8,128)(2,1)S(1)}, bf16[32,768]{1,0:T(8,128)(2,1)S(1)}, u32[]{:S(2)}, u32[]{:S(2)}) collective-permute-start(bf16[32,768]{1,0:T(8,128)(2,1)S(1)} %get-tuple-element.25), channel_id=1, source_target_pairs={{0,384},{32,416},{64,448},{96,480},{128,256},{160,288},{192,320},{... | collective-permute-start | bytes 147464 | tf_op jit(solution)/shard_map/ppermute | solution.py:165
  69.0 3.8 %collective-permute-done.4.received_ref = bf16[32,768]{1,0:T(8,128)(2,1)S(1)} collective-permute-done((bf16[32,768]{1,0:T(8,128)(2,1)S(1)}, bf16[32,768]{1,0:T(8,128)(2,1)S(1)}, u32[]{:S(2)}, u32[]{:S(2)}) %collective-permute-start.4) | collective-permute-done | bytes 49184 | tf_op jit(solution)/shard_map/ppermute | solution.py:165
  72.8 0.0 all-to-all-done.2
  72.8 0.9 %shard_map.73 = (bf16[512,768]{1,0:T(8,128)(2,1)}, f32[8,4,768]{2,1,0:T(4,128)}) custom-call(bf16[512,768]{1,0:T(8,128)(2,1)S(1)} %bitcast.4, bf16[32,768]{1,0:T(8,128)(2,1)S(1)} %collective-permute-done.4.received_ref, f32[32,768]{1,0:T(8,128)S(1)} %get-tuple-element.26.own_ref), custom_call_target="tpu_custom_call" | custom-call | bytes 2000000 | tf_op jit(solution)/shard_map/pallas_call | solution.py:23
  (1 shorter events, 0.0 us)
Async XLA Ops:
  0.6 21.2 %copy-start = (bf16[512,768]{1,0:T(8,128)(2,1)S(1)}, bf16[512,768]{1,0:T(8,128)(2,1)}, u32[]{:S(2)}) copy-start(bf16[512,768]{1,0:T(8,128)(2,1)} %queries_ref.1) | copy-start | bytes 2359300
  0.6 21.2 %copy-start.1 = (bf16[512,768]{1,0:T(8,128)(2,1)S(1)}, bf16[512,768]{1,0:T(8,128)(2,1)}, u32[]{:S(2)}) copy-start(bf16[512,768]{1,0:T(8,128)(2,1)} %embeddings_ref.3) | copy-start | bytes 2359300
  3.7 18.2 %copy-start.2 = (s32[4,48]{1,0:T(4,128)S(1)}, s32[4,48]{1,0:T(4,128)}, u32[]{:S(2)}) copy-start(s32[4,48]{1,0:T(4,128)} %short_ref.1) | copy-start | bytes 2308
  3.7 18.2 %copy-start.3 = (s32[512]{0:T(512)S(1)}, s32[512]{0:T(512)}, u32[]{:S(2)}) copy-start(s32[512]{0:T(512)} %param.7) | copy-start | bytes 6148
  23.3 15.6 %collective-permute-start = (bf16[4,32,768]{2,1,0:T(8,128)(2,1)S(1)}, bf16[4,32,768]{2,1,0:T(8,128)(2,1)S(1)}, u32[]{:S(2)}, u32[]{:S(2)}) collective-permute-start(bf16[4,32,768]{2,1,0:T(8,128)(2,1)S(1)} %get-tuple-element.18), channel_id=1, source_target_pairs={{0,64},{32,96},{64,0},{96,32},{128,192},{160,224},{192,128},{224,1... | collective-permute-start | bytes 589832 | tf_op jit(solution)/shard_map/ppermute | solution.py:165
  26.3 16.3 %collective-permute-start.1 = (bf16[4,32,768]{2,1,0:T(8,128)(2,1)S(1)}, bf16[4,32,768]{2,1,0:T(8,128)(2,1)S(1)}, u32[]{:S(2)}, u32[]{:S(2)}) collective-permute-start(bf16[4,32,768]{2,1,0:T(8,128)(2,1)S(1)} %get-tuple-element.19), channel_id=1, source_target_pairs={{0,32},{32,0},{64,96},{96,64},{128,160},{160,128},{192,224},{224,1... | collective-permute-start | bytes 589832 | tf_op jit(solution)/shard_map/ppermute | solution.py:165
  29.9 12.7 %collective-permute-start.2 = (bf16[4,32,768]{2,1,0:T(8,128)(2,1)S(1)}, bf16[4,32,768]{2,1,0:T(8,128)(2,1)S(1)}, u32[]{:S(2)}, u32[]{:S(2)}) collective-permute-start(bf16[4,32,768]{2,1,0:T(8,128)(2,1)S(1)} %get-tuple-element.20), channel_id=1, source_target_pairs={{0,96},{32,64},{64,32},{96,0},{128,224},{160,192},{192,160},{224,1... | collective-permute-start | bytes 589832 | tf_op jit(solution)/shard_map/ppermute | solution.py:165
  34.1 19.2 %all-to-all-start.1 = ((bf16[32,16,768]{2,1,0:T(8,128)(2,1)}), bf16[32,16,768]{2,1,0:T(8,128)(2,1)S(1)}, u32[]{:S(2)}, u32[]{:S(2)}) async-start(bf16[32,16,768]{2,1,0:T(8,128)(2,1)} %bitcast.2), calls=%async_computation.1 | async-start | bytes 1572864 | tf_op jit(solution)/shard_map/all_to_all | solution.py:206
  42.7 15.7 %collective-permute-start.3 = (bf16[2,32,768]{2,1,0:T(8,128)(2,1)S(1)}, bf16[2,32,768]{2,1,0:T(8,128)(2,1)S(1)}, u32[]{:S(2)}, u32[]{:S(2)}) collective-permute-start(bf16[2,32,768]{2,1,0:T(8,128)(2,1)S(1)} %get-tuple-element.22._), channel_id=1, source_target_pairs={{0,128},{32,160},{64,192},{96,224},{128,0},{160,32},{192,64},{224,... | collective-permute-start | bytes 294920 | tf_op jit(solution)/shard_map/ppermute | solution.py:165
  54.3 18.6 %all-to-all-start.2 = ((bf16[32,16,768]{2,1,0:T(8,128)(2,1)}), bf16[32,16,768]{2,1,0:T(8,128)(2,1)S(1)}, u32[]{:S(2)}, u32[]{:S(2)}) async-start(bf16[32,16,768]{2,1,0:T(8,128)(2,1)} %shard_map.71._), calls=%async_computation.2 | async-start | bytes 1572864 | tf_op jit(solution)/shard_map/all_to_all | solution.py:218
  58.5 14.4 %collective-permute-start.4 = (bf16[32,768]{1,0:T(8,128)(2,1)S(1)}, bf16[32,768]{1,0:T(8,128)(2,1)S(1)}, u32[]{:S(2)}, u32[]{:S(2)}) collective-permute-start(bf16[32,768]{1,0:T(8,128)(2,1)S(1)} %get-tuple-element.25), channel_id=1, source_target_pairs={{0,384},{32,416},{64,448},{96,480},{128,256},{160,288},{192,320},{... | collective-permute-start | bytes 147464 | tf_op jit(solution)/shard_map/ppermute | solution.py:165

commit v10 on v9

--- a/solution.py
+++ b/solution.py
@@ -88,9 +88,9 @@
 
 
 def log_total_of(stats_ref):
-    logs = stats_ref[:, 0, :]
-    top = jnp.max(logs, axis=0, keepdims=True)
-    return top + jnp.log(jnp.sum(jnp.exp(logs - top), axis=0, keepdims=True))
+    both = stats_ref[...]
+    top = jnp.max(both, axis=0)
+    return (top + jnp.log(jnp.sum(jnp.exp(both - top[None]), axis=0)))[0:1]
 
 
 def gradient_kernel(

time: 74.3 us -> 74.3 us (level)
  no operation moved by 1% of the time
where the time goes in v10:
time: 74.3 us; the launch traced here: 73.8 us
  starting transfers between devices  36.1 us (49%)
  blocking collectives  18.1 us (24%)
  waiting for transfers between devices  10.7 us (14%)
  Pallas kernels  8.01 us (11%)
  between operations  0.78 us (1%)
    ppermute x5, starting transfers between devices, exchanged(): lax.ppermute(x, 'dp', [(i, i ^ flip) for i in range(lax.axis_size('dp'))])  27.2 us
    all_to_all x1, blocking collectives, body(): stats = lax.all_to_all(stats, 'label', 0, 0)  18.1 us
    pallas_call x7, Pallas kernels, call(): pl.pallas_call(kernel, out_shape=out_shape, in_specs=specs, out_specs=tup...  8.01 us
    ppermute x5, waiting for transfers between devices, exchanged(): lax.ppermute(x, 'dp', [(i, i ^ flip) for i in range(lax.axis_size('dp'))])  7.47 us
    all_to_all x1, starting transfers between devices, body(): lax.all_to_all(query_part.reshape(groups, rows // groups, width), 'label'...  4.81 us
    all_to_all x1, starting transfers between devices, body(): query_grad = lax.all_to_all(spread, 'label', 0, 0).reshape(rows, width)  4.13 us
    all_to_all x1, waiting for transfers between devices, body(): lax.all_to_all(query_part.reshape(groups, rows // groups, width), 'label'...  3.25 us
  transfers between devices with their start and end apart: 7, of which 3 were waited for; matrix products, arithmetic and copies ran while one was open for 0% of the time, Pallas kernels for 4%

profile of v10, /device:TPU:1, one launch (start us, length us, event | category | flops | bytes accessed | tf_op | source)
XLA Modules:
  0.0 73.8 jit_solution(9793141320687695052)
XLA Ops:
  0.6 0.0 copy-start
  0.6 0.0 copy-start.1
  0.6 3.0 %shard_map.67 = f32[32,2,512]{2,1,0:T(2,128)} custom-call(s32[4,48]{1,0:T(4,128)} %short_ref.1, s32[1,512]{1,0:T(1,128)} %bitcast.5, bf16[512,768]{1,0:T(8,128)(2,1)} %queries_ref.1, bf16[512,768]{1,0:T(8,128)(2,1)} %embeddings_ref.3), custom_call_target="tpu_custom_call" | custom-call | flops 402653184 | bytes 2000000 | tf_op jit(solution)/shard_map/pallas_call | solution.py:23
  3.7 0.0 copy-start.2
  3.7 0.0 copy-start.3
  3.7 18.1 %all_to_all.15.stats_ref = f32[32,2,512]{2,1,0:T(2,128)S(1)} all-to-all(f32[32,2,512]{2,1,0:T(2,128)} %shard_map.67), channel_id=1, replica_groups=mesh['dp'=16,'label'=32] {'label'}, dimensions={0} | all-to-all | bytes 262144 | tf_op jit(solution)/shard_map/all_to_all | solution.py:187
  21.8 0.0 copy-done
  21.8 0.0 copy-done.1
  21.8 0.0 copy-done.2
  21.9 0.0 copy-done.3
  21.9 1.5 %shard_map.68 = (bf16[512,512]{1,0:T(8,128)(2,1)S(1)}, f32[4,32,768]{2,1,0:T(8,128)S(1)}, bf16[4,32,768]{2,1,0:T(8,128)(2,1)S(1)}, bf16[4,32,768]{2,1,0:T(8,128)(2,1)S(1)}, bf16[4,32,768]{2,1,0:T(8,128)(2,1)S(1)}) custom-call(s32[4,48]{1,0:T(4,128)S(1)} %copy-done.2, s32[1,512]{1,0:T(1,128)S(1)} %bitcast.6, f32[32,2,512]{2,1,0:T(2,128)S(1)} %all_to_all.15.stats_ref, ...), custom_call_target="tpu_custom_call" | custom-call | flops 805306368 | bytes 2000000 | tf_op jit(solution)/shard_map/pallas_call | solution.py:23
  23.3 3.0 %collective-permute-start = (bf16[4,32,768]{2,1,0:T(8,128)(2,1)S(1)}, bf16[4,32,768]{2,1,0:T(8,128)(2,1)S(1)}, u32[]{:S(2)}, u32[]{:S(2)}) collective-permute-start(bf16[4,32,768]{2,1,0:T(8,128)(2,1)S(1)} %get-tuple-element.18), channel_id=1, source_target_pairs={{0,64},{32,96},{64,0},{96,32},{128,192},{160,224},{192,128},{224,1... | collective-permute-start | bytes 589832 | tf_op jit(solution)/shard_map/ppermute | solution.py:165
  26.3 3.5 %collective-permute-start.1 = (bf16[4,32,768]{2,1,0:T(8,128)(2,1)S(1)}, bf16[4,32,768]{2,1,0:T(8,128)(2,1)S(1)}, u32[]{:S(2)}, u32[]{:S(2)}) collective-permute-start(bf16[4,32,768]{2,1,0:T(8,128)(2,1)S(1)} %get-tuple-element.19), channel_id=1, source_target_pairs={{0,32},{32,0},{64,96},{96,64},{128,160},{160,128},{192,224},{224,1... | collective-permute-start | bytes 589832 | tf_op jit(solution)/shard_map/ppermute | solution.py:165
  29.9 2.7 %collective-permute-start.2 = (bf16[4,32,768]{2,1,0:T(8,128)(2,1)S(1)}, bf16[4,32,768]{2,1,0:T(8,128)(2,1)S(1)}, u32[]{:S(2)}, u32[]{:S(2)}) collective-permute-start(bf16[4,32,768]{2,1,0:T(8,128)(2,1)S(1)} %get-tuple-element.20), channel_id=1, source_target_pairs={{0,96},{32,64},{64,32},{96,0},{128,224},{160,192},{192,160},{224,1... | collective-permute-start | bytes 589832 | tf_op jit(solution)/shard_map/ppermute | solution.py:165
  32.6 1.5 %shard_map.69 = (bf16[512,768]{1,0:T(8,128)(2,1)}, f32[1,512]{1,0:T(1,128)}) custom-call(bf16[512,512]{1,0:T(8,128)(2,1)S(1)} %get-tuple-element.16.grad_ref, bf16[512,768]{1,0:T(8,128)(2,1)S(1)} %copy-done.1, f32[32,2,512]{2,1,0:T(2,128)S(1)} %all_to_all.15.stats_ref), custom_call_target="tpu_custom_call" | custom-call | flops 60000002048 | bytes 2000000 | tf_op jit(solution)/shard_map/pallas_call | solution.py:23
  34.1 4.8 %all-to-all-start.1 = ((bf16[32,16,768]{2,1,0:T(8,128)(2,1)}), bf16[32,16,768]{2,1,0:T(8,128)(2,1)S(1)}, u32[]{:S(2)}, u32[]{:S(2)}) async-start(bf16[32,16,768]{2,1,0:T(8,128)(2,1)} %bitcast.2), calls=%async_computation.1 | async-start | bytes 1572864 | tf_op jit(solution)/shard_map/all_to_all | solution.py:206
  38.9 0.0 collective-permute-done.a_ref
  39.0 3.6 %collective-permute-done.1.b_ref = bf16[4,32,768]{2,1,0:T(8,128)(2,1)S(1)} collective-permute-done((bf16[4,32,768]{2,1,0:T(8,128)(2,1)S(1)}, bf16[4,32,768]{2,1,0:T(8,128)(2,1)S(1)}, u32[]{:S(2)}, u32[]{:S(2)}) %collective-permute-start.1) | collective-permute-done | bytes 196640 | tf_op jit(solution)/shard_map/ppermute | solution.py:165
  42.6 0.0 collective-permute-done.2.c_ref
  42.6 0.1 shard_map.70
  42.7 7.3 %collective-permute-start.3 = (bf16[2,32,768]{2,1,0:T(8,128)(2,1)S(1)}, bf16[2,32,768]{2,1,0:T(8,128)(2,1)S(1)}, u32[]{:S(2)}, u32[]{:S(2)}) collective-permute-start(bf16[2,32,768]{2,1,0:T(8,128)(2,1)S(1)} %get-tuple-element.22._), channel_id=1, source_target_pairs={{0,128},{32,160},{64,192},{96,224},{128,0},{160,32},{192,64},{224,... | collective-permute-start | bytes 294920 | tf_op jit(solution)/shard_map/ppermute | solution.py:165
  50.0 3.3 %all-to-all-done.1.parts_ref = bf16[32,16,768]{2,1,0:T(8,128)(2,1)S(1)} async-done(((bf16[32,16,768]{2,1,0:T(8,128)(2,1)}), bf16[32,16,768]{2,1,0:T(8,128)(2,1)S(1)}, u32[]{:S(2)}, u32[]{:S(2)}) %all-to-all-start.1) | async-done | bytes 786464 | tf_op jit(solution)/shard_map/all_to_all | solution.py:206
  53.3 1.0 %shard_map.71._ = bf16[32,16,768]{2,1,0:T(8,128)(2,1)} custom-call(bf16[2,32,768]{2,1,0:T(8,128)(2,1)S(1)} %get-tuple-element.22._, bf16[32,16,768]{2,1,0:T(8,128)(2,1)S(1)} %all-to-all-done.1.parts_ref), custom_call_target="tpu_custom_call" | custom-call | flops 60000002048 | bytes 2000000 | tf_op jit(solution)/shard_map/pallas_call | solution.py:23
  54.3 4.1 %all-to-all-start.2 = ((bf16[32,16,768]{2,1,0:T(8,128)(2,1)}), bf16[32,16,768]{2,1,0:T(8,128)(2,1)S(1)}, u32[]{:S(2)}, u32[]{:S(2)}) async-start(bf16[32,16,768]{2,1,0:T(8,128)(2,1)} %shard_map.71._), calls=%async_computation.2 | async-start | bytes 1572864 | tf_op jit(solution)/shard_map/all_to_all | solution.py:218
  58.4 0.0 collective-permute-done.3.received_ref
  58.5 10.6 %collective-permute-start.4 = (bf16[32,768]{1,0:T(8,128)(2,1)S(1)}, bf16[32,768]{1,0:T(8,128)(2,1)S(1)}, u32[]{:S(2)}, u32[]{:S(2)}) collective-permute-start(bf16[32,768]{1,0:T(8,128)(2,1)S(1)} %get-tuple-element.25), channel_id=1, source_target_pairs={{0,384},{32,416},{64,448},{96,480},{128,256},{160,288},{192,320},{... | collective-permute-start | bytes 147464 | tf_op jit(solution)/shard_map/ppermute | solution.py:165
  69.0 3.8 %collective-permute-done.4.received_ref = bf16[32,768]{1,0:T(8,128)(2,1)S(1)} collective-permute-done((bf16[32,768]{1,0:T(8,128)(2,1)S(1)}, bf16[32,768]{1,0:T(8,128)(2,1)S(1)}, u32[]{:S(2)}, u32[]{:S(2)}) %collective-permute-start.4) | collective-permute-done | bytes 49184 | tf_op jit(solution)/shard_map/ppermute | solution.py:165
  72.8 0.0 all-to-all-done.2
  72.9 0.9 %shard_map.73 = (bf16[512,768]{1,0:T(8,128)(2,1)}, f32[8,4,768]{2,1,0:T(4,128)}) custom-call(bf16[512,768]{1,0:T(8,128)(2,1)S(1)} %bitcast.4, bf16[32,768]{1,0:T(8,128)(2,1)S(1)} %collective-permute-done.4.received_ref, f32[32,768]{1,0:T(8,128)S(1)} %get-tuple-element.26.own_ref), custom_call_target="tpu_custom_call" | custom-call | bytes 2000000 | tf_op jit(solution)/shard_map/pallas_call | solution.py:23
  (1 shorter events, 0.0 us)
Async XLA Ops:
  0.6 21.2 %copy-start = (bf16[512,768]{1,0:T(8,128)(2,1)S(1)}, bf16[512,768]{1,0:T(8,128)(2,1)}, u32[]{:S(2)}) copy-start(bf16[512,768]{1,0:T(8,128)(2,1)} %queries_ref.1) | copy-start | bytes 2359300
  0.6 21.2 %copy-start.1 = (bf16[512,768]{1,0:T(8,128)(2,1)S(1)}, bf16[512,768]{1,0:T(8,128)(2,1)}, u32[]{:S(2)}) copy-start(bf16[512,768]{1,0:T(8,128)(2,1)} %embeddings_ref.3) | copy-start | bytes 2359300
  3.7 18.2 %copy-start.2 = (s32[4,48]{1,0:T(4,128)S(1)}, s32[4,48]{1,0:T(4,128)}, u32[]{:S(2)}) copy-start(s32[4,48]{1,0:T(4,128)} %short_ref.1) | copy-start | bytes 2308
  3.7 18.2 %copy-start.3 = (s32[512]{0:T(512)S(1)}, s32[512]{0:T(512)}, u32[]{:S(2)}) copy-start(s32[512]{0:T(512)} %param.7) | copy-start | bytes 6148
  23.3 15.6 %collective-permute-start = (bf16[4,32,768]{2,1,0:T(8,128)(2,1)S(1)}, bf16[4,32,768]{2,1,0:T(8,128)(2,1)S(1)}, u32[]{:S(2)}, u32[]{:S(2)}) collective-permute-start(bf16[4,32,768]{2,1,0:T(8,128)(2,1)S(1)} %get-tuple-element.18), channel_id=1, source_target_pairs={{0,64},{32,96},{64,0},{96,32},{128,192},{160,224},{192,128},{224,1... | collective-permute-start | bytes 589832 | tf_op jit(solution)/shard_map/ppermute | solution.py:165
  26.3 16.3 %collective-permute-start.1 = (bf16[4,32,768]{2,1,0:T(8,128)(2,1)S(1)}, bf16[4,32,768]{2,1,0:T(8,128)(2,1)S(1)}, u32[]{:S(2)}, u32[]{:S(2)}) collective-permute-start(bf16[4,32,768]{2,1,0:T(8,128)(2,1)S(1)} %get-tuple-element.19), channel_id=1, source_target_pairs={{0,32},{32,0},{64,96},{96,64},{128,160},{160,128},{192,224},{224,1... | collective-permute-start | bytes 589832 | tf_op jit(solution)/shard_map/ppermute | solution.py:165
  29.9 12.7 %collective-permute-start.2 = (bf16[4,32,768]{2,1,0:T(8,128)(2,1)S(1)}, bf16[4,32,768]{2,1,0:T(8,128)(2,1)S(1)}, u32[]{:S(2)}, u32[]{:S(2)}) collective-permute-start(bf16[4,32,768]{2,1,0:T(8,128)(2,1)S(1)} %get-tuple-element.20), channel_id=1, source_target_pairs={{0,96},{32,64},{64,32},{96,0},{128,224},{160,192},{192,160},{224,1... | collective-permute-start | bytes 589832 | tf_op jit(solution)/shard_map/ppermute | solution.py:165
  34.1 19.2 %all-to-all-start.1 = ((bf16[32,16,768]{2,1,0:T(8,128)(2,1)}), bf16[32,16,768]{2,1,0:T(8,128)(2,1)S(1)}, u32[]{:S(2)}, u32[]{:S(2)}) async-start(bf16[32,16,768]{2,1,0:T(8,128)(2,1)} %bitcast.2), calls=%async_computation.1 | async-start | bytes 1572864 | tf_op jit(solution)/shard_map/all_to_all | solution.py:206
  42.7 15.7 %collective-permute-start.3 = (bf16[2,32,768]{2,1,0:T(8,128)(2,1)S(1)}, bf16[2,32,768]{2,1,0:T(8,128)(2,1)S(1)}, u32[]{:S(2)}, u32[]{:S(2)}) collective-permute-start(bf16[2,32,768]{2,1,0:T(8,128)(2,1)S(1)} %get-tuple-element.22._), channel_id=1, source_target_pairs={{0,128},{32,160},{64,192},{96,224},{128,0},{160,32},{192,64},{224,... | collective-permute-start | bytes 294920 | tf_op jit(solution)/shard_map/ppermute | solution.py:165
  54.3 18.6 %all-to-all-start.2 = ((bf16[32,16,768]{2,1,0:T(8,128)(2,1)}), bf16[32,16,768]{2,1,0:T(8,128)(2,1)S(1)}, u32[]{:S(2)}, u32[]{:S(2)}) async-start(bf16[32,16,768]{2,1,0:T(8,128)(2,1)} %shard_map.71._), calls=%async_computation.2 | async-start | bytes 1572864 | tf_op jit(solution)/shard_map/all_to_all | solution.py:218
  58.5 14.4 %collective-permute-start.4 = (bf16[32,768]{1,0:T(8,128)(2,1)S(1)}, bf16[32,768]{1,0:T(8,128)(2,1)S(1)}, u32[]{:S(2)}, u32[]{:S(2)}) collective-permute-start(bf16[32,768]{1,0:T(8,128)(2,1)S(1)} %get-tuple-element.25), channel_id=1, source_target_pairs={{0,384},{32,416},{64,448},{96,480},{128,256},{160,288},{192,320},{... | collective-permute-start | bytes 147464 | tf_op jit(solution)/shard_map/ppermute | solution.py:165
